TPU v7x, 32 devices: a whole 2x2x4 slice. The times are simulated.
32 devices in a mesh: lb: 4 (over x, core), rb: 4 (over z), rep: 2 (over y).
Axes of the slice: x: 2, y: 2, z: 4, core: 2. Of those that a mesh axis runs over, the one named last changes fastest.
Arguments:
- left_factor: bfloat16 [1024, 1024], P('lb', 'rep'), may hold values from -5 to 5
- boundary_site: bfloat16 [1024, 16, 1024], P('rep', None, 'rb'), may hold values from -6 to 6
- double_layer: float32 [16, 16], replicated, may hold values from -1.5 to 1.5
Outputs:
- site_q: float32 [16, 1024, 1024], P('rep', 'lb', 'rb')
- factor: float32 [1024, 1024], P('lb')
All inputs are finite; a program needn't handle non-finite values.
Results may differ from a plain program's by a relative error of at most 0.0032.
Values sent between devices are 32-bit elements; how exact they have to be, the bound alone decides.
No kernel may reach another device: no remote copies, remote signals or barrier semaphores. Data moves between devices by JAX's collectives and lax.ppermute only.
A program may use at most 128 MiB of HBM per device.

v0:
```python
import functools
import math

import jax
import jax.numpy as jnp
from jax import lax
from jax.experimental import pallas as pl
from jax.experimental.pallas import tpu as pltpu
from jax.sharding import PartitionSpec as P

BLOCK = 128


def swap(array, step):
    axis, size, distance = step
    return lax.ppermute(array, axis, [(i, i ^ distance) for i in range(size)])


def steps_of(axis, size):
    return [(axis, size, 1 << i) for i in range(size.bit_length() - 1)]


def gather_slots(held, steps):
    for step in steps:
        held = held + [(slot ^ step[2], swap(piece, step)) for slot, piece in held]
    return held


def cut_steps(steps, rows):
    count = 0
    while count < len(steps) and rows % 16 == 0:
        rows, count = rows // 2, count + 1
    return count


def position(steps):
    place = jnp.int32(0)
    for axis, _, distance in steps:
        place = place * 2 + lax.rem(lax.div(lax.axis_index(axis), distance), 2)
    return place


def swap_parts(parts, steps):
    parts = lax.optimization_barrier(parts)
    return lax.optimization_barrier([swap(part, step) for part, step in zip(parts, steps)])


def reduce_parts(parts, orders, cuts):
    for at in range(cuts):
        half = parts[0].shape[0] // 2
        got = swap_parts([part[half:] for part in parts], [order[at] for order in orders])
        parts = [part[:half] + other for part, other in zip(parts, got)]
    return parts


def gather_parts(parts, orders, cuts):
    for at in range(cuts - 1, -1, -1):
        got = swap_parts(parts, [order[at] for order in orders])
        parts = [jnp.concatenate([part, other], 0) for part, other in zip(parts, got)]
    return parts


HIGHEST = lax.Precision.HIGHEST
GROUP = 16
PIECES = 2


def dot(a, b, transposed=False):
    dims = (((1,), (1 if transposed else 0,)), ((), ()))
    return lax.dot_general(a, b, dims, preferred_element_type=jnp.float32)


def absorb_kernel(east_parts, legs_ref, site_ref, double_ref, *out_refs):
    phys = double_ref.shape[0]
    legs = sum(east_parts)
    row = lax.broadcasted_iota(jnp.int32, (legs * GROUP, GROUP * phys), 0)
    column = lax.broadcasted_iota(jnp.int32, (legs * GROUP, GROUP * phys), 1)
    chosen = jnp.concatenate(
        [
            jnp.where(lax.broadcasted_iota(jnp.int32, (GROUP, phys), 1) == legs_ref[i], 1.0, 0.0)
            for i in range(legs)
        ],
        0,
    )
    values = lax.dot_general(
        chosen, double_ref[...], (((1,), (1,)), ((), ())), precision=HIGHEST, preferred_element_type=jnp.float32
    )
    spread = jnp.where(
        lax.broadcasted_iota(jnp.int32, (phys, GROUP * phys), 0)
        == lax.rem(lax.broadcasted_iota(jnp.int32, (phys, GROUP * phys), 1), phys),
        1.0,
        0.0,
    )
    values = jnp.dot(values, spread, precision=HIGHEST, preferred_element_type=jnp.float32)
    both = jnp.concatenate(split(jnp.where(lax.rem(row, GROUP) == lax.div(column, phys), values, 0.0), 2), 0)
    groups = site_ref.shape[0] // (GROUP * phys)
    for g in range(groups):
        rows = site_ref[g * GROUP * phys : (g + 1) * GROUP * phys, :]
        absorbed = dot(both, rows)
        absorbed = (absorbed[: legs * GROUP] + absorbed[legs * GROUP :]).astype(jnp.bfloat16)
        leg = 0
        for out_ref, count in zip(out_refs, east_parts):
            for e in range(count):
                piece = absorbed[(leg + e) * GROUP : (leg + e + 1) * GROUP]
                out_ref[e, g * GROUP : (g + 1) * GROUP, :] = piece.astype(out_ref.dtype)
            leg += count


def absorb(boundary_site, double_layer, legs, east_parts, dtype):
    legs = jnp.stack(legs).astype(jnp.int32)
    depth, phys, right = boundary_site.shape
    tiles = max(1, depth // 128)
    tile = depth // tiles
    out_shape, out_specs = [], []
    for count in east_parts:
        out_shape.append(jax.ShapeDtypeStruct((count, depth, right), dtype))
        out_specs.append(pl.BlockSpec((count, tile, right), lambda t: (0, t, 0)))
    return pl.pallas_call(
        functools.partial(absorb_kernel, east_parts),
        grid=(tiles,),
        out_shape=out_shape,
        in_specs=[
            pl.BlockSpec(memory_space=pltpu.SMEM),
            pl.BlockSpec((tile * phys, right), lambda t: (t, 0)),
            pl.BlockSpec(memory_space=pltpu.VMEM),
        ],
        out_specs=out_specs,
        compiler_params=pltpu.CompilerParams(vmem_limit_bytes=32 * 2**20),
        cost_estimate=pl.CostEstimate(
            flops=2 * 2 * depth * right * GROUP * phys * sum(east_parts), bytes_accessed=8 * depth * right * phys, transcendentals=0
        ),
    )(legs, boundary_site.reshape(depth * phys, right), double_layer)


def gram_kernel(chi, chunk, third, blocks, place_ref, *refs):
    block_refs, left_refs = refs[:blocks], refs[blocks:-7]
    kept_ref, sent_ref, left, columns, high, low, packed = refs[-7:]
    rows, width = left_refs[0].shape
    across = chi // width
    for i, left_ref in enumerate(left_refs):
        row_at = pl.multiple_of((place_ref[0] ^ (i // across)) * rows, 16)
        column_at = pl.multiple_of((place_ref[1] ^ (i % across)) * width, 128)
        left[pl.ds(row_at, rows), pl.ds(column_at, width)] = left_ref[...].astype(jnp.bfloat16)
    count, depth, width = block_refs[0].shape
    n = chi // BLOCK
    for i, block_ref in enumerate(block_refs):
        at = pl.ds(pl.multiple_of((place_ref[1] ^ i) * depth, depth), depth)
        for e in range(count):
            columns[at, e * width : (e + 1) * width] = block_ref[e].astype(jnp.bfloat16)
    for i in range(n // 2):
        at = slice(2 * i * BLOCK, 2 * (i + 1) * BLOCK)
        high[at], low[at] = split(dot(left[at], columns[...]), 2)
    for i in range(n):
        group, lo = (i, 0) if i < n // 2 else (n - 1 - i, (n - i) * BLOCK)
        at, upto = slice(i * BLOCK, (i + 1) * BLOCK), slice(0, (i + 1) * BLOCK)
        both = dot(jnp.concatenate([high[at], low[at]], 0), high[upto], True)
        packed[group * BLOCK : (group + 1) * BLOCK, lo : lo + (i + 1) * BLOCK] = (
            both[:BLOCK] + both[BLOCK:] + dot(high[at], low[upto], True)
        )
    half = kept_ref.shape[0]
    for part in range(3):
        lanes = slice(part * third, (part + 1) * third)
        for t in range(packed.shape[0] // chunk):
            rows_at = pl.ds(pl.multiple_of((place_ref[2 + part] ^ t) * chunk, 8), chunk)
            at = t * chunk
            to_ref = kept_ref if at < half else sent_ref
            to_ref[at % half : at % half + chunk, lanes] = packed[rows_at, lanes]


def gram_of_columns(blocks, left_blocks, places, chi, chunk):
    rows, width = chi // 2, chi + BLOCK
    count, _, right = blocks[0].shape
    whole = pl.BlockSpec(memory_space=pltpu.VMEM)
    return pl.pallas_call(
        functools.partial(gram_kernel, chi, chunk, width // 3, len(blocks)),
        out_shape=[jax.ShapeDtypeStruct((rows // 2, width), jnp.float32)] * 2
        + [jax.ShapeDtypeStruct((chi, chi), jnp.bfloat16)],
        in_specs=[pl.BlockSpec(memory_space=pltpu.SMEM)] + [whole] * (len(blocks) + len(left_blocks)),
        out_specs=[whole, whole, whole],
        scratch_shapes=[pltpu.VMEM((chi, count * right), jnp.bfloat16)] * 3 + [pltpu.VMEM((rows, width), jnp.float32)],
        compiler_params=pltpu.CompilerParams(vmem_limit_bytes=40 * 2**20),
        cost_estimate=pl.CostEstimate(
            flops=5 * chi * chi * count * right, bytes_accessed=12 * chi * chi, transcendentals=0
        ),
    )(places, *blocks, *left_blocks)


def sub(x, s):
    return jnp.broadcast_to(x[s : s + 1, :], x.shape)


def lane(x, k):
    return jnp.broadcast_to(x[:, k : k + 1], x.shape)


def inverse_factor(block, tasks):
    n, wide = BLOCK // 8, 8
    rows = [block[8 * b : 8 * b + 8] for b in range(n)]
    sub_id = lax.broadcasted_iota(jnp.int32, (8, BLOCK), 0)
    lane_id = lax.broadcasted_iota(jnp.int32, (8, BLOCK), 1)
    pivots = []
    head = [lane(rows[0], c) for c in range(wide)]
    for b in range(n):
        k = wide * b
        cols = [[head[c]] + [lane(rows[i], k + c) for i in range(b + 1, n)] for c in range(wide)]
        if b + 1 < n:
            head = [lane(rows[b + 1], k + wide + c) for c in range(wide)]
        inside = (lane_id >= k) & (lane_id < k + wide)
        for i in range(b, n):
            rows[i] = jnp.where(inside, 0.0, rows[i])
        pivot = jnp.ones((8, BLOCK), jnp.float32)
        for c in range(wide):
            d = sub(cols[c][0], c)
            inverse = 1.0 / d
            pivot = jnp.where(sub_id == c, d, pivot)
            for c2 in range(c + 1, wide):
                m = sub(cols[c][0], c2) * inverse
                for i in range(n - b):
                    cols[c2][i] = cols[c2][i] - cols[c][i] * m
            factors = [cols[c][i] * inverse for i in range(n - b)]
            if b + 1 < n:
                for c2 in range(wide):
                    head[c2] = head[c2] - factors[1] * sub(cols[c][1], c2)
            factors[0] = jnp.where(sub_id > c, factors[0], 0.0)
            row = jnp.where(lane_id == k + c, 1.0, sub(rows[b], c))
            for i in range(n - b):
                rows[b + i] = rows[b + i] - factors[i] * row
        pivots.append(pivot)
        for task in tasks[len(tasks) * b // n : len(tasks) * (b + 1) // n]:
            task()
    out = []
    for b in range(n):
        diagonal = sub_id + 8 * b
        row = jnp.where(lane_id < diagonal, rows[b], jnp.where(lane_id == diagonal, 1.0, 0.0))
        out.append(row * lax.rsqrt(pivots[b]))
    return jnp.concatenate(out, 0)


def split(x, pieces):
    out = []
    for i in range(pieces):
        out.append(x.astype(jnp.bfloat16))
        if i + 1 < pieces:
            x = x - out[-1].astype(jnp.float32)
    return out


def product(a, b):
    rows = a[0].shape[0]
    both = dot(jnp.concatenate(a, 0), b[0])
    return both[:rows] + both[rows:] + dot(a[0], b[1])


def factor_kernel(scale, chunk, place_ref, mine_ref, other_ref, left, *refs):
    factor_ref, weights_ref, packed, gram, now, later, inverses, solved, lows, low = refs
    chi = left.shape[0]
    n = chi // BLOCK
    half, third = mine_ref.shape[0], mine_ref.shape[1] // 3
    for part in range(3):
        lanes = slice(part * third, (part + 1) * third)
        for t in range(2 * half // chunk):
            at = pl.ds(pl.multiple_of((place_ref[2 + part] ^ t) * chunk, 8), chunk)
            from_ref = mine_ref if t * chunk < half else other_ref
            packed[at, lanes] = from_ref[t * chunk % half : t * chunk % half + chunk, lanes]
    for i in range(n):
        group, lo = (i, 0) if i < n // 2 else (n - 1 - i, (n - i) * BLOCK)
        for k in range(i + 1):
            block = packed[group * BLOCK : (group + 1) * BLOCK, lo + k * BLOCK : lo + (k + 1) * BLOCK]
            gram[i * BLOCK : (i + 1) * BLOCK, k * BLOCK : (k + 1) * BLOCK] = block
            if k < i:
                gram[k * BLOCK : (k + 1) * BLOCK, i * BLOCK : (i + 1) * BLOCK] = block.T

    wide = 2 * BLOCK
    every, top, bottom = slice(0, wide), slice(0, BLOCK), slice(BLOCK, wide)
    chunks = [slice(c, c + wide) for c in range(0, 2 * chi, wide)]
    earlier, before_last = slice(0, chi - 2 * wide), slice(0, chi - 3 * BLOCK)
    bind = functools.partial

    def span(first, size):
        return pl.ds(pl.multiple_of(first, BLOCK), size)

    def fresh(rows, columns):
        if columns.start < chi:
            return gram[rows, columns]
        return left[rows, columns.start - chi : columns.stop - chi].astype(jnp.float32)

    def solve(at, inverse, rows, columns, of_gram):
        values = product(inverse, split(now[rows, columns], PIECES))
        for i, piece in enumerate(split(values, PIECES)):
            solved[i, at, columns] = piece
        if of_gram:
            column = values.T
            low[columns, at] = column
            for i, piece in enumerate(split(column, PIECES)):
                lows[i, columns, at] = piece

    def taken(rows, before, columns):
        return product(
            [lows[i, rows, before] for i in range(PIECES)], [solved[i, before, columns] for i in range(PIECES)]
        )

    def less(to, at, source, rows, before, columns):
        to[at, columns] = source[at, columns] - taken(rows, before, columns)

    def fresh_less(rows, before, columns):
        later[:, columns] = fresh(rows, columns) - taken(rows, before, columns)

    def solve_all(at, inverse, rows):
        return [bind(solve, at, inverse, rows, columns, columns.start < chi) for columns in chunks]

    def less_all(*args):
        return [bind(less, *args, columns) for columns in chunks]

    for i in range(PIECES):
        solved[i] = jnp.zeros_like(solved[i])
        lows[i] = jnp.zeros_like(lows[i])
        inverses[i] = jnp.zeros_like(inverses[i])
    now[...] = jnp.zeros_like(now)
    for columns in chunks:
        later[:, columns] = fresh(every, columns)
    now[top, :BLOCK] = later[top, :BLOCK]

    def body(j, _):
        lo = j * wide
        last = span(lax.rem(lo + chi - BLOCK, chi), BLOCK)
        first, second, pair = span(lo, BLOCK), span(lo + BLOCK, BLOCK), span(lo, wide)
        following = jnp.minimum(lo + wide, chi - wide)
        next_pair, next_first = span(following, wide), span(following, BLOCK)

        inverse = [inverses[i] for i in range(PIECES)]
        tasks = solve_all(last, inverse, bottom) + less_all(now, every, later, pair, last)
        of_left = [columns for columns in chunks if columns.start >= chi]
        tasks += [bind(fresh_less, next_pair, earlier, columns) for columns in of_left]
        inverse = split(inverse_factor(now[top, first], tasks), PIECES)
        solve(first, inverse, top, second, True)
        block = now[bottom, second] - taken(second, first, second)

        tasks = solve_all(first, inverse, top) + less_all(now, bottom, now, second, first)
        tasks += [bind(fresh_less, next_pair, before_last, columns) for columns in chunks if columns.start < chi]
        tasks += [bind(less, later, every, later, next_pair, first, columns) for columns in of_left]
        inverse = split(inverse_factor(block, tasks), PIECES)
        for i, piece in enumerate(inverse):
            inverses[i] = piece
        solve(second, inverse, bottom, next_pair, True)
        now[top, next_first] = later[top, next_first] - taken(next_first, second, next_first)
        return 0

    lax.fori_loop(0, chi // wide, body, 0)
    for task in solve_all(slice(chi - BLOCK, chi), [inverses[i] for i in range(PIECES)], bottom):
        task()

    count = factor_ref.shape[0]
    first = place_ref[0] * count
    mine = pl.ds(pl.multiple_of(first, 16), count)
    row_id = lax.broadcasted_iota(jnp.int32, (count, chi), 0) + first
    column_id = lax.broadcasted_iota(jnp.int32, (count, chi), 1)
    factor_ref[...] = jnp.where(column_id <= row_id, low[mine, :] * (1.0 / scale), 0.0)
    weights_ref[...] = solved[0, mine, chi:]


def factorize(mine, other, left, places, rows, chunk, scale):
    chi = left.shape[0]
    whole = pl.BlockSpec(memory_space=pltpu.VMEM)
    return pl.pallas_call(
        functools.partial(factor_kernel, scale, chunk),
        out_shape=[
            jax.ShapeDtypeStruct((rows, chi), jnp.float32),
            jax.ShapeDtypeStruct((rows, chi), jnp.bfloat16),
        ],
        in_specs=[pl.BlockSpec(memory_space=pltpu.SMEM)] + [whole] * 3,
        out_specs=[whole, whole],
        scratch_shapes=[
            pltpu.VMEM((chi // 2, chi + BLOCK), jnp.float32),
            pltpu.VMEM((chi, chi), jnp.float32),
            pltpu.VMEM((2 * BLOCK, 2 * chi), jnp.float32),
            pltpu.VMEM((2 * BLOCK, 2 * chi), jnp.float32),
            pltpu.VMEM((PIECES, BLOCK, BLOCK), jnp.bfloat16),
            pltpu.VMEM((PIECES, chi, 2 * chi), jnp.bfloat16),
            pltpu.VMEM((PIECES, chi, chi), jnp.bfloat16),
            pltpu.VMEM((chi, chi), jnp.float32),
        ],
        compiler_params=pltpu.CompilerParams(vmem_limit_bytes=52 * 2**20),
        cost_estimate=pl.CostEstimate(flops=20 * 2 * chi**3, bytes_accessed=16 * chi**2, transcendentals=0),
    )(places, mine, other, left)


def site_kernel(scale, slots, place_ref, weights_ref, own_ref, *refs):
    *got_refs, out_ref = refs
    depth = own_ref.shape[1]
    mine = weights_ref[:, pl.ds(pl.multiple_of(place_ref[1] * depth, depth), depth)]
    first = pl.multiple_of((place_ref[1] ^ 1) * depth, depth)
    count = own_ref.shape[0] // slots
    for slot in range(slots):
        for i in range(count):
            e = (place_ref[0] ^ slot) * count + i
            total, at = dot(mine, own_ref[e]), first
            for got_ref in got_refs[slot::slots]:
                part = got_ref.shape[1]
                total = total + dot(weights_ref[:, pl.ds(at, part)], got_ref[i].astype(jnp.bfloat16))
                at = pl.multiple_of(at + part, BLOCK)
            out_ref[e] = scale * total


def make_site(weights, own, got, places, scale):
    rows, chi = weights.shape
    east, _, right = own.shape
    whole = pl.BlockSpec(memory_space=pltpu.VMEM)
    pieces = sum(got, [])
    return pl.pallas_call(
        functools.partial(site_kernel, scale, len(got[0])),
        out_shape=jax.ShapeDtypeStruct((east, rows, right), jnp.float32),
        in_specs=[pl.BlockSpec(memory_space=pltpu.SMEM)] + [whole] * (2 + len(pieces)),
        out_specs=whole,
        compiler_params=pltpu.CompilerParams(vmem_limit_bytes=32 * 2**20),
        cost_estimate=pl.CostEstimate(
            flops=2 * rows * chi * east * right, bytes_accessed=8 * east * chi * right, transcendentals=0
        ),
    )(places, weights, own, *pieces)


def shards(sizes, left_factor, boundary_site, double_layer):
    lb, rb, rep = sizes["lb"], sizes["rb"], sizes["rep"]
    l, p = lax.axis_index("lb"), lax.axis_index("rep")
    depth, phys, right = boundary_site.shape
    east = phys // rep
    chi = depth * rep
    row_count = left_factor.shape[0]
    scale = math.sqrt(phys * rb * right)
    steps = {axis: steps_of(axis, size) for axis, size in sizes.items()}
    core, across = steps["lb"][:1], steps["lb"][1:]

    left_blocks = gather_slots([(0, left_factor.astype(jnp.float32))], steps["rep"])
    left_blocks = [piece for _, piece in sorted(left_blocks, key=lambda pair: pair[0])]
    left_blocks = [gather_slots([(0, piece)], across[::-1] + core) for piece in left_blocks]
    left_blocks = [sorted(pieces, key=lambda pair: pair[0]) for pieces in left_blocks]
    left_blocks = [left_blocks[q][s][1] for s in range(lb) for q in range(rep)]

    east_part, right_parts = max(1, east // lb), max(1, lb // east)
    right_part = right // right_parts
    east_at, right_at = (l // right_parts) * east_part, (l % right_parts) * right_part
    legs = [(p ^ s) * east + east_at + i for s in range(1, rep) for i in range(east_part)]
    sent = absorb(boundary_site, double_layer, legs, [east_part] * (rep - 1), jnp.float32)
    if right_parts > 1:
        sent = [lax.dynamic_slice_in_dim(piece, right_at, right_part, 2) for piece in sent]
    got = [swap(piece, ("rep", rep, s)) for s, piece in zip(range(1, rep), sent)]
    (own,) = absorb(boundary_site, double_layer, [p * east + i for i in range(east)], [east], jnp.bfloat16)
    share = lax.dynamic_slice(own, (east_at, 0, right_at), (east_part, depth, right_part))
    got, left_blocks = lax.optimization_barrier((got, left_blocks))

    near = across[:1] + steps["rep"][:1] + steps["rb"][:1]
    far = [step for step in across + steps["rep"] + steps["rb"] if step not in near]
    orders = [near[i:] + near[:i] for i in range(3)]
    cut = cut_steps(near, chi // 4)
    chunk = (chi // 4) >> cut
    bits = [position(core + order[:cut]) for order in orders]
    places = jnp.stack([l, p] + bits).astype(jnp.int32)
    kept, sent, left = gram_of_columns([share] + got, left_blocks, places, chi, chunk)
    whole = kept + swap(sent, core[0])
    third = whole.shape[1] // 3
    parts = [whole[:, i * third : (i + 1) * third] for i in range(3)]
    parts = reduce_parts(parts, orders, cut)
    whole = jnp.concatenate(parts, 1)
    cut_depth = depth // 4
    ahead = rep == 2 and right_parts == 1 and len(across) == 1 and far and cut_depth % BLOCK == 0
    after = [got[0][:, cut_depth:]] if ahead else got
    pairs = [[piece, swap(piece, core[0])] for piece in after]
    whole, pairs = lax.optimization_barrier((whole, pairs))
    for i, step in enumerate(far):
        if ahead and i == 0:
            early = got[0][:, :cut_depth]
            other, crossed = swap_parts([whole, early], [step, across[0]])
            early = gather_slots([(0, early), (across[0][2], crossed)], core)
        else:
            other = swap(whole, step)
        whole = whole + other
    parts = [whole[:, i * third : (i + 1) * third] for i in range(3)]
    parts = gather_parts(parts, orders, cut)
    whole = jnp.concatenate(parts, 1)
    other = swap(whole, core[0])
    pairs, whole = lax.optimization_barrier((pairs, whole))
    got = [gather_slots(list(zip(range(2), pair)), across[::-1]) for pair in pairs]

    factor, weights = factorize(whole, other, left, places, row_count, chunk, scale)
    if rep == 2 and right_parts == 1:
        pieces = [[piece for _, piece in sorted(held, key=lambda pair: pair[0])] for held in ([early] if ahead else []) + got]
        site_q = make_site(weights, own, pieces, places, scale)
    else:
        nothing = double_layer[0, 0] * 0.0
        site = jnp.zeros((east, chi, right), jnp.bfloat16)
        site = lax.dynamic_update_slice(site, own, (0, p * depth, 0))
        for s, pieces in zip(range(1, rep), got):
            for slot, piece in pieces:
                owner = l ^ slot
                at = ((owner // right_parts) * east_part, (p ^ s) * depth, (owner % right_parts) * right_part)
                site = lax.dynamic_update_slice(site, (piece + nothing).astype(jnp.bfloat16), at)
        site_q = jnp.einsum("ik,ekr->eir", weights, site, preferred_element_type=jnp.float32) * scale
    return (site_q, factor)


def solution(mesh):
    return jax.shard_map(
        functools.partial(shards, dict(mesh.shape)),
        mesh=mesh,
        in_specs=(P("lb", "rep"), P("rep", None, "rb"), P()),
        out_specs=(P("rep", "lb", "rb"), P("lb", None)),
        check_vma=False,
    )
```

profile of v0, /device:TPU:0, one launch (start us, length us, event | category | flops | bytes accessed | tf_op | source)
XLA Modules:
  0.0 150.8 jit_solution(13311372420430638675)
XLA Ops:
  0.6 1.0 convert_element_type.3.refs_2_
  1.6 3.0 %collective-permute-start.1 = (f32[256,512]{1,0:T(8,128)S(1)}, f32[256,512]{1,0:T(8,128)S(1)}, u32[]{:S(2)}, u32[]{:S(2)}) collective-permute-start(f32[256,512]{1,0:T(8,128)S(1)} %convert_element_type.3.refs_2_), channel_id=1, source_target_pairs={{0,1},{1,0},{2,3},{3,2},{4,5},{5,4},{6,7},{7,6},{8,9},{9,8},{10,11... | collective-permute-start | bytes 1572872 | tf_op jit(solution)/shard_map/ppermute | solution.py:16
  4.7 1.5 collective-permute-start.4
  6.2 2.2 %copy-done = bf16[512,16,256]{2,1,0:T(8,128)(2,1)S(1)} copy-done((bf16[512,16,256]{2,1,0:T(8,128)(2,1)S(1)}, bf16[512,16,256]{2,1,0:T(8,128)(2,1)}, u32[]{:S(2)}) %copy-start) | copy-done | bytes 4194328
  8.4 0.7 copy-done.2
  9.1 3.0 %shard_map.51 = f32[2,512,256]{2,1,0:T(8,128)S(1)} custom-call(s32[2]{0:T(128)S(1)} %pad_add_fusion.legs_ref, bf16[8192,256]{1,0:T(8,128)(2,1)S(1)} %bitcast.16, f32[16,16]{1,0:T(8,128)S(1)} %copy-done.2), custom_call_target="tpu_custom_call" | custom-call | flops 268435456 | bytes 16777216 | tf_op jit(solution)/shard_map/pallas_call | solution.py:118
  12.2 0.6 collective-permute-start
  12.7 4.7 %collective-permute-done.1.refs_3_ = f32[256,512]{1,0:T(8,128)S(1)} collective-permute-done((f32[256,512]{1,0:T(8,128)S(1)}, f32[256,512]{1,0:T(8,128)S(1)}, u32[]{:S(2)}, u32[]{:S(2)}) %collective-permute-start.1) | collective-permute-done | bytes 524320 | tf_op jit(solution)/shard_map/ppermute | solution.py:16
  17.4 2.0 %collective-permute-start.5 = (f32[256,512]{1,0:T(8,128)S(1)}, f32[256,512]{1,0:T(8,128)}, u32[]{:S(2)}, u32[]{:S(2)}) collective-permute-start(f32[256,512]{1,0:T(8,128)S(1)} %collective-permute-done.1.refs_3_), channel_id=1, source_target_pairs={{0,16},{8,24},{16,0},{24,8},{1,17},{9,25},{17,1},{25,9},{2,18},{10... | collective-permute-start | bytes 1572872 | tf_op jit(solution)/shard_map/ppermute | solution.py:16
  20.0 9.9 %collective-permute-done.5.refs_7_ = f32[256,512]{1,0:T(8,128)} collective-permute-done((f32[256,512]{1,0:T(8,128)S(1)}, f32[256,512]{1,0:T(8,128)}, u32[]{:S(2)}, u32[]{:S(2)}) %collective-permute-start.5) | collective-permute-done | bytes 524320 | tf_op jit(solution)/shard_map/ppermute | solution.py:16
  30.1 2.2 %copy-done.1 = bf16[512,16,256]{2,1,0:T(8,128)(2,1)S(1)} copy-done((bf16[512,16,256]{2,1,0:T(8,128)(2,1)S(1)}, bf16[512,16,256]{2,1,0:T(8,128)(2,1)}, u32[]{:S(2)}) %copy-start.1) | copy-done | bytes 4194328
  32.3 4.4 %shard_map.50.own_ref = bf16[8,512,256]{2,1,0:T(8,128)(2,1)S(1)} custom-call(s32[8]{0:T(128)S(1)} %stack.68.legs_ref, bf16[8192,256]{1,0:T(8,128)(2,1)S(1)} %bitcast.17, f32[16,16]{1,0:T(8,128)S(1)} %copy-done.3), custom_call_target="tpu_custom_call" | custom-call | flops 1073741824 | bytes 16777216 | tf_op jit(solution)/shard_map/pallas_call | solution.py:118
  36.8 2.3 %collective-permute-done.refs_1_ = f32[2,512,256]{2,1,0:T(8,128)S(1)} collective-permute-done((f32[2,512,256]{2,1,0:T(8,128)S(1)}, f32[2,512,256]{2,1,0:T(8,128)S(1)}, u32[]{:S(2)}, u32[]{:S(2)}) %collective-permute-start) | collective-permute-done | bytes 1048608 | tf_op jit(solution)/shard_map/ppermute | solution.py:16
  39.1 6.2 %shard_map.52 = (f32[256,1152]{1,0:T(8,128)S(1)}, f32[256,1152]{1,0:T(8,128)S(1)}, bf16[1024,1024]{1,0:T(8,128)(2,1)S(1)}) custom-call(s32[5]{0:T(128)S(1)} %stack.59.place_ref, bf16[2,512,256]{2,1,0:T(8,128)(2,1)S(1)} %constant_dynamic-slice_fusion.refs_0_, f32[2,512,256]{2,1,0:T(8,128)S(1)} %collective-permute-done.refs_1_, ...), custom_call_target="tpu_custom_call" | custom-call | flops 2684354560 | bytes 12582912 | tf_op jit(solution)/shard_map/pallas_call | solution.py:174
  45.3 2.8 %collective-permute-done.8 = f32[256,1152]{1,0:T(8,128)S(1)} collective-permute-done((f32[256,1152]{1,0:T(8,128)S(1)}, f32[256,1152]{1,0:T(8,128)S(1)}, u32[]{:S(2)}, u32[]{:S(2)}) %collective-permute-start.8) | collective-permute-done | bytes 1179680 | tf_op jit(solution)/shard_map/ppermute | solution.py:16
  48.4 1.8 %collective-permute-start.10 = (f32[128,384]{1,0:T(8,128)S(1)}, f32[128,384]{1,0:T(8,128)S(1)}, u32[]{:S(2)}, u32[]{:S(2)}) collective-permute-start(f32[128,384]{1,0:T(8,128)S(1)} %get-tuple-element.74), channel_id=1, source_target_pairs={{0,1},{1,0},{2,3},{3,2},{4,5},{5,4},{6,7},{7,6},{8,9},{9,8},{10,11... | collective-permute-start | bytes 589832 | tf_op jit(solution)/shard_map/ppermute | solution.py:16
  50.2 1.6 %collective-permute-start.11 = (f32[128,384]{1,0:T(8,128)S(1)}, f32[128,384]{1,0:T(8,128)S(1)}, u32[]{:S(2)}, u32[]{:S(2)}) collective-permute-start(f32[128,384]{1,0:T(8,128)S(1)} %get-tuple-element.75), channel_id=1, source_target_pairs={{0,2},{2,0},{4,6},{6,4},{1,3},{3,1},{5,7},{7,5},{8,10},{10,8},{12,... | collective-permute-start | bytes 589832 | tf_op jit(solution)/shard_map/ppermute | solution.py:16
  51.7 1.5 collective-permute-start.9
  53.2 2.1 %collective-permute-done.10 = f32[128,384]{1,0:T(8,128)S(1)} collective-permute-done((f32[128,384]{1,0:T(8,128)S(1)}, f32[128,384]{1,0:T(8,128)S(1)}, u32[]{:S(2)}, u32[]{:S(2)}) %collective-permute-start.10) | collective-permute-done | bytes 196640 | tf_op jit(solution)/shard_map/ppermute | solution.py:16
  55.4 1.5 collective-permute-done.11
  56.8 1.3 collective-permute-done.9
  59.2 1.6 %collective-permute-start.14 = (f32[64,384]{1,0:T(8,128)S(1)}, f32[64,384]{1,0:T(8,128)S(1)}, u32[]{:S(2)}, u32[]{:S(2)}) collective-permute-start(f32[64,384]{1,0:T(8,128)S(1)} %slice.110), channel_id=1, source_target_pairs={{0,16},{8,24},{16,0},{24,8},{1,17},{9,25},{17,1},{25,9},{2,18},{10... | collective-permute-start | bytes 294920 | tf_op jit(solution)/shard_map/ppermute | solution.py:16
  60.8 2.2 %collective-permute-done.12 = f32[64,384]{1,0:T(8,128)S(1)} collective-permute-done((f32[64,384]{1,0:T(8,128)S(1)}, f32[64,384]{1,0:T(8,128)S(1)}, u32[]{:S(2)}, u32[]{:S(2)}) %collective-permute-start.12) | collective-permute-done | bytes 98336 | tf_op jit(solution)/shard_map/ppermute | solution.py:16
  63.9 1.8 %collective-permute-start.15 = (f32[32,384]{1,0:T(8,128)S(1)}, f32[32,384]{1,0:T(8,128)S(1)}, u32[]{:S(2)}, u32[]{:S(2)}) collective-permute-start(f32[32,384]{1,0:T(8,128)S(1)} %slice.112), channel_id=1, source_target_pairs={{0,2},{2,0},{4,6},{6,4},{1,3},{3,1},{5,7},{7,5},{8,10},{10,8},{12,... | collective-permute-start | bytes 147464 | tf_op jit(solution)/shard_map/ppermute | solution.py:16
  65.6 1.5 collective-permute-start.16
  67.1 1.5 %collective-permute-start.17 = (f32[32,384]{1,0:T(8,128)S(1)}, f32[32,384]{1,0:T(8,128)S(1)}, u32[]{:S(2)}, u32[]{:S(2)}) collective-permute-start(f32[32,384]{1,0:T(8,128)S(1)} %slice.116), channel_id=1, source_target_pairs={{0,1},{1,0},{2,3},{3,2},{4,5},{5,4},{6,7},{7,6},{8,9},{9,8},{10,11... | collective-permute-start | bytes 147464 | tf_op jit(solution)/shard_map/ppermute | solution.py:16
  68.8 0.9 collective-permute-done.16
  69.7 1.5 collective-permute-done.17
  71.3 0.6 collective-permute-start.20
  71.9 2.6 %collective-permute-start.19 = (f32[32,1152]{1,0:T(8,128)S(1)}, f32[32,1152]{1,0:T(8,128)S(1)}, u32[]{:S(2)}, u32[]{:S(2)}) collective-permute-start(f32[32,1152]{1,0:T(8,128)S(1)} %pad_maximum_fusion.3), channel_id=1, source_target_pairs={{0,4},{2,6},{4,0},{6,2},{1,5},{3,7},{5,1},{7,3},{8,12},{10,14},{12... | collective-permute-start | bytes 442376 | tf_op jit(solution)/shard_map/ppermute | solution.py:16
  74.5 6.7 %collective-permute-done.19 = f32[32,1152]{1,0:T(8,128)S(1)} collective-permute-done((f32[32,1152]{1,0:T(8,128)S(1)}, f32[32,1152]{1,0:T(8,128)S(1)}, u32[]{:S(2)}, u32[]{:S(2)}) %collective-permute-start.19) | collective-permute-done | bytes 147488 | tf_op jit(solution)/shard_map/ppermute | solution.py:16
  81.3 1.5 %collective-permute-start.22 = (f32[32,384]{1,0:T(8,128)S(1)}, f32[32,384]{1,0:T(8,128)S(1)}, u32[]{:S(2)}, u32[]{:S(2)}) collective-permute-start(f32[32,384]{1,0:T(8,128)S(1)} %get-tuple-element.98), channel_id=1, source_target_pairs={{0,16},{8,24},{16,0},{24,8},{1,17},{9,25},{17,1},{25,9},{2,18},{10... | collective-permute-start | bytes 147464 | tf_op jit(solution)/shard_map/ppermute | solution.py:16
  83.4 2.0 %collective-permute-done.21 = f32[32,384]{1,0:T(8,128)S(1)} collective-permute-done((f32[32,384]{1,0:T(8,128)S(1)}, f32[32,384]{1,0:T(8,128)S(1)}, u32[]{:S(2)}, u32[]{:S(2)}) %collective-permute-start.21) | collective-permute-done | bytes 49184 | tf_op jit(solution)/shard_map/ppermute | solution.py:16
  85.5 1.5 collective-permute-done.23
  87.0 0.6 collective-permute-start.24
  87.6 1.9 %collective-permute-start.25 = (f32[64,384]{1,0:T(8,128)S(1)}, f32[64,384]{1,0:T(8,128)S(1)}, u32[]{:S(2)}, u32[]{:S(2)}) collective-permute-start(f32[64,384]{1,0:T(8,128)S(1)} %pad_maximum_fusion.5), channel_id=1, source_target_pairs={{0,2},{2,0},{4,6},{6,4},{1,3},{3,1},{5,7},{7,5},{8,10},{10,8},{12,... | collective-permute-start | bytes 294920 | tf_op jit(solution)/shard_map/ppermute | solution.py:16
  90.0 1.7 %collective-permute-done.24 = f32[64,384]{1,0:T(8,128)S(1)} collective-permute-done((f32[64,384]{1,0:T(8,128)S(1)}, f32[64,384]{1,0:T(8,128)S(1)}, u32[]{:S(2)}, u32[]{:S(2)}) %collective-permute-start.24) | collective-permute-done | bytes 98336 | tf_op jit(solution)/shard_map/ppermute | solution.py:16
  92.2 2.2 %collective-permute-done.26 = f32[64,384]{1,0:T(8,128)S(1)} collective-permute-done((f32[64,384]{1,0:T(8,128)S(1)}, f32[64,384]{1,0:T(8,128)S(1)}, u32[]{:S(2)}, u32[]{:S(2)}) %collective-permute-start.26) | collective-permute-done | bytes 98336 | tf_op jit(solution)/shard_map/ppermute | solution.py:16
  94.5 0.8 collective-permute-start.27
  95.2 1.5 collective-permute-start.28
  96.8 3.4 %collective-permute-done.27 = f32[128,384]{1,0:T(8,128)S(1)} collective-permute-done((f32[128,384]{1,0:T(8,128)S(1)}, f32[128,384]{1,0:T(8,128)S(1)}, u32[]{:S(2)}, u32[]{:S(2)}) %collective-permute-start.27) | collective-permute-done | bytes 196640 | tf_op jit(solution)/shard_map/ppermute | solution.py:16
  100.2 0.7 collective-permute-done.28
  100.9 1.5 collective-permute-done.29
  103.1 1.2 collective-permute-start.33
  104.3 0.8 collective-permute-start.34
  105.4 1.0 copy-done.5
  106.4 40.9 %shard_map.53 = (f32[256,1024]{1,0:T(8,128)}, bf16[256,1024]{1,0:T(8,128)(2,1)S(1)}) custom-call(s32[5]{0:T(128)S(1)} %stack.59.place_ref, f32[256,1152]{1,0:T(8,128)S(1)} %maximum_maximum_fusion.mine_ref, f32[256,1152]{1,0:T(8,128)} %copy-done.5, bf16[1024,1024]{1,0:T(8,128)(2,1)} %copy-done.4), custom_call_target="tpu_custom_call" | custom-call | flops 42949672960 | bytes 16777216 | tf_op jit(solution)/shard_map/pallas_call | solution.py:364
  147.4 3.4 %shard_map.54 = f32[8,256,256]{2,1,0:T(8,128)} custom-call(s32[5]{0:T(128)S(1)} %stack.59.place_ref, bf16[256,1024]{1,0:T(8,128)(2,1)S(1)} %get-tuple-element.117.weights_ref, bf16[8,512,256]{2,1,0:T(8,128)(2,1)S(1)} %shard_map.50.own_ref, f32[2,128,256]{2,1,0:T(8,128)S(1)} %slice.97.refs_0_, f32[2,128,256]{2,1,0:T(8,128)S(1)} %collective-permute-done.31.refs_1_, ...), custom_call_target="tpu_custom_call" | custom-call | flops 1073741824 | bytes 16777216 | tf_op jit(solution)/shard_map/pallas_call | solution.py:409
  (70 shorter events, 6.0 us)
Async XLA Ops:
  1.6 15.8 %collective-permute-start.1 = (f32[256,512]{1,0:T(8,128)S(1)}, f32[256,512]{1,0:T(8,128)S(1)}, u32[]{:S(2)}, u32[]{:S(2)}) collective-permute-start(f32[256,512]{1,0:T(8,128)S(1)} %convert_element_type.3.refs_2_), channel_id=1, source_target_pairs={{0,1},{1,0},{2,3},{3,2},{4,5},{5,4},{6,7},{7,6},{8,9},{9,8},{10,11... | collective-permute-start | bytes 1572872 | tf_op jit(solution)/shard_map/ppermute | solution.py:16
  4.7 15.3 %collective-permute-start.4 = (f32[256,512]{1,0:T(8,128)S(1)}, f32[256,512]{1,0:T(8,128)}, u32[]{:S(2)}, u32[]{:S(2)}) collective-permute-start(f32[256,512]{1,0:T(8,128)S(1)} %convert_element_type.3.refs_2_), channel_id=1, source_target_pairs={{0,16},{8,24},{16,0},{24,8},{1,17},{9,25},{17,1},{25,9},{2,18},{10... | collective-permute-start | bytes 1572872 | tf_op jit(solution)/shard_map/ppermute | solution.py:16
  6.2 2.2 %copy-start = (bf16[512,16,256]{2,1,0:T(8,128)(2,1)S(1)}, bf16[512,16,256]{2,1,0:T(8,128)(2,1)}, u32[]{:S(2)}) copy-start(bf16[512,16,256]{2,1,0:T(8,128)(2,1)} %param.4) | copy-start | bytes 12582916
  8.4 0.7 copy-start.2
  9.1 21.0 %copy-start.3 = (f32[16,16]{1,0:T(8,128)S(1)}, f32[16,16]{1,0:T(8,128)}, u32[]{:S(2)}) copy-start(f32[16,16]{1,0:T(8,128)} %double_ref.3) | copy-start | bytes 3076
  12.2 26.9 %collective-permute-start = (f32[2,512,256]{2,1,0:T(8,128)S(1)}, f32[2,512,256]{2,1,0:T(8,128)S(1)}, u32[]{:S(2)}, u32[]{:S(2)}) collective-permute-start(f32[2,512,256]{2,1,0:T(8,128)S(1)} %shard_map.51), channel_id=1, source_target_pairs={{0,1},{1,0},{2,3},{3,2},{4,5},{5,4},{6,7},{7,6},{8,9},{9,8},{10,11... | collective-permute-start | bytes 3145736 | tf_op jit(solution)/shard_map/ppermute | solution.py:16
  17.4 12.5 %collective-permute-start.5 = (f32[256,512]{1,0:T(8,128)S(1)}, f32[256,512]{1,0:T(8,128)}, u32[]{:S(2)}, u32[]{:S(2)}) collective-permute-start(f32[256,512]{1,0:T(8,128)S(1)} %collective-permute-done.1.refs_3_), channel_id=1, source_target_pairs={{0,16},{8,24},{16,0},{24,8},{1,17},{9,25},{17,1},{25,9},{2,18},{10... | collective-permute-start | bytes 1572872 | tf_op jit(solution)/shard_map/ppermute | solution.py:16
  19.5 17.3 %collective-permute-start.2 = (f32[256,512]{1,0:T(8,128)S(1)}, f32[256,512]{1,0:T(8,128)}, u32[]{:S(2)}, u32[]{:S(2)}) collective-permute-start(f32[256,512]{1,0:T(8,128)S(1)} %convert_element_type.3.refs_2_), channel_id=1, source_target_pairs={{0,8},{8,0},{16,24},{24,16},{1,9},{9,1},{17,25},{25,17},{2,10},{10... | collective-permute-start | bytes 1572872 | tf_op jit(solution)/shard_map/ppermute | solution.py:16
  19.5 19.6 %collective-permute-start.3 = (f32[256,512]{1,0:T(8,128)S(1)}, f32[256,512]{1,0:T(8,128)}, u32[]{:S(2)}, u32[]{:S(2)}) collective-permute-start(f32[256,512]{1,0:T(8,128)S(1)} %collective-permute-done.1.refs_3_), channel_id=1, source_target_pairs={{0,8},{8,0},{16,24},{24,16},{1,9},{9,1},{17,25},{25,17},{2,10},{10... | collective-permute-start | bytes 1572872 | tf_op jit(solution)/shard_map/ppermute | solution.py:16
  20.0 19.1 %collective-permute-start.6 = (f32[256,512]{1,0:T(8,128)}, f32[256,512]{1,0:T(8,128)}, u32[]{:S(2)}, u32[]{:S(2)}) collective-permute-start(f32[256,512]{1,0:T(8,128)} %collective-permute-done.4.refs_6_), channel_id=1, source_target_pairs={{0,8},{8,0},{16,24},{24,16},{1,9},{9,1},{17,25},{25,17},{2,10},{10... | collective-permute-start | bytes 1572872 | tf_op jit(solution)/shard_map/ppermute | solution.py:16
  29.9 9.2 %collective-permute-start.7 = (f32[256,512]{1,0:T(8,128)}, f32[256,512]{1,0:T(8,128)}, u32[]{:S(2)}, u32[]{:S(2)}) collective-permute-start(f32[256,512]{1,0:T(8,128)} %collective-permute-done.5.refs_7_), channel_id=1, source_target_pairs={{0,8},{8,0},{16,24},{24,16},{1,9},{9,1},{17,25},{25,17},{2,10},{10... | collective-permute-start | bytes 1572872 | tf_op jit(solution)/shard_map/ppermute | solution.py:16
  30.1 2.2 %copy-start.1 = (bf16[512,16,256]{2,1,0:T(8,128)(2,1)S(1)}, bf16[512,16,256]{2,1,0:T(8,128)(2,1)}, u32[]{:S(2)}) copy-start(bf16[512,16,256]{2,1,0:T(8,128)(2,1)} %param.4) | copy-start | bytes 12582916
  45.3 3.1 %copy-start.4 = (bf16[1024,1024]{1,0:T(8,128)(2,1)}, bf16[1024,1024]{1,0:T(8,128)(2,1)S(1)}, u32[]{:S(2)}) copy-start(bf16[1024,1024]{1,0:T(8,128)(2,1)S(1)} %get-tuple-element.116.left) | copy-start | bytes 6291460
  45.3 2.9 %collective-permute-start.8 = (f32[256,1152]{1,0:T(8,128)S(1)}, f32[256,1152]{1,0:T(8,128)S(1)}, u32[]{:S(2)}, u32[]{:S(2)}) collective-permute-start(f32[256,1152]{1,0:T(8,128)S(1)} %get-tuple-element.72), channel_id=1, source_target_pairs={{0,8},{8,0},{16,24},{24,16},{1,9},{9,1},{17,25},{25,17},{2,10},{10... | collective-permute-start | bytes 3538952 | tf_op jit(solution)/shard_map/ppermute | solution.py:16
  48.4 7.0 %collective-permute-start.10 = (f32[128,384]{1,0:T(8,128)S(1)}, f32[128,384]{1,0:T(8,128)S(1)}, u32[]{:S(2)}, u32[]{:S(2)}) collective-permute-start(f32[128,384]{1,0:T(8,128)S(1)} %get-tuple-element.74), channel_id=1, source_target_pairs={{0,1},{1,0},{2,3},{3,2},{4,5},{5,4},{6,7},{7,6},{8,9},{9,8},{10,11... | collective-permute-start | bytes 589832 | tf_op jit(solution)/shard_map/ppermute | solution.py:16
  50.2 6.7 %collective-permute-start.11 = (f32[128,384]{1,0:T(8,128)S(1)}, f32[128,384]{1,0:T(8,128)S(1)}, u32[]{:S(2)}, u32[]{:S(2)}) collective-permute-start(f32[128,384]{1,0:T(8,128)S(1)} %get-tuple-element.75), channel_id=1, source_target_pairs={{0,2},{2,0},{4,6},{6,4},{1,3},{3,1},{5,7},{7,5},{8,10},{10,8},{12,... | collective-permute-start | bytes 589832 | tf_op jit(solution)/shard_map/ppermute | solution.py:16
  51.7 6.4 %collective-permute-start.9 = (f32[128,384]{1,0:T(8,128)S(1)}, f32[128,384]{1,0:T(8,128)S(1)}, u32[]{:S(2)}, u32[]{:S(2)}) collective-permute-start(f32[128,384]{1,0:T(8,128)S(1)} %get-tuple-element.73), channel_id=1, source_target_pairs={{0,16},{8,24},{16,0},{24,8},{1,17},{9,25},{17,1},{25,9},{2,18},{10... | collective-permute-start | bytes 589832 | tf_op jit(solution)/shard_map/ppermute | solution.py:16
  58.3 4.7 %collective-permute-start.12 = (f32[64,384]{1,0:T(8,128)S(1)}, f32[64,384]{1,0:T(8,128)S(1)}, u32[]{:S(2)}, u32[]{:S(2)}) collective-permute-start(f32[64,384]{1,0:T(8,128)S(1)} %slice.106), channel_id=1, source_target_pairs={{0,1},{1,0},{2,3},{3,2},{4,5},{5,4},{6,7},{7,6},{8,9},{9,8},{10,11... | collective-permute-start | bytes 294920 | tf_op jit(solution)/shard_map/ppermute | solution.py:16
  58.9 4.6 %collective-permute-start.13 = (f32[64,384]{1,0:T(8,128)S(1)}, f32[64,384]{1,0:T(8,128)S(1)}, u32[]{:S(2)}, u32[]{:S(2)}) collective-permute-start(f32[64,384]{1,0:T(8,128)S(1)} %slice.108), channel_id=1, source_target_pairs={{0,2},{2,0},{4,6},{6,4},{1,3},{3,1},{5,7},{7,5},{8,10},{10,8},{12,... | collective-permute-start | bytes 294920 | tf_op jit(solution)/shard_map/ppermute | solution.py:16
  59.2 4.6 %collective-permute-start.14 = (f32[64,384]{1,0:T(8,128)S(1)}, f32[64,384]{1,0:T(8,128)S(1)}, u32[]{:S(2)}, u32[]{:S(2)}) collective-permute-start(f32[64,384]{1,0:T(8,128)S(1)} %slice.110), channel_id=1, source_target_pairs={{0,16},{8,24},{16,0},{24,8},{1,17},{9,25},{17,1},{25,9},{2,18},{10... | collective-permute-start | bytes 294920 | tf_op jit(solution)/shard_map/ppermute | solution.py:16
  63.9 5.0 %collective-permute-start.15 = (f32[32,384]{1,0:T(8,128)S(1)}, f32[32,384]{1,0:T(8,128)S(1)}, u32[]{:S(2)}, u32[]{:S(2)}) collective-permute-start(f32[32,384]{1,0:T(8,128)S(1)} %slice.112), channel_id=1, source_target_pairs={{0,2},{2,0},{4,6},{6,4},{1,3},{3,1},{5,7},{7,5},{8,10},{10,8},{12,... | collective-permute-start | bytes 147464 | tf_op jit(solution)/shard_map/ppermute | solution.py:16
  65.6 4.1 %collective-permute-start.16 = (f32[32,384]{1,0:T(8,128)S(1)}, f32[32,384]{1,0:T(8,128)S(1)}, u32[]{:S(2)}, u32[]{:S(2)}) collective-permute-start(f32[32,384]{1,0:T(8,128)S(1)} %slice.114), channel_id=1, source_target_pairs={{0,16},{8,24},{16,0},{24,8},{1,17},{9,25},{17,1},{25,9},{2,18},{10... | collective-permute-start | bytes 147464 | tf_op jit(solution)/shard_map/ppermute | solution.py:16
  67.1 4.1 %collective-permute-start.17 = (f32[32,384]{1,0:T(8,128)S(1)}, f32[32,384]{1,0:T(8,128)S(1)}, u32[]{:S(2)}, u32[]{:S(2)}) collective-permute-start(f32[32,384]{1,0:T(8,128)S(1)} %slice.116), channel_id=1, source_target_pairs={{0,1},{1,0},{2,3},{3,2},{4,5},{5,4},{6,7},{7,6},{8,9},{9,8},{10,11... | collective-permute-start | bytes 147464 | tf_op jit(solution)/shard_map/ppermute | solution.py:16
  68.7 2.6 %collective-permute-start.18 = (f32[2,384,256]{2,1,0:T(8,128)S(1)}, f32[2,384,256]{2,1,0:T(8,128)S(1)}, u32[]{:S(2)}, u32[]{:S(2)}) collective-permute-start(f32[2,384,256]{2,1,0:T(8,128)S(1)} %slice.96.refs_4_), channel_id=1, source_target_pairs={{0,8},{8,0},{16,24},{24,16},{1,9},{9,1},{17,25},{25,17},{2,10},{10... | collective-permute-start | bytes 2359304 | tf_op jit(solution)/shard_map/ppermute | solution.py:16
  71.3 9.9 %collective-permute-start.20 = (f32[2,128,256]{2,1,0:T(8,128)S(1)}, f32[2,128,256]{2,1,0:T(8,128)S(1)}, u32[]{:S(2)}, u32[]{:S(2)}) collective-permute-start(f32[2,128,256]{2,1,0:T(8,128)S(1)} %slice.97.refs_0_), channel_id=1, source_target_pairs={{0,16},{8,24},{16,0},{24,8},{1,17},{9,25},{17,1},{25,9},{2,18},{10... | collective-permute-start | bytes 786440 | tf_op jit(solution)/shard_map/ppermute | solution.py:16
  71.9 9.3 %collective-permute-start.19 = (f32[32,1152]{1,0:T(8,128)S(1)}, f32[32,1152]{1,0:T(8,128)S(1)}, u32[]{:S(2)}, u32[]{:S(2)}) collective-permute-start(f32[32,1152]{1,0:T(8,128)S(1)} %pad_maximum_fusion.3), channel_id=1, source_target_pairs={{0,4},{2,6},{4,0},{6,2},{1,5},{3,7},{5,1},{7,3},{8,12},{10,14},{12... | collective-permute-start | bytes 442376 | tf_op jit(solution)/shard_map/ppermute | solution.py:16
  81.2 4.2 %collective-permute-start.21 = (f32[32,384]{1,0:T(8,128)S(1)}, f32[32,384]{1,0:T(8,128)S(1)}, u32[]{:S(2)}, u32[]{:S(2)}) collective-permute-start(f32[32,384]{1,0:T(8,128)S(1)} %get-tuple-element.97), channel_id=1, source_target_pairs={{0,2},{2,0},{4,6},{6,4},{1,3},{3,1},{5,7},{7,5},{8,10},{10,8},{12,... | collective-permute-start | bytes 147464 | tf_op jit(solution)/shard_map/ppermute | solution.py:16
  81.3 4.2 %collective-permute-start.22 = (f32[32,384]{1,0:T(8,128)S(1)}, f32[32,384]{1,0:T(8,128)S(1)}, u32[]{:S(2)}, u32[]{:S(2)}) collective-permute-start(f32[32,384]{1,0:T(8,128)S(1)} %get-tuple-element.98), channel_id=1, source_target_pairs={{0,16},{8,24},{16,0},{24,8},{1,17},{9,25},{17,1},{25,9},{2,18},{10... | collective-permute-start | bytes 147464 | tf_op jit(solution)/shard_map/ppermute | solution.py:16
  82.9 4.1 %collective-permute-start.23 = (f32[32,384]{1,0:T(8,128)S(1)}, f32[32,384]{1,0:T(8,128)S(1)}, u32[]{:S(2)}, u32[]{:S(2)}) collective-permute-start(f32[32,384]{1,0:T(8,128)S(1)} %get-tuple-element.99), channel_id=1, source_target_pairs={{0,1},{1,0},{2,3},{3,2},{4,5},{5,4},{6,7},{7,6},{8,9},{9,8},{10,11... | collective-permute-start | bytes 147464 | tf_op jit(solution)/shard_map/ppermute | solution.py:16
  87.0 4.7 %collective-permute-start.24 = (f32[64,384]{1,0:T(8,128)S(1)}, f32[64,384]{1,0:T(8,128)S(1)}, u32[]{:S(2)}, u32[]{:S(2)}) collective-permute-start(f32[64,384]{1,0:T(8,128)S(1)} %pad_maximum_fusion.4), channel_id=1, source_target_pairs={{0,1},{1,0},{2,3},{3,2},{4,5},{5,4},{6,7},{7,6},{8,9},{9,8},{10,11... | collective-permute-start | bytes 294920 | tf_op jit(solution)/shard_map/ppermute | solution.py:16
  87.6 4.6 %collective-permute-start.25 = (f32[64,384]{1,0:T(8,128)S(1)}, f32[64,384]{1,0:T(8,128)S(1)}, u32[]{:S(2)}, u32[]{:S(2)}) collective-permute-start(f32[64,384]{1,0:T(8,128)S(1)} %pad_maximum_fusion.5), channel_id=1, source_target_pairs={{0,2},{2,0},{4,6},{6,4},{1,3},{3,1},{5,7},{7,5},{8,10},{10,8},{12,... | collective-permute-start | bytes 294920 | tf_op jit(solution)/shard_map/ppermute | solution.py:16
  89.5 4.9 %collective-permute-start.26 = (f32[64,384]{1,0:T(8,128)S(1)}, f32[64,384]{1,0:T(8,128)S(1)}, u32[]{:S(2)}, u32[]{:S(2)}) collective-permute-start(f32[64,384]{1,0:T(8,128)S(1)} %pad_maximum_fusion.6), channel_id=1, source_target_pairs={{0,16},{8,24},{16,0},{24,8},{1,17},{9,25},{17,1},{25,9},{2,18},{10... | collective-permute-start | bytes 294920 | tf_op jit(solution)/shard_map/ppermute | solution.py:16
  94.5 5.7 %collective-permute-start.27 = (f32[128,384]{1,0:T(8,128)S(1)}, f32[128,384]{1,0:T(8,128)S(1)}, u32[]{:S(2)}, u32[]{:S(2)}) collective-permute-start(f32[128,384]{1,0:T(8,128)S(1)} %pad_maximum_fusion), channel_id=1, source_target_pairs={{0,16},{8,24},{16,0},{24,8},{1,17},{9,25},{17,1},{25,9},{2,18},{10... | collective-permute-start | bytes 589832 | tf_op jit(solution)/shard_map/ppermute | solution.py:16
  95.2 5.7 %collective-permute-start.28 = (f32[128,384]{1,0:T(8,128)S(1)}, f32[128,384]{1,0:T(8,128)S(1)}, u32[]{:S(2)}, u32[]{:S(2)}) collective-permute-start(f32[128,384]{1,0:T(8,128)S(1)} %pad_maximum_fusion.1), channel_id=1, source_target_pairs={{0,1},{1,0},{2,3},{3,2},{4,5},{5,4},{6,7},{7,6},{8,9},{9,8},{10,11... | collective-permute-start | bytes 589832 | tf_op jit(solution)/shard_map/ppermute | solution.py:16
  96.7 5.7 %collective-permute-start.29 = (f32[128,384]{1,0:T(8,128)S(1)}, f32[128,384]{1,0:T(8,128)S(1)}, u32[]{:S(2)}, u32[]{:S(2)}) collective-permute-start(f32[128,384]{1,0:T(8,128)S(1)} %pad_maximum_fusion.2), channel_id=1, source_target_pairs={{0,2},{2,0},{4,6},{6,4},{1,3},{3,1},{5,7},{7,5},{8,10},{10,8},{12,... | collective-permute-start | bytes 589832 | tf_op jit(solution)/shard_map/ppermute | solution.py:16
  102.5 2.9 %collective-permute-start.30 = (f32[256,1152]{1,0:T(8,128)S(1)}, f32[256,1152]{1,0:T(8,128)S(1)}, u32[]{:S(2)}, u32[]{:S(2)}) collective-permute-start(f32[256,1152]{1,0:T(8,128)S(1)} %maximum_maximum_fusion.mine_ref), channel_id=1, source_target_pairs={{0,8},{8,0},{16,24},{24,16},{1,9},{9,1},{17,25},{25,17},{2,10},{10... | collective-permute-start | bytes 3538952 | tf_op jit(solution)/shard_map/ppermute | solution.py:16
  102.5 44.8 %collective-permute-start.31 = (f32[2,128,256]{2,1,0:T(8,128)S(1)}, f32[2,128,256]{2,1,0:T(8,128)S(1)}, u32[]{:S(2)}, u32[]{:S(2)}) collective-permute-start(f32[2,128,256]{2,1,0:T(8,128)S(1)} %slice.97.refs_0_), channel_id=1, source_target_pairs={{0,8},{8,0},{16,24},{24,16},{1,9},{9,1},{17,25},{25,17},{2,10},{10... | collective-permute-start | bytes 786440 | tf_op jit(solution)/shard_map/ppermute | solution.py:16
  103.0 44.3 %collective-permute-start.32 = (f32[2,128,256]{2,1,0:T(8,128)S(1)}, f32[2,128,256]{2,1,0:T(8,128)S(1)}, u32[]{:S(2)}, u32[]{:S(2)}) collective-permute-start(f32[2,128,256]{2,1,0:T(8,128)S(1)} %collective-permute-done.20.refs_2_), channel_id=1, source_target_pairs={{0,8},{8,0},{16,24},{24,16},{1,9},{9,1},{17,25},{25,17},{2,10},{10... | collective-permute-start | bytes 786440 | tf_op jit(solution)/shard_map/ppermute | solution.py:16
  103.1 44.2 %collective-permute-start.33 = (f32[2,384,256]{2,1,0:T(8,128)S(1)}, f32[2,384,256]{2,1,0:T(8,128)S(1)}, u32[]{:S(2)}, u32[]{:S(2)}) collective-permute-start(f32[2,384,256]{2,1,0:T(8,128)S(1)} %slice.96.refs_4_), channel_id=1, source_target_pairs={{0,16},{8,24},{16,0},{24,8},{1,17},{9,25},{17,1},{25,9},{2,18},{10... | collective-permute-start | bytes 2359304 | tf_op jit(solution)/shard_map/ppermute | solution.py:16
  104.3 43.1 %collective-permute-start.34 = (f32[2,384,256]{2,1,0:T(8,128)S(1)}, f32[2,384,256]{2,1,0:T(8,128)S(1)}, u32[]{:S(2)}, u32[]{:S(2)}) collective-permute-start(f32[2,384,256]{2,1,0:T(8,128)S(1)} %collective-permute-done.18.refs_5_), channel_id=1, source_target_pairs={{0,16},{8,24},{16,0},{24,8},{1,17},{9,25},{17,1},{25,9},{2,18},{10... | collective-permute-start | bytes 2359304 | tf_op jit(solution)/shard_map/ppermute | solution.py:16
  105.4 1.0 copy-start.5
where the time goes:
time: 151 us
  Pallas kernels  58 us (38%)
  waiting for transfers between devices  50.5 us (33%)
  starting transfers between devices  33.3 us (22%)
  local copies, waits for them, and re-layouts  6.49 us (4%)
  other arithmetic  1.54 us (1%)
    ppermute x35, waiting for transfers between devices, swap(): return lax.ppermute(array, axis, [(i, i ^ distance) for i in range(size)])  50.5 us
    pallas_call x1, Pallas kernels, factorize(): pl.pallas_call(functools.partial(factor_kernel, scale, chunk), out_shape=...  40.9 us
    ppermute x35, starting transfers between devices, swap(): return lax.ppermute(array, axis, [(i, i ^ distance) for i in range(size)])  33.3 us
    pallas_call x2, Pallas kernels, absorb(): pl.pallas_call(functools.partial(absorb_kernel, east_parts), grid=(tiles,...  7.48 us
    pallas_call x1, Pallas kernels, gram_of_columns(): pl.pallas_call(functools.partial(gram_kernel, chi, chunk, width // 3, len...  6.17 us
    unnamed x12, local copies, waits for them, and re-layouts  6.11 us
    pallas_call x1, Pallas kernels, make_site(): pl.pallas_call(functools.partial(site_kernel, scale, len(got[0])), out_sh...  3.44 us
  transfers between devices with their start and end apart: 35, of which 23 were waited for; matrix products, arithmetic and copies ran while one was open for 0% of the time, Pallas kernels for 32%

commit v1 on v0

--- a/solution.py
+++ b/solution.py
@@ -193,7 +193,7 @@
     return jnp.broadcast_to(x[:, k : k + 1], x.shape)
 
 
-def inverse_factor(block, tasks):
+def inverse_factor(block, tasks, spread):
     n, wide = BLOCK // 8, 8
     rows = [block[8 * b : 8 * b + 8] for b in range(n)]
     sub_id = lax.broadcasted_iota(jnp.int32, (8, BLOCK), 0)
@@ -209,22 +209,36 @@
         for i in range(b, n):
             rows[i] = jnp.where(inside, 0.0, rows[i])
         pivot = jnp.ones((8, BLOCK), jnp.float32)
+        near = min(2, n - b)
+        multiples, scaled = {}, []
         for c in range(wide):
             d = sub(cols[c][0], c)
             inverse = 1.0 / d
             pivot = jnp.where(sub_id == c, d, pivot)
             for c2 in range(c + 1, wide):
-                m = sub(cols[c][0], c2) * inverse
-                for i in range(n - b):
-                    cols[c2][i] = cols[c2][i] - cols[c][i] * m
-            factors = [cols[c][i] * inverse for i in range(n - b)]
+                multiples[c2, c] = sub(cols[c][0], c2) * inverse
+                for i in range(near):
+                    cols[c2][i] = cols[c2][i] - cols[c][i] * multiples[c2, c]
+            factors = [cols[c][i] * inverse for i in range(near)]
             if b + 1 < n:
+                at = (b % 2 * wide + c) * 8
+                spread[at : at + 8, :] = cols[c][1]
                 for c2 in range(wide):
-                    head[c2] = head[c2] - factors[1] * sub(cols[c][1], c2)
+                    head[c2] = head[c2] - factors[1] * jnp.broadcast_to(spread[at + c2 : at + c2 + 1, :], (8, BLOCK))
             factors[0] = jnp.where(sub_id > c, factors[0], 0.0)
             row = jnp.where(lane_id == k + c, 1.0, sub(rows[b], c))
-            for i in range(n - b):
+            scaled.append(row * inverse)
+            for i in range(near):
                 rows[b + i] = rows[b + i] - factors[i] * row
+        if b + 2 < n:
+            for c in range(wide - 1, 0, -1):
+                for c2 in range(c):
+                    scaled[c2] = scaled[c2] - multiples[c, c2] * scaled[c]
+            for i in range(2, n - b):
+                total = cols[0][i] * scaled[0]
+                for c in range(1, wide):
+                    total = total + cols[c][i] * scaled[c]
+                rows[b + i] = rows[b + i] - total
         pivots.append(pivot)
         for task in tasks[len(tasks) * b // n : len(tasks) * (b + 1) // n]:
             task()
@@ -252,7 +266,7 @@
 
 
 def factor_kernel(scale, chunk, place_ref, mine_ref, other_ref, left, *refs):
-    factor_ref, weights_ref, packed, gram, now, later, inverses, solved, lows, low = refs
+    factor_ref, weights_ref, packed, gram, now, later, inverses, spread, solved, lows, low = refs
     chi = left.shape[0]
     n = chi // BLOCK
     half, third = mine_ref.shape[0], mine_ref.shape[1] // 3
@@ -312,8 +326,8 @@
         return [bind(less, *args, columns) for columns in chunks]
 
     for i in range(PIECES):
-        solved[i] = jnp.zeros_like(solved[i])
-        lows[i] = jnp.zeros_like(lows[i])
+        solved[i, before_last] = jnp.zeros((chi - 3 * BLOCK, 2 * chi), jnp.bfloat16)
+        lows[i, :, before_last] = jnp.zeros((chi, chi - 3 * BLOCK), jnp.bfloat16)
         inverses[i] = jnp.zeros_like(inverses[i])
     now[...] = jnp.zeros_like(now)
     for columns in chunks:
@@ -331,14 +345,14 @@
         tasks = solve_all(last, inverse, bottom) + less_all(now, every, later, pair, last)
         of_left = [columns for columns in chunks if columns.start >= chi]
         tasks += [bind(fresh_less, next_pair, earlier, columns) for columns in of_left]
-        inverse = split(inverse_factor(now[top, first], tasks), PIECES)
+        inverse = split(inverse_factor(now[top, first], tasks, spread), PIECES)
         solve(first, inverse, top, second, True)
         block = now[bottom, second] - taken(second, first, second)
 
         tasks = solve_all(first, inverse, top) + less_all(now, bottom, now, second, first)
         tasks += [bind(fresh_less, next_pair, before_last, columns) for columns in chunks if columns.start < chi]
         tasks += [bind(less, later, every, later, next_pair, first, columns) for columns in of_left]
-        inverse = split(inverse_factor(block, tasks), PIECES)
+        inverse = split(inverse_factor(block, tasks, spread), PIECES)
         for i, piece in enumerate(inverse):
             inverses[i] = piece
         solve(second, inverse, bottom, next_pair, True)
@@ -346,7 +360,7 @@
         return 0
 
     lax.fori_loop(0, chi // wide, body, 0)
-    for task in solve_all(slice(chi - BLOCK, chi), [inverses[i] for i in range(PIECES)], bottom):
+    for task in solve_all(slice(chi - BLOCK, chi), [inverses[i] for i in range(PIECES)], bottom)[chi // wide - 1 :]:
         task()
 
     count = factor_ref.shape[0]
@@ -375,6 +389,7 @@
             pltpu.VMEM((2 * BLOCK, 2 * chi), jnp.float32),
             pltpu.VMEM((2 * BLOCK, 2 * chi), jnp.float32),
             pltpu.VMEM((PIECES, BLOCK, BLOCK), jnp.bfloat16),
+            pltpu.VMEM((BLOCK, BLOCK), jnp.float32),
             pltpu.VMEM((PIECES, chi, 2 * chi), jnp.bfloat16),
             pltpu.VMEM((PIECES, chi, chi), jnp.bfloat16),
             pltpu.VMEM((chi, chi), jnp.float32),

time: 151 us -> 147 us (0.974)
  Pallas kernels: 58 us -> 53.7 us
    pallas_call x1, Pallas kernels: 40.9 us -> 36.6 us  [factorize(): pl.pallas_call(functools.partial(factor_kernel, scale, chunk), out_shape=...]
  transfers between devices with their start and end apart: 35 -> 35, of which waited for: 23 -> 23; matrix products, arithmetic and copies ran while one was open for 0% -> 0% of each run, Pallas kernels for 32% -> 30%
where the time goes in v1:
time: 147 us; the launch traced here: 146 us
  Pallas kernels  53.7 us (37%)
  waiting for transfers between devices  50.5 us (34%)
  starting transfers between devices  33.3 us (23%)
  local copies, waits for them, and re-layouts  6.49 us (4%)
  other arithmetic  1.54 us (1%)
    ppermute x35, waiting for transfers between devices, swap(): return lax.ppermute(array, axis, [(i, i ^ distance) for i in range(size)])  50.5 us
    pallas_call x1, Pallas kernels, factorize(): pl.pallas_call(functools.partial(factor_kernel, scale, chunk), out_shape=...  36.6 us
    ppermute x35, starting transfers between devices, swap(): return lax.ppermute(array, axis, [(i, i ^ distance) for i in range(size)])  33.3 us
    pallas_call x2, Pallas kernels, absorb(): pl.pallas_call(functools.partial(absorb_kernel, east_parts), grid=(tiles,...  7.48 us
    pallas_call x1, Pallas kernels, gram_of_columns(): pl.pallas_call(functools.partial(gram_kernel, chi, chunk, width // 3, len...  6.17 us
    unnamed x12, local copies, waits for them, and re-layouts  6.11 us
    pallas_call x1, Pallas kernels, make_site(): pl.pallas_call(functools.partial(site_kernel, scale, len(got[0])), out_sh...  3.44 us
  transfers between devices with their start and end apart: 35, of which 23 were waited for; matrix products, arithmetic and copies ran while one was open for 0% of the time, Pallas kernels for 30%

profile of v1, /device:TPU:0, one launch (start us, length us, event | category | flops | bytes accessed | tf_op | source)
XLA Modules:
  0.0 146.4 jit_solution(7577315705636349002)
XLA Ops:
  0.6 1.0 convert_element_type.3.refs_2_
  1.6 3.0 %collective-permute-start.1 = (f32[256,512]{1,0:T(8,128)S(1)}, f32[256,512]{1,0:T(8,128)S(1)}, u32[]{:S(2)}, u32[]{:S(2)}) collective-permute-start(f32[256,512]{1,0:T(8,128)S(1)} %convert_element_type.3.refs_2_), channel_id=1, source_target_pairs={{0,1},{1,0},{2,3},{3,2},{4,5},{5,4},{6,7},{7,6},{8,9},{9,8},{10,11... | collective-permute-start | bytes 1572872 | tf_op jit(solution)/shard_map/ppermute | solution.py:16
  4.7 1.5 %collective-permute-start.4 = (f32[256,512]{1,0:T(8,128)S(1)}, f32[256,512]{1,0:T(8,128)}, u32[]{:S(2)}, u32[]{:S(2)}) collective-permute-start(f32[256,512]{1,0:T(8,128)S(1)} %convert_element_type.3.refs_2_), channel_id=1, source_target_pairs={{0,16},{8,24},{16,0},{24,8},{1,17},{9,25},{17,1},{25,9},{2,18},{10... | collective-permute-start | bytes 1572872 | tf_op jit(solution)/shard_map/ppermute | solution.py:16
  6.2 2.2 %copy-done = bf16[512,16,256]{2,1,0:T(8,128)(2,1)S(1)} copy-done((bf16[512,16,256]{2,1,0:T(8,128)(2,1)S(1)}, bf16[512,16,256]{2,1,0:T(8,128)(2,1)}, u32[]{:S(2)}) %copy-start) | copy-done | bytes 4194328
  8.4 0.7 copy-done.2
  9.1 3.0 %shard_map.51 = f32[2,512,256]{2,1,0:T(8,128)S(1)} custom-call(s32[2]{0:T(128)S(1)} %pad_add_fusion.legs_ref, bf16[8192,256]{1,0:T(8,128)(2,1)S(1)} %bitcast.16, f32[16,16]{1,0:T(8,128)S(1)} %copy-done.2), custom_call_target="tpu_custom_call" | custom-call | flops 268435456 | bytes 16777216 | tf_op jit(solution)/shard_map/pallas_call | solution.py:118
  12.2 0.6 collective-permute-start
  12.7 4.7 %collective-permute-done.1.refs_3_ = f32[256,512]{1,0:T(8,128)S(1)} collective-permute-done((f32[256,512]{1,0:T(8,128)S(1)}, f32[256,512]{1,0:T(8,128)S(1)}, u32[]{:S(2)}, u32[]{:S(2)}) %collective-permute-start.1) | collective-permute-done | bytes 524320 | tf_op jit(solution)/shard_map/ppermute | solution.py:16
  17.4 2.0 %collective-permute-start.5 = (f32[256,512]{1,0:T(8,128)S(1)}, f32[256,512]{1,0:T(8,128)}, u32[]{:S(2)}, u32[]{:S(2)}) collective-permute-start(f32[256,512]{1,0:T(8,128)S(1)} %collective-permute-done.1.refs_3_), channel_id=1, source_target_pairs={{0,16},{8,24},{16,0},{24,8},{1,17},{9,25},{17,1},{25,9},{2,18},{10... | collective-permute-start | bytes 1572872 | tf_op jit(solution)/shard_map/ppermute | solution.py:16
  20.0 9.9 %collective-permute-done.5.refs_7_ = f32[256,512]{1,0:T(8,128)} collective-permute-done((f32[256,512]{1,0:T(8,128)S(1)}, f32[256,512]{1,0:T(8,128)}, u32[]{:S(2)}, u32[]{:S(2)}) %collective-permute-start.5) | collective-permute-done | bytes 524320 | tf_op jit(solution)/shard_map/ppermute | solution.py:16
  30.1 2.2 %copy-done.1 = bf16[512,16,256]{2,1,0:T(8,128)(2,1)S(1)} copy-done((bf16[512,16,256]{2,1,0:T(8,128)(2,1)S(1)}, bf16[512,16,256]{2,1,0:T(8,128)(2,1)}, u32[]{:S(2)}) %copy-start.1) | copy-done | bytes 4194328
  32.3 4.4 %shard_map.50.own_ref = bf16[8,512,256]{2,1,0:T(8,128)(2,1)S(1)} custom-call(s32[8]{0:T(128)S(1)} %stack.68.legs_ref, bf16[8192,256]{1,0:T(8,128)(2,1)S(1)} %bitcast.17, f32[16,16]{1,0:T(8,128)S(1)} %copy-done.3), custom_call_target="tpu_custom_call" | custom-call | flops 1073741824 | bytes 16777216 | tf_op jit(solution)/shard_map/pallas_call | solution.py:118
  36.8 2.3 %collective-permute-done.refs_1_ = f32[2,512,256]{2,1,0:T(8,128)S(1)} collective-permute-done((f32[2,512,256]{2,1,0:T(8,128)S(1)}, f32[2,512,256]{2,1,0:T(8,128)S(1)}, u32[]{:S(2)}, u32[]{:S(2)}) %collective-permute-start) | collective-permute-done | bytes 1048608 | tf_op jit(solution)/shard_map/ppermute | solution.py:16
  39.1 6.2 %shard_map.52 = (f32[256,1152]{1,0:T(8,128)S(1)}, f32[256,1152]{1,0:T(8,128)S(1)}, bf16[1024,1024]{1,0:T(8,128)(2,1)S(1)}) custom-call(s32[5]{0:T(128)S(1)} %stack.59.place_ref, bf16[2,512,256]{2,1,0:T(8,128)(2,1)S(1)} %constant_dynamic-slice_fusion.refs_0_, f32[2,512,256]{2,1,0:T(8,128)S(1)} %collective-permute-done.refs_1_, ...), custom_call_target="tpu_custom_call" | custom-call | flops 2684354560 | bytes 12582912 | tf_op jit(solution)/shard_map/pallas_call | solution.py:174
  45.3 2.8 %collective-permute-done.8 = f32[256,1152]{1,0:T(8,128)S(1)} collective-permute-done((f32[256,1152]{1,0:T(8,128)S(1)}, f32[256,1152]{1,0:T(8,128)S(1)}, u32[]{:S(2)}, u32[]{:S(2)}) %collective-permute-start.8) | collective-permute-done | bytes 1179680 | tf_op jit(solution)/shard_map/ppermute | solution.py:16
  48.4 1.8 %collective-permute-start.10 = (f32[128,384]{1,0:T(8,128)S(1)}, f32[128,384]{1,0:T(8,128)S(1)}, u32[]{:S(2)}, u32[]{:S(2)}) collective-permute-start(f32[128,384]{1,0:T(8,128)S(1)} %get-tuple-element.74), channel_id=1, source_target_pairs={{0,1},{1,0},{2,3},{3,2},{4,5},{5,4},{6,7},{7,6},{8,9},{9,8},{10,11... | collective-permute-start | bytes 589832 | tf_op jit(solution)/shard_map/ppermute | solution.py:16
  50.2 1.6 %collective-permute-start.11 = (f32[128,384]{1,0:T(8,128)S(1)}, f32[128,384]{1,0:T(8,128)S(1)}, u32[]{:S(2)}, u32[]{:S(2)}) collective-permute-start(f32[128,384]{1,0:T(8,128)S(1)} %get-tuple-element.75), channel_id=1, source_target_pairs={{0,2},{2,0},{4,6},{6,4},{1,3},{3,1},{5,7},{7,5},{8,10},{10,8},{12,... | collective-permute-start | bytes 589832 | tf_op jit(solution)/shard_map/ppermute | solution.py:16
  51.7 1.5 %collective-permute-start.9 = (f32[128,384]{1,0:T(8,128)S(1)}, f32[128,384]{1,0:T(8,128)S(1)}, u32[]{:S(2)}, u32[]{:S(2)}) collective-permute-start(f32[128,384]{1,0:T(8,128)S(1)} %get-tuple-element.73), channel_id=1, source_target_pairs={{0,16},{8,24},{16,0},{24,8},{1,17},{9,25},{17,1},{25,9},{2,18},{10... | collective-permute-start | bytes 589832 | tf_op jit(solution)/shard_map/ppermute | solution.py:16
  53.2 2.1 %collective-permute-done.10 = f32[128,384]{1,0:T(8,128)S(1)} collective-permute-done((f32[128,384]{1,0:T(8,128)S(1)}, f32[128,384]{1,0:T(8,128)S(1)}, u32[]{:S(2)}, u32[]{:S(2)}) %collective-permute-start.10) | collective-permute-done | bytes 196640 | tf_op jit(solution)/shard_map/ppermute | solution.py:16
  55.4 1.5 collective-permute-done.11
  56.8 1.3 collective-permute-done.9
  59.2 1.6 %collective-permute-start.14 = (f32[64,384]{1,0:T(8,128)S(1)}, f32[64,384]{1,0:T(8,128)S(1)}, u32[]{:S(2)}, u32[]{:S(2)}) collective-permute-start(f32[64,384]{1,0:T(8,128)S(1)} %slice.110), channel_id=1, source_target_pairs={{0,16},{8,24},{16,0},{24,8},{1,17},{9,25},{17,1},{25,9},{2,18},{10... | collective-permute-start | bytes 294920 | tf_op jit(solution)/shard_map/ppermute | solution.py:16
  60.8 2.2 %collective-permute-done.12 = f32[64,384]{1,0:T(8,128)S(1)} collective-permute-done((f32[64,384]{1,0:T(8,128)S(1)}, f32[64,384]{1,0:T(8,128)S(1)}, u32[]{:S(2)}, u32[]{:S(2)}) %collective-permute-start.12) | collective-permute-done | bytes 98336 | tf_op jit(solution)/shard_map/ppermute | solution.py:16
  63.9 1.8 %collective-permute-start.15 = (f32[32,384]{1,0:T(8,128)S(1)}, f32[32,384]{1,0:T(8,128)S(1)}, u32[]{:S(2)}, u32[]{:S(2)}) collective-permute-start(f32[32,384]{1,0:T(8,128)S(1)} %slice.112), channel_id=1, source_target_pairs={{0,2},{2,0},{4,6},{6,4},{1,3},{3,1},{5,7},{7,5},{8,10},{10,8},{12,... | collective-permute-start | bytes 147464 | tf_op jit(solution)/shard_map/ppermute | solution.py:16
  65.6 1.5 %collective-permute-start.16 = (f32[32,384]{1,0:T(8,128)S(1)}, f32[32,384]{1,0:T(8,128)S(1)}, u32[]{:S(2)}, u32[]{:S(2)}) collective-permute-start(f32[32,384]{1,0:T(8,128)S(1)} %slice.114), channel_id=1, source_target_pairs={{0,16},{8,24},{16,0},{24,8},{1,17},{9,25},{17,1},{25,9},{2,18},{10... | collective-permute-start | bytes 147464 | tf_op jit(solution)/shard_map/ppermute | solution.py:16
  67.1 1.5 %collective-permute-start.17 = (f32[32,384]{1,0:T(8,128)S(1)}, f32[32,384]{1,0:T(8,128)S(1)}, u32[]{:S(2)}, u32[]{:S(2)}) collective-permute-start(f32[32,384]{1,0:T(8,128)S(1)} %slice.116), channel_id=1, source_target_pairs={{0,1},{1,0},{2,3},{3,2},{4,5},{5,4},{6,7},{7,6},{8,9},{9,8},{10,11... | collective-permute-start | bytes 147464 | tf_op jit(solution)/shard_map/ppermute | solution.py:16
  68.8 0.9 collective-permute-done.16
  69.7 1.5 %collective-permute-done.17 = f32[32,384]{1,0:T(8,128)S(1)} collective-permute-done((f32[32,384]{1,0:T(8,128)S(1)}, f32[32,384]{1,0:T(8,128)S(1)}, u32[]{:S(2)}, u32[]{:S(2)}) %collective-permute-start.17) | collective-permute-done | bytes 49184 | tf_op jit(solution)/shard_map/ppermute | solution.py:16
  71.3 0.6 collective-permute-start.20
  71.9 2.6 %collective-permute-start.19 = (f32[32,1152]{1,0:T(8,128)S(1)}, f32[32,1152]{1,0:T(8,128)S(1)}, u32[]{:S(2)}, u32[]{:S(2)}) collective-permute-start(f32[32,1152]{1,0:T(8,128)S(1)} %pad_maximum_fusion.3), channel_id=1, source_target_pairs={{0,4},{2,6},{4,0},{6,2},{1,5},{3,7},{5,1},{7,3},{8,12},{10,14},{12... | collective-permute-start | bytes 442376 | tf_op jit(solution)/shard_map/ppermute | solution.py:16
  74.5 6.7 %collective-permute-done.19 = f32[32,1152]{1,0:T(8,128)S(1)} collective-permute-done((f32[32,1152]{1,0:T(8,128)S(1)}, f32[32,1152]{1,0:T(8,128)S(1)}, u32[]{:S(2)}, u32[]{:S(2)}) %collective-permute-start.19) | collective-permute-done | bytes 147488 | tf_op jit(solution)/shard_map/ppermute | solution.py:16
  81.3 1.5 %collective-permute-start.22 = (f32[32,384]{1,0:T(8,128)S(1)}, f32[32,384]{1,0:T(8,128)S(1)}, u32[]{:S(2)}, u32[]{:S(2)}) collective-permute-start(f32[32,384]{1,0:T(8,128)S(1)} %get-tuple-element.98), channel_id=1, source_target_pairs={{0,16},{8,24},{16,0},{24,8},{1,17},{9,25},{17,1},{25,9},{2,18},{10... | collective-permute-start | bytes 147464 | tf_op jit(solution)/shard_map/ppermute | solution.py:16
  83.4 2.0 %collective-permute-done.21 = f32[32,384]{1,0:T(8,128)S(1)} collective-permute-done((f32[32,384]{1,0:T(8,128)S(1)}, f32[32,384]{1,0:T(8,128)S(1)}, u32[]{:S(2)}, u32[]{:S(2)}) %collective-permute-start.21) | collective-permute-done | bytes 49184 | tf_op jit(solution)/shard_map/ppermute | solution.py:16
  85.5 1.5 %collective-permute-done.23 = f32[32,384]{1,0:T(8,128)S(1)} collective-permute-done((f32[32,384]{1,0:T(8,128)S(1)}, f32[32,384]{1,0:T(8,128)S(1)}, u32[]{:S(2)}, u32[]{:S(2)}) %collective-permute-start.23) | collective-permute-done | bytes 49184 | tf_op jit(solution)/shard_map/ppermute | solution.py:16
  87.0 0.6 collective-permute-start.24
  87.6 1.9 %collective-permute-start.25 = (f32[64,384]{1,0:T(8,128)S(1)}, f32[64,384]{1,0:T(8,128)S(1)}, u32[]{:S(2)}, u32[]{:S(2)}) collective-permute-start(f32[64,384]{1,0:T(8,128)S(1)} %pad_maximum_fusion.5), channel_id=1, source_target_pairs={{0,2},{2,0},{4,6},{6,4},{1,3},{3,1},{5,7},{7,5},{8,10},{10,8},{12,... | collective-permute-start | bytes 294920 | tf_op jit(solution)/shard_map/ppermute | solution.py:16
  90.0 1.7 %collective-permute-done.24 = f32[64,384]{1,0:T(8,128)S(1)} collective-permute-done((f32[64,384]{1,0:T(8,128)S(1)}, f32[64,384]{1,0:T(8,128)S(1)}, u32[]{:S(2)}, u32[]{:S(2)}) %collective-permute-start.24) | collective-permute-done | bytes 98336 | tf_op jit(solution)/shard_map/ppermute | solution.py:16
  92.2 2.2 %collective-permute-done.26 = f32[64,384]{1,0:T(8,128)S(1)} collective-permute-done((f32[64,384]{1,0:T(8,128)S(1)}, f32[64,384]{1,0:T(8,128)S(1)}, u32[]{:S(2)}, u32[]{:S(2)}) %collective-permute-start.26) | collective-permute-done | bytes 98336 | tf_op jit(solution)/shard_map/ppermute | solution.py:16
  94.5 0.8 collective-permute-start.27
  95.2 1.5 %collective-permute-start.28 = (f32[128,384]{1,0:T(8,128)S(1)}, f32[128,384]{1,0:T(8,128)S(1)}, u32[]{:S(2)}, u32[]{:S(2)}) collective-permute-start(f32[128,384]{1,0:T(8,128)S(1)} %pad_maximum_fusion.1), channel_id=1, source_target_pairs={{0,1},{1,0},{2,3},{3,2},{4,5},{5,4},{6,7},{7,6},{8,9},{9,8},{10,11... | collective-permute-start | bytes 589832 | tf_op jit(solution)/shard_map/ppermute | solution.py:16
  96.8 3.4 %collective-permute-done.27 = f32[128,384]{1,0:T(8,128)S(1)} collective-permute-done((f32[128,384]{1,0:T(8,128)S(1)}, f32[128,384]{1,0:T(8,128)S(1)}, u32[]{:S(2)}, u32[]{:S(2)}) %collective-permute-start.27) | collective-permute-done | bytes 196640 | tf_op jit(solution)/shard_map/ppermute | solution.py:16
  100.2 0.7 collective-permute-done.28
  100.9 1.5 %collective-permute-done.29 = f32[128,384]{1,0:T(8,128)S(1)} collective-permute-done((f32[128,384]{1,0:T(8,128)S(1)}, f32[128,384]{1,0:T(8,128)S(1)}, u32[]{:S(2)}, u32[]{:S(2)}) %collective-permute-start.29) | collective-permute-done | bytes 196640 | tf_op jit(solution)/shard_map/ppermute | solution.py:16
  103.1 1.2 collective-permute-start.33
  104.3 0.8 collective-permute-start.34
  105.4 1.0 copy-done.5
  106.4 36.6 %shard_map.53 = (f32[256,1024]{1,0:T(8,128)}, bf16[256,1024]{1,0:T(8,128)(2,1)S(1)}) custom-call(s32[5]{0:T(128)S(1)} %stack.59.place_ref, f32[256,1152]{1,0:T(8,128)S(1)} %maximum_maximum_fusion.mine_ref, f32[256,1152]{1,0:T(8,128)} %copy-done.5, bf16[1024,1024]{1,0:T(8,128)(2,1)} %copy-done.4), custom_call_target="tpu_custom_call" | custom-call | flops 42949672960 | bytes 16777216 | tf_op jit(solution)/shard_map/pallas_call | solution.py:378
  143.0 3.4 %shard_map.54 = f32[8,256,256]{2,1,0:T(8,128)} custom-call(s32[5]{0:T(128)S(1)} %stack.59.place_ref, bf16[256,1024]{1,0:T(8,128)(2,1)S(1)} %get-tuple-element.117.weights_ref, bf16[8,512,256]{2,1,0:T(8,128)(2,1)S(1)} %shard_map.50.own_ref, f32[2,128,256]{2,1,0:T(8,128)S(1)} %slice.97.refs_0_, f32[2,128,256]{2,1,0:T(8,128)S(1)} %collective-permute-done.31.refs_1_, ...), custom_call_target="tpu_custom_call" | custom-call | flops 1073741824 | bytes 16777216 | tf_op jit(solution)/shard_map/pallas_call | solution.py:424
  (70 shorter events, 6.0 us)
Async XLA Ops:
  1.6 15.8 %collective-permute-start.1 = (f32[256,512]{1,0:T(8,128)S(1)}, f32[256,512]{1,0:T(8,128)S(1)}, u32[]{:S(2)}, u32[]{:S(2)}) collective-permute-start(f32[256,512]{1,0:T(8,128)S(1)} %convert_element_type.3.refs_2_), channel_id=1, source_target_pairs={{0,1},{1,0},{2,3},{3,2},{4,5},{5,4},{6,7},{7,6},{8,9},{9,8},{10,11... | collective-permute-start | bytes 1572872 | tf_op jit(solution)/shard_map/ppermute | solution.py:16
  4.7 15.3 %collective-permute-start.4 = (f32[256,512]{1,0:T(8,128)S(1)}, f32[256,512]{1,0:T(8,128)}, u32[]{:S(2)}, u32[]{:S(2)}) collective-permute-start(f32[256,512]{1,0:T(8,128)S(1)} %convert_element_type.3.refs_2_), channel_id=1, source_target_pairs={{0,16},{8,24},{16,0},{24,8},{1,17},{9,25},{17,1},{25,9},{2,18},{10... | collective-permute-start | bytes 1572872 | tf_op jit(solution)/shard_map/ppermute | solution.py:16
  6.2 2.2 %copy-start = (bf16[512,16,256]{2,1,0:T(8,128)(2,1)S(1)}, bf16[512,16,256]{2,1,0:T(8,128)(2,1)}, u32[]{:S(2)}) copy-start(bf16[512,16,256]{2,1,0:T(8,128)(2,1)} %param.4) | copy-start | bytes 12582916
  8.4 0.7 copy-start.2
  9.1 21.0 %copy-start.3 = (f32[16,16]{1,0:T(8,128)S(1)}, f32[16,16]{1,0:T(8,128)}, u32[]{:S(2)}) copy-start(f32[16,16]{1,0:T(8,128)} %double_ref.3) | copy-start | bytes 3076
  12.2 26.9 %collective-permute-start = (f32[2,512,256]{2,1,0:T(8,128)S(1)}, f32[2,512,256]{2,1,0:T(8,128)S(1)}, u32[]{:S(2)}, u32[]{:S(2)}) collective-permute-start(f32[2,512,256]{2,1,0:T(8,128)S(1)} %shard_map.51), channel_id=1, source_target_pairs={{0,1},{1,0},{2,3},{3,2},{4,5},{5,4},{6,7},{7,6},{8,9},{9,8},{10,11... | collective-permute-start | bytes 3145736 | tf_op jit(solution)/shard_map/ppermute | solution.py:16
  17.4 12.5 %collective-permute-start.5 = (f32[256,512]{1,0:T(8,128)S(1)}, f32[256,512]{1,0:T(8,128)}, u32[]{:S(2)}, u32[]{:S(2)}) collective-permute-start(f32[256,512]{1,0:T(8,128)S(1)} %collective-permute-done.1.refs_3_), channel_id=1, source_target_pairs={{0,16},{8,24},{16,0},{24,8},{1,17},{9,25},{17,1},{25,9},{2,18},{10... | collective-permute-start | bytes 1572872 | tf_op jit(solution)/shard_map/ppermute | solution.py:16
  19.5 17.3 %collective-permute-start.2 = (f32[256,512]{1,0:T(8,128)S(1)}, f32[256,512]{1,0:T(8,128)}, u32[]{:S(2)}, u32[]{:S(2)}) collective-permute-start(f32[256,512]{1,0:T(8,128)S(1)} %convert_element_type.3.refs_2_), channel_id=1, source_target_pairs={{0,8},{8,0},{16,24},{24,16},{1,9},{9,1},{17,25},{25,17},{2,10},{10... | collective-permute-start | bytes 1572872 | tf_op jit(solution)/shard_map/ppermute | solution.py:16
  19.5 19.6 %collective-permute-start.3 = (f32[256,512]{1,0:T(8,128)S(1)}, f32[256,512]{1,0:T(8,128)}, u32[]{:S(2)}, u32[]{:S(2)}) collective-permute-start(f32[256,512]{1,0:T(8,128)S(1)} %collective-permute-done.1.refs_3_), channel_id=1, source_target_pairs={{0,8},{8,0},{16,24},{24,16},{1,9},{9,1},{17,25},{25,17},{2,10},{10... | collective-permute-start | bytes 1572872 | tf_op jit(solution)/shard_map/ppermute | solution.py:16
  20.0 19.1 %collective-permute-start.6 = (f32[256,512]{1,0:T(8,128)}, f32[256,512]{1,0:T(8,128)}, u32[]{:S(2)}, u32[]{:S(2)}) collective-permute-start(f32[256,512]{1,0:T(8,128)} %collective-permute-done.4.refs_6_), channel_id=1, source_target_pairs={{0,8},{8,0},{16,24},{24,16},{1,9},{9,1},{17,25},{25,17},{2,10},{10... | collective-permute-start | bytes 1572872 | tf_op jit(solution)/shard_map/ppermute | solution.py:16
  29.9 9.2 %collective-permute-start.7 = (f32[256,512]{1,0:T(8,128)}, f32[256,512]{1,0:T(8,128)}, u32[]{:S(2)}, u32[]{:S(2)}) collective-permute-start(f32[256,512]{1,0:T(8,128)} %collective-permute-done.5.refs_7_), channel_id=1, source_target_pairs={{0,8},{8,0},{16,24},{24,16},{1,9},{9,1},{17,25},{25,17},{2,10},{10... | collective-permute-start | bytes 1572872 | tf_op jit(solution)/shard_map/ppermute | solution.py:16
  30.1 2.2 %copy-start.1 = (bf16[512,16,256]{2,1,0:T(8,128)(2,1)S(1)}, bf16[512,16,256]{2,1,0:T(8,128)(2,1)}, u32[]{:S(2)}) copy-start(bf16[512,16,256]{2,1,0:T(8,128)(2,1)} %param.4) | copy-start | bytes 12582916
  45.3 3.1 %copy-start.4 = (bf16[1024,1024]{1,0:T(8,128)(2,1)}, bf16[1024,1024]{1,0:T(8,128)(2,1)S(1)}, u32[]{:S(2)}) copy-start(bf16[1024,1024]{1,0:T(8,128)(2,1)S(1)} %get-tuple-element.116.left) | copy-start | bytes 6291460
  45.3 2.9 %collective-permute-start.8 = (f32[256,1152]{1,0:T(8,128)S(1)}, f32[256,1152]{1,0:T(8,128)S(1)}, u32[]{:S(2)}, u32[]{:S(2)}) collective-permute-start(f32[256,1152]{1,0:T(8,128)S(1)} %get-tuple-element.72), channel_id=1, source_target_pairs={{0,8},{8,0},{16,24},{24,16},{1,9},{9,1},{17,25},{25,17},{2,10},{10... | collective-permute-start | bytes 3538952 | tf_op jit(solution)/shard_map/ppermute | solution.py:16
  48.4 7.0 %collective-permute-start.10 = (f32[128,384]{1,0:T(8,128)S(1)}, f32[128,384]{1,0:T(8,128)S(1)}, u32[]{:S(2)}, u32[]{:S(2)}) collective-permute-start(f32[128,384]{1,0:T(8,128)S(1)} %get-tuple-element.74), channel_id=1, source_target_pairs={{0,1},{1,0},{2,3},{3,2},{4,5},{5,4},{6,7},{7,6},{8,9},{9,8},{10,11... | collective-permute-start | bytes 589832 | tf_op jit(solution)/shard_map/ppermute | solution.py:16
  50.2 6.7 %collective-permute-start.11 = (f32[128,384]{1,0:T(8,128)S(1)}, f32[128,384]{1,0:T(8,128)S(1)}, u32[]{:S(2)}, u32[]{:S(2)}) collective-permute-start(f32[128,384]{1,0:T(8,128)S(1)} %get-tuple-element.75), channel_id=1, source_target_pairs={{0,2},{2,0},{4,6},{6,4},{1,3},{3,1},{5,7},{7,5},{8,10},{10,8},{12,... | collective-permute-start | bytes 589832 | tf_op jit(solution)/shard_map/ppermute | solution.py:16
  51.7 6.4 %collective-permute-start.9 = (f32[128,384]{1,0:T(8,128)S(1)}, f32[128,384]{1,0:T(8,128)S(1)}, u32[]{:S(2)}, u32[]{:S(2)}) collective-permute-start(f32[128,384]{1,0:T(8,128)S(1)} %get-tuple-element.73), channel_id=1, source_target_pairs={{0,16},{8,24},{16,0},{24,8},{1,17},{9,25},{17,1},{25,9},{2,18},{10... | collective-permute-start | bytes 589832 | tf_op jit(solution)/shard_map/ppermute | solution.py:16
  58.3 4.7 %collective-permute-start.12 = (f32[64,384]{1,0:T(8,128)S(1)}, f32[64,384]{1,0:T(8,128)S(1)}, u32[]{:S(2)}, u32[]{:S(2)}) collective-permute-start(f32[64,384]{1,0:T(8,128)S(1)} %slice.106), channel_id=1, source_target_pairs={{0,1},{1,0},{2,3},{3,2},{4,5},{5,4},{6,7},{7,6},{8,9},{9,8},{10,11... | collective-permute-start | bytes 294920 | tf_op jit(solution)/shard_map/ppermute | solution.py:16
  58.9 4.6 %collective-permute-start.13 = (f32[64,384]{1,0:T(8,128)S(1)}, f32[64,384]{1,0:T(8,128)S(1)}, u32[]{:S(2)}, u32[]{:S(2)}) collective-permute-start(f32[64,384]{1,0:T(8,128)S(1)} %slice.108), channel_id=1, source_target_pairs={{0,2},{2,0},{4,6},{6,4},{1,3},{3,1},{5,7},{7,5},{8,10},{10,8},{12,... | collective-permute-start | bytes 294920 | tf_op jit(solution)/shard_map/ppermute | solution.py:16
  59.2 4.6 %collective-permute-start.14 = (f32[64,384]{1,0:T(8,128)S(1)}, f32[64,384]{1,0:T(8,128)S(1)}, u32[]{:S(2)}, u32[]{:S(2)}) collective-permute-start(f32[64,384]{1,0:T(8,128)S(1)} %slice.110), channel_id=1, source_target_pairs={{0,16},{8,24},{16,0},{24,8},{1,17},{9,25},{17,1},{25,9},{2,18},{10... | collective-permute-start | bytes 294920 | tf_op jit(solution)/shard_map/ppermute | solution.py:16
  63.9 5.0 %collective-permute-start.15 = (f32[32,384]{1,0:T(8,128)S(1)}, f32[32,384]{1,0:T(8,128)S(1)}, u32[]{:S(2)}, u32[]{:S(2)}) collective-permute-start(f32[32,384]{1,0:T(8,128)S(1)} %slice.112), channel_id=1, source_target_pairs={{0,2},{2,0},{4,6},{6,4},{1,3},{3,1},{5,7},{7,5},{8,10},{10,8},{12,... | collective-permute-start | bytes 147464 | tf_op jit(solution)/shard_map/ppermute | solution.py:16
  65.6 4.1 %collective-permute-start.16 = (f32[32,384]{1,0:T(8,128)S(1)}, f32[32,384]{1,0:T(8,128)S(1)}, u32[]{:S(2)}, u32[]{:S(2)}) collective-permute-start(f32[32,384]{1,0:T(8,128)S(1)} %slice.114), channel_id=1, source_target_pairs={{0,16},{8,24},{16,0},{24,8},{1,17},{9,25},{17,1},{25,9},{2,18},{10... | collective-permute-start | bytes 147464 | tf_op jit(solution)/shard_map/ppermute | solution.py:16
  67.1 4.1 %collective-permute-start.17 = (f32[32,384]{1,0:T(8,128)S(1)}, f32[32,384]{1,0:T(8,128)S(1)}, u32[]{:S(2)}, u32[]{:S(2)}) collective-permute-start(f32[32,384]{1,0:T(8,128)S(1)} %slice.116), channel_id=1, source_target_pairs={{0,1},{1,0},{2,3},{3,2},{4,5},{5,4},{6,7},{7,6},{8,9},{9,8},{10,11... | collective-permute-start | bytes 147464 | tf_op jit(solution)/shard_map/ppermute | solution.py:16
  68.7 2.6 %collective-permute-start.18 = (f32[2,384,256]{2,1,0:T(8,128)S(1)}, f32[2,384,256]{2,1,0:T(8,128)S(1)}, u32[]{:S(2)}, u32[]{:S(2)}) collective-permute-start(f32[2,384,256]{2,1,0:T(8,128)S(1)} %slice.96.refs_4_), channel_id=1, source_target_pairs={{0,8},{8,0},{16,24},{24,16},{1,9},{9,1},{17,25},{25,17},{2,10},{10... | collective-permute-start | bytes 2359304 | tf_op jit(solution)/shard_map/ppermute | solution.py:16
  71.3 9.9 %collective-permute-start.20 = (f32[2,128,256]{2,1,0:T(8,128)S(1)}, f32[2,128,256]{2,1,0:T(8,128)S(1)}, u32[]{:S(2)}, u32[]{:S(2)}) collective-permute-start(f32[2,128,256]{2,1,0:T(8,128)S(1)} %slice.97.refs_0_), channel_id=1, source_target_pairs={{0,16},{8,24},{16,0},{24,8},{1,17},{9,25},{17,1},{25,9},{2,18},{10... | collective-permute-start | bytes 786440 | tf_op jit(solution)/shard_map/ppermute | solution.py:16
  71.9 9.3 %collective-permute-start.19 = (f32[32,1152]{1,0:T(8,128)S(1)}, f32[32,1152]{1,0:T(8,128)S(1)}, u32[]{:S(2)}, u32[]{:S(2)}) collective-permute-start(f32[32,1152]{1,0:T(8,128)S(1)} %pad_maximum_fusion.3), channel_id=1, source_target_pairs={{0,4},{2,6},{4,0},{6,2},{1,5},{3,7},{5,1},{7,3},{8,12},{10,14},{12... | collective-permute-start | bytes 442376 | tf_op jit(solution)/shard_map/ppermute | solution.py:16
  81.2 4.2 %collective-permute-start.21 = (f32[32,384]{1,0:T(8,128)S(1)}, f32[32,384]{1,0:T(8,128)S(1)}, u32[]{:S(2)}, u32[]{:S(2)}) collective-permute-start(f32[32,384]{1,0:T(8,128)S(1)} %get-tuple-element.97), channel_id=1, source_target_pairs={{0,2},{2,0},{4,6},{6,4},{1,3},{3,1},{5,7},{7,5},{8,10},{10,8},{12,... | collective-permute-start | bytes 147464 | tf_op jit(solution)/shard_map/ppermute | solution.py:16
  81.3 4.2 %collective-permute-start.22 = (f32[32,384]{1,0:T(8,128)S(1)}, f32[32,384]{1,0:T(8,128)S(1)}, u32[]{:S(2)}, u32[]{:S(2)}) collective-permute-start(f32[32,384]{1,0:T(8,128)S(1)} %get-tuple-element.98), channel_id=1, source_target_pairs={{0,16},{8,24},{16,0},{24,8},{1,17},{9,25},{17,1},{25,9},{2,18},{10... | collective-permute-start | bytes 147464 | tf_op jit(solution)/shard_map/ppermute | solution.py:16
  82.9 4.1 %collective-permute-start.23 = (f32[32,384]{1,0:T(8,128)S(1)}, f32[32,384]{1,0:T(8,128)S(1)}, u32[]{:S(2)}, u32[]{:S(2)}) collective-permute-start(f32[32,384]{1,0:T(8,128)S(1)} %get-tuple-element.99), channel_id=1, source_target_pairs={{0,1},{1,0},{2,3},{3,2},{4,5},{5,4},{6,7},{7,6},{8,9},{9,8},{10,11... | collective-permute-start | bytes 147464 | tf_op jit(solution)/shard_map/ppermute | solution.py:16
  87.0 4.7 %collective-permute-start.24 = (f32[64,384]{1,0:T(8,128)S(1)}, f32[64,384]{1,0:T(8,128)S(1)}, u32[]{:S(2)}, u32[]{:S(2)}) collective-permute-start(f32[64,384]{1,0:T(8,128)S(1)} %pad_maximum_fusion.4), channel_id=1, source_target_pairs={{0,1},{1,0},{2,3},{3,2},{4,5},{5,4},{6,7},{7,6},{8,9},{9,8},{10,11... | collective-permute-start | bytes 294920 | tf_op jit(solution)/shard_map/ppermute | solution.py:16
  87.6 4.6 %collective-permute-start.25 = (f32[64,384]{1,0:T(8,128)S(1)}, f32[64,384]{1,0:T(8,128)S(1)}, u32[]{:S(2)}, u32[]{:S(2)}) collective-permute-start(f32[64,384]{1,0:T(8,128)S(1)} %pad_maximum_fusion.5), channel_id=1, source_target_pairs={{0,2},{2,0},{4,6},{6,4},{1,3},{3,1},{5,7},{7,5},{8,10},{10,8},{12,... | collective-permute-start | bytes 294920 | tf_op jit(solution)/shard_map/ppermute | solution.py:16
  89.5 4.9 %collective-permute-start.26 = (f32[64,384]{1,0:T(8,128)S(1)}, f32[64,384]{1,0:T(8,128)S(1)}, u32[]{:S(2)}, u32[]{:S(2)}) collective-permute-start(f32[64,384]{1,0:T(8,128)S(1)} %pad_maximum_fusion.6), channel_id=1, source_target_pairs={{0,16},{8,24},{16,0},{24,8},{1,17},{9,25},{17,1},{25,9},{2,18},{10... | collective-permute-start | bytes 294920 | tf_op jit(solution)/shard_map/ppermute | solution.py:16
  94.5 5.7 %collective-permute-start.27 = (f32[128,384]{1,0:T(8,128)S(1)}, f32[128,384]{1,0:T(8,128)S(1)}, u32[]{:S(2)}, u32[]{:S(2)}) collective-permute-start(f32[128,384]{1,0:T(8,128)S(1)} %pad_maximum_fusion), channel_id=1, source_target_pairs={{0,16},{8,24},{16,0},{24,8},{1,17},{9,25},{17,1},{25,9},{2,18},{10... | collective-permute-start | bytes 589832 | tf_op jit(solution)/shard_map/ppermute | solution.py:16
  95.2 5.7 %collective-permute-start.28 = (f32[128,384]{1,0:T(8,128)S(1)}, f32[128,384]{1,0:T(8,128)S(1)}, u32[]{:S(2)}, u32[]{:S(2)}) collective-permute-start(f32[128,384]{1,0:T(8,128)S(1)} %pad_maximum_fusion.1), channel_id=1, source_target_pairs={{0,1},{1,0},{2,3},{3,2},{4,5},{5,4},{6,7},{7,6},{8,9},{9,8},{10,11... | collective-permute-start | bytes 589832 | tf_op jit(solution)/shard_map/ppermute | solution.py:16
  96.7 5.7 %collective-permute-start.29 = (f32[128,384]{1,0:T(8,128)S(1)}, f32[128,384]{1,0:T(8,128)S(1)}, u32[]{:S(2)}, u32[]{:S(2)}) collective-permute-start(f32[128,384]{1,0:T(8,128)S(1)} %pad_maximum_fusion.2), channel_id=1, source_target_pairs={{0,2},{2,0},{4,6},{6,4},{1,3},{3,1},{5,7},{7,5},{8,10},{10,8},{12,... | collective-permute-start | bytes 589832 | tf_op jit(solution)/shard_map/ppermute | solution.py:16
  102.5 2.9 %collective-permute-start.30 = (f32[256,1152]{1,0:T(8,128)S(1)}, f32[256,1152]{1,0:T(8,128)S(1)}, u32[]{:S(2)}, u32[]{:S(2)}) collective-permute-start(f32[256,1152]{1,0:T(8,128)S(1)} %maximum_maximum_fusion.mine_ref), channel_id=1, source_target_pairs={{0,8},{8,0},{16,24},{24,16},{1,9},{9,1},{17,25},{25,17},{2,10},{10... | collective-permute-start | bytes 3538952 | tf_op jit(solution)/shard_map/ppermute | solution.py:16
  102.5 40.4 %collective-permute-start.31 = (f32[2,128,256]{2,1,0:T(8,128)S(1)}, f32[2,128,256]{2,1,0:T(8,128)S(1)}, u32[]{:S(2)}, u32[]{:S(2)}) collective-permute-start(f32[2,128,256]{2,1,0:T(8,128)S(1)} %slice.97.refs_0_), channel_id=1, source_target_pairs={{0,8},{8,0},{16,24},{24,16},{1,9},{9,1},{17,25},{25,17},{2,10},{10... | collective-permute-start | bytes 786440 | tf_op jit(solution)/shard_map/ppermute | solution.py:16
  103.0 39.9 %collective-permute-start.32 = (f32[2,128,256]{2,1,0:T(8,128)S(1)}, f32[2,128,256]{2,1,0:T(8,128)S(1)}, u32[]{:S(2)}, u32[]{:S(2)}) collective-permute-start(f32[2,128,256]{2,1,0:T(8,128)S(1)} %collective-permute-done.20.refs_2_), channel_id=1, source_target_pairs={{0,8},{8,0},{16,24},{24,16},{1,9},{9,1},{17,25},{25,17},{2,10},{10... | collective-permute-start | bytes 786440 | tf_op jit(solution)/shard_map/ppermute | solution.py:16
  103.1 39.9 %collective-permute-start.33 = (f32[2,384,256]{2,1,0:T(8,128)S(1)}, f32[2,384,256]{2,1,0:T(8,128)S(1)}, u32[]{:S(2)}, u32[]{:S(2)}) collective-permute-start(f32[2,384,256]{2,1,0:T(8,128)S(1)} %slice.96.refs_4_), channel_id=1, source_target_pairs={{0,16},{8,24},{16,0},{24,8},{1,17},{9,25},{17,1},{25,9},{2,18},{10... | collective-permute-start | bytes 2359304 | tf_op jit(solution)/shard_map/ppermute | solution.py:16
  104.3 38.7 %collective-permute-start.34 = (f32[2,384,256]{2,1,0:T(8,128)S(1)}, f32[2,384,256]{2,1,0:T(8,128)S(1)}, u32[]{:S(2)}, u32[]{:S(2)}) collective-permute-start(f32[2,384,256]{2,1,0:T(8,128)S(1)} %collective-permute-done.18.refs_5_), channel_id=1, source_target_pairs={{0,16},{8,24},{16,0},{24,8},{1,17},{9,25},{17,1},{25,9},{2,18},{10... | collective-permute-start | bytes 2359304 | tf_op jit(solution)/shard_map/ppermute | solution.py:16
  105.4 1.0 copy-start.5

commit v2 on v1

--- a/solution.py
+++ b/solution.py
@@ -287,7 +287,7 @@
     wide = 2 * BLOCK
     every, top, bottom = slice(0, wide), slice(0, BLOCK), slice(BLOCK, wide)
     chunks = [slice(c, c + wide) for c in range(0, 2 * chi, wide)]
-    earlier, before_last = slice(0, chi - 2 * wide), slice(0, chi - 3 * BLOCK)
+    earlier = slice(0, chi - 2 * wide)
     bind = functools.partial
 
     def span(first, size):
@@ -326,15 +326,18 @@
         return [bind(less, *args, columns) for columns in chunks]
 
     for i in range(PIECES):
-        solved[i, before_last] = jnp.zeros((chi - 3 * BLOCK, 2 * chi), jnp.bfloat16)
-        lows[i, :, before_last] = jnp.zeros((chi, chi - 3 * BLOCK), jnp.bfloat16)
+        solved[i, earlier] = jnp.zeros((chi - 2 * wide, 2 * chi), jnp.bfloat16)
+        lows[i, :, earlier] = jnp.zeros((chi, chi - 2 * wide), jnp.bfloat16)
         inverses[i] = jnp.zeros_like(inverses[i])
     now[...] = jnp.zeros_like(now)
     for columns in chunks:
         later[:, columns] = fresh(every, columns)
-    now[top, :BLOCK] = later[top, :BLOCK]
-
-    def body(j, _):
+
+    def next_block(inverse, row, block):
+        values = product(inverse, split(row, PIECES))
+        return block - product(split(values.T, PIECES), split(values, PIECES))
+
+    def body(j, block):
         lo = j * wide
         last = span(lax.rem(lo + chi - BLOCK, chi), BLOCK)
         first, second, pair = span(lo, BLOCK), span(lo + BLOCK, BLOCK), span(lo, wide)
@@ -343,23 +346,18 @@
 
         inverse = [inverses[i] for i in range(PIECES)]
         tasks = solve_all(last, inverse, bottom) + less_all(now, every, later, pair, last)
-        of_left = [columns for columns in chunks if columns.start >= chi]
-        tasks += [bind(fresh_less, next_pair, earlier, columns) for columns in of_left]
-        inverse = split(inverse_factor(now[top, first], tasks, spread), PIECES)
-        solve(first, inverse, top, second, True)
-        block = now[bottom, second] - taken(second, first, second)
+        tasks += [bind(fresh_less, next_pair, earlier, columns) for columns in chunks]
+        inverse = split(inverse_factor(block, tasks, spread), PIECES)
+        block = next_block(inverse, now[top, second], now[bottom, second])
 
         tasks = solve_all(first, inverse, top) + less_all(now, bottom, now, second, first)
-        tasks += [bind(fresh_less, next_pair, before_last, columns) for columns in chunks if columns.start < chi]
-        tasks += [bind(less, later, every, later, next_pair, first, columns) for columns in of_left]
+        tasks += less_all(later, every, later, next_pair, first)
         inverse = split(inverse_factor(block, tasks, spread), PIECES)
         for i, piece in enumerate(inverse):
             inverses[i] = piece
-        solve(second, inverse, bottom, next_pair, True)
-        now[top, next_first] = later[top, next_first] - taken(next_first, second, next_first)
-        return 0
-
-    lax.fori_loop(0, chi // wide, body, 0)
+        return next_block(inverse, now[bottom, next_first], later[top, next_first])
+
+    lax.fori_loop(0, chi // wide, body, gram[:BLOCK, :BLOCK])
     for task in solve_all(slice(chi - BLOCK, chi), [inverses[i] for i in range(PIECES)], bottom)[chi // wide - 1 :]:
         task()
 

time: 147 us -> 144 us (0.980)
  Pallas kernels: 53.7 us -> 50.3 us
    pallas_call x1, Pallas kernels: 36.6 us -> 33.2 us  [factorize(): pl.pallas_call(functools.partial(factor_kernel, scale, chunk), out_shape=...]
  transfers between devices with their start and end apart: 35 -> 35, of which waited for: 23 -> 24; matrix products, arithmetic and copies ran while one was open for 0% -> 0% of each run, Pallas kernels for 30% -> 28%
where the time goes in v2:
time: 144 us; the launch traced here: 143 us
  waiting for transfers between devices  50.7 us (35%)
  Pallas kernels  50.3 us (35%)
  starting transfers between devices  33.3 us (23%)
  local copies, waits for them, and re-layouts  6.49 us (5%)
  other arithmetic  1.54 us (1%)
    ppermute x35, waiting for transfers between devices, swap(): return lax.ppermute(array, axis, [(i, i ^ distance) for i in range(size)])  50.7 us
    ppermute x35, starting transfers between devices, swap(): return lax.ppermute(array, axis, [(i, i ^ distance) for i in range(size)])  33.3 us
    pallas_call x1, Pallas kernels, factorize(): pl.pallas_call(functools.partial(factor_kernel, scale, chunk), out_shape=...  33.2 us
    pallas_call x2, Pallas kernels, absorb(): pl.pallas_call(functools.partial(absorb_kernel, east_parts), grid=(tiles,...  7.48 us
    pallas_call x1, Pallas kernels, gram_of_columns(): pl.pallas_call(functools.partial(gram_kernel, chi, chunk, width // 3, len...  6.17 us
    unnamed x12, local copies, waits for them, and re-layouts  6.11 us
    pallas_call x1, Pallas kernels, make_site(): pl.pallas_call(functools.partial(site_kernel, scale, len(got[0])), out_sh...  3.43 us
  transfers between devices with their start and end apart: 35, of which 24 were waited for; matrix products, arithmetic and copies ran while one was open for 0% of the time, Pallas kernels for 28%

profile of v2, /device:TPU:0, one launch (start us, length us, event | category | flops | bytes accessed | tf_op | source)
XLA Modules:
  0.0 143.3 jit_solution(13330577855549408166)
XLA Ops:
  0.6 1.0 convert_element_type.3.refs_2_
  1.6 3.0 %collective-permute-start.1 = (f32[256,512]{1,0:T(8,128)S(1)}, f32[256,512]{1,0:T(8,128)S(1)}, u32[]{:S(2)}, u32[]{:S(2)}) collective-permute-start(f32[256,512]{1,0:T(8,128)S(1)} %convert_element_type.3.refs_2_), channel_id=1, source_target_pairs={{0,1},{1,0},{2,3},{3,2},{4,5},{5,4},{6,7},{7,6},{8,9},{9,8},{10,11... | collective-permute-start | bytes 1572872 | tf_op jit(solution)/shard_map/ppermute | solution.py:16
  4.7 1.5 %collective-permute-start.4 = (f32[256,512]{1,0:T(8,128)S(1)}, f32[256,512]{1,0:T(8,128)}, u32[]{:S(2)}, u32[]{:S(2)}) collective-permute-start(f32[256,512]{1,0:T(8,128)S(1)} %convert_element_type.3.refs_2_), channel_id=1, source_target_pairs={{0,16},{8,24},{16,0},{24,8},{1,17},{9,25},{17,1},{25,9},{2,18},{10... | collective-permute-start | bytes 1572872 | tf_op jit(solution)/shard_map/ppermute | solution.py:16
  6.2 2.2 %copy-done = bf16[512,16,256]{2,1,0:T(8,128)(2,1)S(1)} copy-done((bf16[512,16,256]{2,1,0:T(8,128)(2,1)S(1)}, bf16[512,16,256]{2,1,0:T(8,128)(2,1)}, u32[]{:S(2)}) %copy-start) | copy-done | bytes 4194328
  8.4 0.7 copy-done.2
  9.1 3.0 %shard_map.51 = f32[2,512,256]{2,1,0:T(8,128)S(1)} custom-call(s32[2]{0:T(128)S(1)} %pad_add_fusion.legs_ref, bf16[8192,256]{1,0:T(8,128)(2,1)S(1)} %bitcast.16, f32[16,16]{1,0:T(8,128)S(1)} %copy-done.2), custom_call_target="tpu_custom_call" | custom-call | flops 268435456 | bytes 16777216 | tf_op jit(solution)/shard_map/pallas_call | solution.py:118
  12.2 0.6 collective-permute-start
  12.7 4.7 %collective-permute-done.1.refs_3_ = f32[256,512]{1,0:T(8,128)S(1)} collective-permute-done((f32[256,512]{1,0:T(8,128)S(1)}, f32[256,512]{1,0:T(8,128)S(1)}, u32[]{:S(2)}, u32[]{:S(2)}) %collective-permute-start.1) | collective-permute-done | bytes 524320 | tf_op jit(solution)/shard_map/ppermute | solution.py:16
  17.4 2.0 %collective-permute-start.5 = (f32[256,512]{1,0:T(8,128)S(1)}, f32[256,512]{1,0:T(8,128)}, u32[]{:S(2)}, u32[]{:S(2)}) collective-permute-start(f32[256,512]{1,0:T(8,128)S(1)} %collective-permute-done.1.refs_3_), channel_id=1, source_target_pairs={{0,16},{8,24},{16,0},{24,8},{1,17},{9,25},{17,1},{25,9},{2,18},{10... | collective-permute-start | bytes 1572872 | tf_op jit(solution)/shard_map/ppermute | solution.py:16
  20.0 9.9 %collective-permute-done.5.refs_7_ = f32[256,512]{1,0:T(8,128)} collective-permute-done((f32[256,512]{1,0:T(8,128)S(1)}, f32[256,512]{1,0:T(8,128)}, u32[]{:S(2)}, u32[]{:S(2)}) %collective-permute-start.5) | collective-permute-done | bytes 524320 | tf_op jit(solution)/shard_map/ppermute | solution.py:16
  30.1 2.2 %copy-done.1 = bf16[512,16,256]{2,1,0:T(8,128)(2,1)S(1)} copy-done((bf16[512,16,256]{2,1,0:T(8,128)(2,1)S(1)}, bf16[512,16,256]{2,1,0:T(8,128)(2,1)}, u32[]{:S(2)}) %copy-start.1) | copy-done | bytes 4194328
  32.3 4.4 %shard_map.50.own_ref = bf16[8,512,256]{2,1,0:T(8,128)(2,1)S(1)} custom-call(s32[8]{0:T(128)S(1)} %stack.68.legs_ref, bf16[8192,256]{1,0:T(8,128)(2,1)S(1)} %bitcast.17, f32[16,16]{1,0:T(8,128)S(1)} %copy-done.3), custom_call_target="tpu_custom_call" | custom-call | flops 1073741824 | bytes 16777216 | tf_op jit(solution)/shard_map/pallas_call | solution.py:118
  36.8 2.3 %collective-permute-done.refs_1_ = f32[2,512,256]{2,1,0:T(8,128)S(1)} collective-permute-done((f32[2,512,256]{2,1,0:T(8,128)S(1)}, f32[2,512,256]{2,1,0:T(8,128)S(1)}, u32[]{:S(2)}, u32[]{:S(2)}) %collective-permute-start) | collective-permute-done | bytes 1048608 | tf_op jit(solution)/shard_map/ppermute | solution.py:16
  39.1 6.2 %shard_map.52 = (f32[256,1152]{1,0:T(8,128)S(1)}, f32[256,1152]{1,0:T(8,128)S(1)}, bf16[1024,1024]{1,0:T(8,128)(2,1)S(1)}) custom-call(s32[5]{0:T(128)S(1)} %stack.59.place_ref, bf16[2,512,256]{2,1,0:T(8,128)(2,1)S(1)} %constant_dynamic-slice_fusion.refs_0_, f32[2,512,256]{2,1,0:T(8,128)S(1)} %collective-permute-done.refs_1_, ...), custom_call_target="tpu_custom_call" | custom-call | flops 2684354560 | bytes 12582912 | tf_op jit(solution)/shard_map/pallas_call | solution.py:174
  45.3 2.8 %collective-permute-done.8 = f32[256,1152]{1,0:T(8,128)S(1)} collective-permute-done((f32[256,1152]{1,0:T(8,128)S(1)}, f32[256,1152]{1,0:T(8,128)S(1)}, u32[]{:S(2)}, u32[]{:S(2)}) %collective-permute-start.8) | collective-permute-done | bytes 1179680 | tf_op jit(solution)/shard_map/ppermute | solution.py:16
  48.4 1.8 %collective-permute-start.10 = (f32[128,384]{1,0:T(8,128)S(1)}, f32[128,384]{1,0:T(8,128)S(1)}, u32[]{:S(2)}, u32[]{:S(2)}) collective-permute-start(f32[128,384]{1,0:T(8,128)S(1)} %get-tuple-element.74), channel_id=1, source_target_pairs={{0,1},{1,0},{2,3},{3,2},{4,5},{5,4},{6,7},{7,6},{8,9},{9,8},{10,11... | collective-permute-start | bytes 589832 | tf_op jit(solution)/shard_map/ppermute | solution.py:16
  50.2 1.6 %collective-permute-start.11 = (f32[128,384]{1,0:T(8,128)S(1)}, f32[128,384]{1,0:T(8,128)S(1)}, u32[]{:S(2)}, u32[]{:S(2)}) collective-permute-start(f32[128,384]{1,0:T(8,128)S(1)} %get-tuple-element.75), channel_id=1, source_target_pairs={{0,2},{2,0},{4,6},{6,4},{1,3},{3,1},{5,7},{7,5},{8,10},{10,8},{12,... | collective-permute-start | bytes 589832 | tf_op jit(solution)/shard_map/ppermute | solution.py:16
  51.7 1.5 %collective-permute-start.9 = (f32[128,384]{1,0:T(8,128)S(1)}, f32[128,384]{1,0:T(8,128)S(1)}, u32[]{:S(2)}, u32[]{:S(2)}) collective-permute-start(f32[128,384]{1,0:T(8,128)S(1)} %get-tuple-element.73), channel_id=1, source_target_pairs={{0,16},{8,24},{16,0},{24,8},{1,17},{9,25},{17,1},{25,9},{2,18},{10... | collective-permute-start | bytes 589832 | tf_op jit(solution)/shard_map/ppermute | solution.py:16
  53.2 2.1 %collective-permute-done.10 = f32[128,384]{1,0:T(8,128)S(1)} collective-permute-done((f32[128,384]{1,0:T(8,128)S(1)}, f32[128,384]{1,0:T(8,128)S(1)}, u32[]{:S(2)}, u32[]{:S(2)}) %collective-permute-start.10) | collective-permute-done | bytes 196640 | tf_op jit(solution)/shard_map/ppermute | solution.py:16
  55.4 1.5 %collective-permute-done.11 = f32[128,384]{1,0:T(8,128)S(1)} collective-permute-done((f32[128,384]{1,0:T(8,128)S(1)}, f32[128,384]{1,0:T(8,128)S(1)}, u32[]{:S(2)}, u32[]{:S(2)}) %collective-permute-start.11) | collective-permute-done | bytes 196640 | tf_op jit(solution)/shard_map/ppermute | solution.py:16
  56.8 1.3 collective-permute-done.9
  59.2 1.6 %collective-permute-start.14 = (f32[64,384]{1,0:T(8,128)S(1)}, f32[64,384]{1,0:T(8,128)S(1)}, u32[]{:S(2)}, u32[]{:S(2)}) collective-permute-start(f32[64,384]{1,0:T(8,128)S(1)} %slice.110), channel_id=1, source_target_pairs={{0,16},{8,24},{16,0},{24,8},{1,17},{9,25},{17,1},{25,9},{2,18},{10... | collective-permute-start | bytes 294920 | tf_op jit(solution)/shard_map/ppermute | solution.py:16
  60.8 2.2 %collective-permute-done.12 = f32[64,384]{1,0:T(8,128)S(1)} collective-permute-done((f32[64,384]{1,0:T(8,128)S(1)}, f32[64,384]{1,0:T(8,128)S(1)}, u32[]{:S(2)}, u32[]{:S(2)}) %collective-permute-start.12) | collective-permute-done | bytes 98336 | tf_op jit(solution)/shard_map/ppermute | solution.py:16
  63.9 1.8 %collective-permute-start.15 = (f32[32,384]{1,0:T(8,128)S(1)}, f32[32,384]{1,0:T(8,128)S(1)}, u32[]{:S(2)}, u32[]{:S(2)}) collective-permute-start(f32[32,384]{1,0:T(8,128)S(1)} %slice.112), channel_id=1, source_target_pairs={{0,2},{2,0},{4,6},{6,4},{1,3},{3,1},{5,7},{7,5},{8,10},{10,8},{12,... | collective-permute-start | bytes 147464 | tf_op jit(solution)/shard_map/ppermute | solution.py:16
  65.6 1.5 %collective-permute-start.16 = (f32[32,384]{1,0:T(8,128)S(1)}, f32[32,384]{1,0:T(8,128)S(1)}, u32[]{:S(2)}, u32[]{:S(2)}) collective-permute-start(f32[32,384]{1,0:T(8,128)S(1)} %slice.114), channel_id=1, source_target_pairs={{0,16},{8,24},{16,0},{24,8},{1,17},{9,25},{17,1},{25,9},{2,18},{10... | collective-permute-start | bytes 147464 | tf_op jit(solution)/shard_map/ppermute | solution.py:16
  67.1 1.5 %collective-permute-start.17 = (f32[32,384]{1,0:T(8,128)S(1)}, f32[32,384]{1,0:T(8,128)S(1)}, u32[]{:S(2)}, u32[]{:S(2)}) collective-permute-start(f32[32,384]{1,0:T(8,128)S(1)} %slice.116), channel_id=1, source_target_pairs={{0,1},{1,0},{2,3},{3,2},{4,5},{5,4},{6,7},{7,6},{8,9},{9,8},{10,11... | collective-permute-start | bytes 147464 | tf_op jit(solution)/shard_map/ppermute | solution.py:16
  68.8 0.9 collective-permute-done.16
  69.7 1.5 %collective-permute-done.17 = f32[32,384]{1,0:T(8,128)S(1)} collective-permute-done((f32[32,384]{1,0:T(8,128)S(1)}, f32[32,384]{1,0:T(8,128)S(1)}, u32[]{:S(2)}, u32[]{:S(2)}) %collective-permute-start.17) | collective-permute-done | bytes 49184 | tf_op jit(solution)/shard_map/ppermute | solution.py:16
  71.3 0.6 collective-permute-start.20
  71.9 2.6 %collective-permute-start.19 = (f32[32,1152]{1,0:T(8,128)S(1)}, f32[32,1152]{1,0:T(8,128)S(1)}, u32[]{:S(2)}, u32[]{:S(2)}) collective-permute-start(f32[32,1152]{1,0:T(8,128)S(1)} %pad_maximum_fusion.3), channel_id=1, source_target_pairs={{0,4},{2,6},{4,0},{6,2},{1,5},{3,7},{5,1},{7,3},{8,12},{10,14},{12... | collective-permute-start | bytes 442376 | tf_op jit(solution)/shard_map/ppermute | solution.py:16
  74.5 6.7 %collective-permute-done.19 = f32[32,1152]{1,0:T(8,128)S(1)} collective-permute-done((f32[32,1152]{1,0:T(8,128)S(1)}, f32[32,1152]{1,0:T(8,128)S(1)}, u32[]{:S(2)}, u32[]{:S(2)}) %collective-permute-start.19) | collective-permute-done | bytes 147488 | tf_op jit(solution)/shard_map/ppermute | solution.py:16
  81.3 1.5 %collective-permute-start.22 = (f32[32,384]{1,0:T(8,128)S(1)}, f32[32,384]{1,0:T(8,128)S(1)}, u32[]{:S(2)}, u32[]{:S(2)}) collective-permute-start(f32[32,384]{1,0:T(8,128)S(1)} %get-tuple-element.98), channel_id=1, source_target_pairs={{0,16},{8,24},{16,0},{24,8},{1,17},{9,25},{17,1},{25,9},{2,18},{10... | collective-permute-start | bytes 147464 | tf_op jit(solution)/shard_map/ppermute | solution.py:16
  83.4 2.0 %collective-permute-done.21 = f32[32,384]{1,0:T(8,128)S(1)} collective-permute-done((f32[32,384]{1,0:T(8,128)S(1)}, f32[32,384]{1,0:T(8,128)S(1)}, u32[]{:S(2)}, u32[]{:S(2)}) %collective-permute-start.21) | collective-permute-done | bytes 49184 | tf_op jit(solution)/shard_map/ppermute | solution.py:16
  85.5 1.5 %collective-permute-done.23 = f32[32,384]{1,0:T(8,128)S(1)} collective-permute-done((f32[32,384]{1,0:T(8,128)S(1)}, f32[32,384]{1,0:T(8,128)S(1)}, u32[]{:S(2)}, u32[]{:S(2)}) %collective-permute-start.23) | collective-permute-done | bytes 49184 | tf_op jit(solution)/shard_map/ppermute | solution.py:16
  87.0 0.6 collective-permute-start.24
  87.6 1.9 %collective-permute-start.25 = (f32[64,384]{1,0:T(8,128)S(1)}, f32[64,384]{1,0:T(8,128)S(1)}, u32[]{:S(2)}, u32[]{:S(2)}) collective-permute-start(f32[64,384]{1,0:T(8,128)S(1)} %pad_maximum_fusion.5), channel_id=1, source_target_pairs={{0,2},{2,0},{4,6},{6,4},{1,3},{3,1},{5,7},{7,5},{8,10},{10,8},{12,... | collective-permute-start | bytes 294920 | tf_op jit(solution)/shard_map/ppermute | solution.py:16
  90.0 1.7 %collective-permute-done.24 = f32[64,384]{1,0:T(8,128)S(1)} collective-permute-done((f32[64,384]{1,0:T(8,128)S(1)}, f32[64,384]{1,0:T(8,128)S(1)}, u32[]{:S(2)}, u32[]{:S(2)}) %collective-permute-start.24) | collective-permute-done | bytes 98336 | tf_op jit(solution)/shard_map/ppermute | solution.py:16
  92.2 2.2 %collective-permute-done.26 = f32[64,384]{1,0:T(8,128)S(1)} collective-permute-done((f32[64,384]{1,0:T(8,128)S(1)}, f32[64,384]{1,0:T(8,128)S(1)}, u32[]{:S(2)}, u32[]{:S(2)}) %collective-permute-start.26) | collective-permute-done | bytes 98336 | tf_op jit(solution)/shard_map/ppermute | solution.py:16
  94.5 0.8 collective-permute-start.27
  95.2 1.5 %collective-permute-start.28 = (f32[128,384]{1,0:T(8,128)S(1)}, f32[128,384]{1,0:T(8,128)S(1)}, u32[]{:S(2)}, u32[]{:S(2)}) collective-permute-start(f32[128,384]{1,0:T(8,128)S(1)} %pad_maximum_fusion.1), channel_id=1, source_target_pairs={{0,1},{1,0},{2,3},{3,2},{4,5},{5,4},{6,7},{7,6},{8,9},{9,8},{10,11... | collective-permute-start | bytes 589832 | tf_op jit(solution)/shard_map/ppermute | solution.py:16
  96.8 3.4 %collective-permute-done.27 = f32[128,384]{1,0:T(8,128)S(1)} collective-permute-done((f32[128,384]{1,0:T(8,128)S(1)}, f32[128,384]{1,0:T(8,128)S(1)}, u32[]{:S(2)}, u32[]{:S(2)}) %collective-permute-start.27) | collective-permute-done | bytes 196640 | tf_op jit(solution)/shard_map/ppermute | solution.py:16
  100.2 0.7 collective-permute-done.28
  100.9 1.5 %collective-permute-done.29 = f32[128,384]{1,0:T(8,128)S(1)} collective-permute-done((f32[128,384]{1,0:T(8,128)S(1)}, f32[128,384]{1,0:T(8,128)S(1)}, u32[]{:S(2)}, u32[]{:S(2)}) %collective-permute-start.29) | collective-permute-done | bytes 196640 | tf_op jit(solution)/shard_map/ppermute | solution.py:16
  103.1 1.2 collective-permute-start.33
  104.3 0.8 collective-permute-start.34
  105.4 1.0 copy-done.5
  106.4 33.2 %shard_map.53 = (f32[256,1024]{1,0:T(8,128)}, bf16[256,1024]{1,0:T(8,128)(2,1)S(1)}) custom-call(s32[5]{0:T(128)S(1)} %stack.59.place_ref, f32[256,1152]{1,0:T(8,128)S(1)} %maximum_maximum_fusion.mine_ref, f32[256,1152]{1,0:T(8,128)} %copy-done.5, bf16[1024,1024]{1,0:T(8,128)(2,1)} %copy-done.4), custom_call_target="tpu_custom_call" | custom-call | flops 42949672960 | bytes 16777216 | tf_op jit(solution)/shard_map/pallas_call | solution.py:376
  139.9 3.4 %shard_map.54 = f32[8,256,256]{2,1,0:T(8,128)} custom-call(s32[5]{0:T(128)S(1)} %stack.59.place_ref, bf16[256,1024]{1,0:T(8,128)(2,1)S(1)} %get-tuple-element.117.weights_ref, bf16[8,512,256]{2,1,0:T(8,128)(2,1)S(1)} %shard_map.50.own_ref, f32[2,128,256]{2,1,0:T(8,128)S(1)} %slice.97.refs_0_, f32[2,128,256]{2,1,0:T(8,128)S(1)} %collective-permute-done.31.refs_1_, ...), custom_call_target="tpu_custom_call" | custom-call | flops 1073741824 | bytes 16777216 | tf_op jit(solution)/shard_map/pallas_call | solution.py:422
  (70 shorter events, 6.2 us)
Async XLA Ops:
  1.6 15.8 %collective-permute-start.1 = (f32[256,512]{1,0:T(8,128)S(1)}, f32[256,512]{1,0:T(8,128)S(1)}, u32[]{:S(2)}, u32[]{:S(2)}) collective-permute-start(f32[256,512]{1,0:T(8,128)S(1)} %convert_element_type.3.refs_2_), channel_id=1, source_target_pairs={{0,1},{1,0},{2,3},{3,2},{4,5},{5,4},{6,7},{7,6},{8,9},{9,8},{10,11... | collective-permute-start | bytes 1572872 | tf_op jit(solution)/shard_map/ppermute | solution.py:16
  4.7 15.3 %collective-permute-start.4 = (f32[256,512]{1,0:T(8,128)S(1)}, f32[256,512]{1,0:T(8,128)}, u32[]{:S(2)}, u32[]{:S(2)}) collective-permute-start(f32[256,512]{1,0:T(8,128)S(1)} %convert_element_type.3.refs_2_), channel_id=1, source_target_pairs={{0,16},{8,24},{16,0},{24,8},{1,17},{9,25},{17,1},{25,9},{2,18},{10... | collective-permute-start | bytes 1572872 | tf_op jit(solution)/shard_map/ppermute | solution.py:16
  6.2 2.2 %copy-start = (bf16[512,16,256]{2,1,0:T(8,128)(2,1)S(1)}, bf16[512,16,256]{2,1,0:T(8,128)(2,1)}, u32[]{:S(2)}) copy-start(bf16[512,16,256]{2,1,0:T(8,128)(2,1)} %param.4) | copy-start | bytes 12582916
  8.4 0.7 copy-start.2
  9.1 21.0 %copy-start.3 = (f32[16,16]{1,0:T(8,128)S(1)}, f32[16,16]{1,0:T(8,128)}, u32[]{:S(2)}) copy-start(f32[16,16]{1,0:T(8,128)} %double_ref.3) | copy-start | bytes 3076
  12.2 26.9 %collective-permute-start = (f32[2,512,256]{2,1,0:T(8,128)S(1)}, f32[2,512,256]{2,1,0:T(8,128)S(1)}, u32[]{:S(2)}, u32[]{:S(2)}) collective-permute-start(f32[2,512,256]{2,1,0:T(8,128)S(1)} %shard_map.51), channel_id=1, source_target_pairs={{0,1},{1,0},{2,3},{3,2},{4,5},{5,4},{6,7},{7,6},{8,9},{9,8},{10,11... | collective-permute-start | bytes 3145736 | tf_op jit(solution)/shard_map/ppermute | solution.py:16
  17.4 12.5 %collective-permute-start.5 = (f32[256,512]{1,0:T(8,128)S(1)}, f32[256,512]{1,0:T(8,128)}, u32[]{:S(2)}, u32[]{:S(2)}) collective-permute-start(f32[256,512]{1,0:T(8,128)S(1)} %collective-permute-done.1.refs_3_), channel_id=1, source_target_pairs={{0,16},{8,24},{16,0},{24,8},{1,17},{9,25},{17,1},{25,9},{2,18},{10... | collective-permute-start | bytes 1572872 | tf_op jit(solution)/shard_map/ppermute | solution.py:16
  19.5 17.3 %collective-permute-start.2 = (f32[256,512]{1,0:T(8,128)S(1)}, f32[256,512]{1,0:T(8,128)}, u32[]{:S(2)}, u32[]{:S(2)}) collective-permute-start(f32[256,512]{1,0:T(8,128)S(1)} %convert_element_type.3.refs_2_), channel_id=1, source_target_pairs={{0,8},{8,0},{16,24},{24,16},{1,9},{9,1},{17,25},{25,17},{2,10},{10... | collective-permute-start | bytes 1572872 | tf_op jit(solution)/shard_map/ppermute | solution.py:16
  19.5 19.6 %collective-permute-start.3 = (f32[256,512]{1,0:T(8,128)S(1)}, f32[256,512]{1,0:T(8,128)}, u32[]{:S(2)}, u32[]{:S(2)}) collective-permute-start(f32[256,512]{1,0:T(8,128)S(1)} %collective-permute-done.1.refs_3_), channel_id=1, source_target_pairs={{0,8},{8,0},{16,24},{24,16},{1,9},{9,1},{17,25},{25,17},{2,10},{10... | collective-permute-start | bytes 1572872 | tf_op jit(solution)/shard_map/ppermute | solution.py:16
  20.0 19.1 %collective-permute-start.6 = (f32[256,512]{1,0:T(8,128)}, f32[256,512]{1,0:T(8,128)}, u32[]{:S(2)}, u32[]{:S(2)}) collective-permute-start(f32[256,512]{1,0:T(8,128)} %collective-permute-done.4.refs_6_), channel_id=1, source_target_pairs={{0,8},{8,0},{16,24},{24,16},{1,9},{9,1},{17,25},{25,17},{2,10},{10... | collective-permute-start | bytes 1572872 | tf_op jit(solution)/shard_map/ppermute | solution.py:16
  29.9 9.2 %collective-permute-start.7 = (f32[256,512]{1,0:T(8,128)}, f32[256,512]{1,0:T(8,128)}, u32[]{:S(2)}, u32[]{:S(2)}) collective-permute-start(f32[256,512]{1,0:T(8,128)} %collective-permute-done.5.refs_7_), channel_id=1, source_target_pairs={{0,8},{8,0},{16,24},{24,16},{1,9},{9,1},{17,25},{25,17},{2,10},{10... | collective-permute-start | bytes 1572872 | tf_op jit(solution)/shard_map/ppermute | solution.py:16
  30.1 2.2 %copy-start.1 = (bf16[512,16,256]{2,1,0:T(8,128)(2,1)S(1)}, bf16[512,16,256]{2,1,0:T(8,128)(2,1)}, u32[]{:S(2)}) copy-start(bf16[512,16,256]{2,1,0:T(8,128)(2,1)} %param.4) | copy-start | bytes 12582916
  45.3 3.1 %copy-start.4 = (bf16[1024,1024]{1,0:T(8,128)(2,1)}, bf16[1024,1024]{1,0:T(8,128)(2,1)S(1)}, u32[]{:S(2)}) copy-start(bf16[1024,1024]{1,0:T(8,128)(2,1)S(1)} %get-tuple-element.116.left) | copy-start | bytes 6291460
  45.3 2.9 %collective-permute-start.8 = (f32[256,1152]{1,0:T(8,128)S(1)}, f32[256,1152]{1,0:T(8,128)S(1)}, u32[]{:S(2)}, u32[]{:S(2)}) collective-permute-start(f32[256,1152]{1,0:T(8,128)S(1)} %get-tuple-element.72), channel_id=1, source_target_pairs={{0,8},{8,0},{16,24},{24,16},{1,9},{9,1},{17,25},{25,17},{2,10},{10... | collective-permute-start | bytes 3538952 | tf_op jit(solution)/shard_map/ppermute | solution.py:16
  48.4 7.0 %collective-permute-start.10 = (f32[128,384]{1,0:T(8,128)S(1)}, f32[128,384]{1,0:T(8,128)S(1)}, u32[]{:S(2)}, u32[]{:S(2)}) collective-permute-start(f32[128,384]{1,0:T(8,128)S(1)} %get-tuple-element.74), channel_id=1, source_target_pairs={{0,1},{1,0},{2,3},{3,2},{4,5},{5,4},{6,7},{7,6},{8,9},{9,8},{10,11... | collective-permute-start | bytes 589832 | tf_op jit(solution)/shard_map/ppermute | solution.py:16
  50.2 6.7 %collective-permute-start.11 = (f32[128,384]{1,0:T(8,128)S(1)}, f32[128,384]{1,0:T(8,128)S(1)}, u32[]{:S(2)}, u32[]{:S(2)}) collective-permute-start(f32[128,384]{1,0:T(8,128)S(1)} %get-tuple-element.75), channel_id=1, source_target_pairs={{0,2},{2,0},{4,6},{6,4},{1,3},{3,1},{5,7},{7,5},{8,10},{10,8},{12,... | collective-permute-start | bytes 589832 | tf_op jit(solution)/shard_map/ppermute | solution.py:16
  51.7 6.4 %collective-permute-start.9 = (f32[128,384]{1,0:T(8,128)S(1)}, f32[128,384]{1,0:T(8,128)S(1)}, u32[]{:S(2)}, u32[]{:S(2)}) collective-permute-start(f32[128,384]{1,0:T(8,128)S(1)} %get-tuple-element.73), channel_id=1, source_target_pairs={{0,16},{8,24},{16,0},{24,8},{1,17},{9,25},{17,1},{25,9},{2,18},{10... | collective-permute-start | bytes 589832 | tf_op jit(solution)/shard_map/ppermute | solution.py:16
  58.3 4.7 %collective-permute-start.12 = (f32[64,384]{1,0:T(8,128)S(1)}, f32[64,384]{1,0:T(8,128)S(1)}, u32[]{:S(2)}, u32[]{:S(2)}) collective-permute-start(f32[64,384]{1,0:T(8,128)S(1)} %slice.106), channel_id=1, source_target_pairs={{0,1},{1,0},{2,3},{3,2},{4,5},{5,4},{6,7},{7,6},{8,9},{9,8},{10,11... | collective-permute-start | bytes 294920 | tf_op jit(solution)/shard_map/ppermute | solution.py:16
  58.9 4.6 %collective-permute-start.13 = (f32[64,384]{1,0:T(8,128)S(1)}, f32[64,384]{1,0:T(8,128)S(1)}, u32[]{:S(2)}, u32[]{:S(2)}) collective-permute-start(f32[64,384]{1,0:T(8,128)S(1)} %slice.108), channel_id=1, source_target_pairs={{0,2},{2,0},{4,6},{6,4},{1,3},{3,1},{5,7},{7,5},{8,10},{10,8},{12,... | collective-permute-start | bytes 294920 | tf_op jit(solution)/shard_map/ppermute | solution.py:16
  59.2 4.6 %collective-permute-start.14 = (f32[64,384]{1,0:T(8,128)S(1)}, f32[64,384]{1,0:T(8,128)S(1)}, u32[]{:S(2)}, u32[]{:S(2)}) collective-permute-start(f32[64,384]{1,0:T(8,128)S(1)} %slice.110), channel_id=1, source_target_pairs={{0,16},{8,24},{16,0},{24,8},{1,17},{9,25},{17,1},{25,9},{2,18},{10... | collective-permute-start | bytes 294920 | tf_op jit(solution)/shard_map/ppermute | solution.py:16
  63.9 5.0 %collective-permute-start.15 = (f32[32,384]{1,0:T(8,128)S(1)}, f32[32,384]{1,0:T(8,128)S(1)}, u32[]{:S(2)}, u32[]{:S(2)}) collective-permute-start(f32[32,384]{1,0:T(8,128)S(1)} %slice.112), channel_id=1, source_target_pairs={{0,2},{2,0},{4,6},{6,4},{1,3},{3,1},{5,7},{7,5},{8,10},{10,8},{12,... | collective-permute-start | bytes 147464 | tf_op jit(solution)/shard_map/ppermute | solution.py:16
  65.6 4.1 %collective-permute-start.16 = (f32[32,384]{1,0:T(8,128)S(1)}, f32[32,384]{1,0:T(8,128)S(1)}, u32[]{:S(2)}, u32[]{:S(2)}) collective-permute-start(f32[32,384]{1,0:T(8,128)S(1)} %slice.114), channel_id=1, source_target_pairs={{0,16},{8,24},{16,0},{24,8},{1,17},{9,25},{17,1},{25,9},{2,18},{10... | collective-permute-start | bytes 147464 | tf_op jit(solution)/shard_map/ppermute | solution.py:16
  67.1 4.1 %collective-permute-start.17 = (f32[32,384]{1,0:T(8,128)S(1)}, f32[32,384]{1,0:T(8,128)S(1)}, u32[]{:S(2)}, u32[]{:S(2)}) collective-permute-start(f32[32,384]{1,0:T(8,128)S(1)} %slice.116), channel_id=1, source_target_pairs={{0,1},{1,0},{2,3},{3,2},{4,5},{5,4},{6,7},{7,6},{8,9},{9,8},{10,11... | collective-permute-start | bytes 147464 | tf_op jit(solution)/shard_map/ppermute | solution.py:16
  68.7 2.6 %collective-permute-start.18 = (f32[2,384,256]{2,1,0:T(8,128)S(1)}, f32[2,384,256]{2,1,0:T(8,128)S(1)}, u32[]{:S(2)}, u32[]{:S(2)}) collective-permute-start(f32[2,384,256]{2,1,0:T(8,128)S(1)} %slice.96.refs_4_), channel_id=1, source_target_pairs={{0,8},{8,0},{16,24},{24,16},{1,9},{9,1},{17,25},{25,17},{2,10},{10... | collective-permute-start | bytes 2359304 | tf_op jit(solution)/shard_map/ppermute | solution.py:16
  71.3 9.9 %collective-permute-start.20 = (f32[2,128,256]{2,1,0:T(8,128)S(1)}, f32[2,128,256]{2,1,0:T(8,128)S(1)}, u32[]{:S(2)}, u32[]{:S(2)}) collective-permute-start(f32[2,128,256]{2,1,0:T(8,128)S(1)} %slice.97.refs_0_), channel_id=1, source_target_pairs={{0,16},{8,24},{16,0},{24,8},{1,17},{9,25},{17,1},{25,9},{2,18},{10... | collective-permute-start | bytes 786440 | tf_op jit(solution)/shard_map/ppermute | solution.py:16
  71.9 9.3 %collective-permute-start.19 = (f32[32,1152]{1,0:T(8,128)S(1)}, f32[32,1152]{1,0:T(8,128)S(1)}, u32[]{:S(2)}, u32[]{:S(2)}) collective-permute-start(f32[32,1152]{1,0:T(8,128)S(1)} %pad_maximum_fusion.3), channel_id=1, source_target_pairs={{0,4},{2,6},{4,0},{6,2},{1,5},{3,7},{5,1},{7,3},{8,12},{10,14},{12... | collective-permute-start | bytes 442376 | tf_op jit(solution)/shard_map/ppermute | solution.py:16
  81.2 4.2 %collective-permute-start.21 = (f32[32,384]{1,0:T(8,128)S(1)}, f32[32,384]{1,0:T(8,128)S(1)}, u32[]{:S(2)}, u32[]{:S(2)}) collective-permute-start(f32[32,384]{1,0:T(8,128)S(1)} %get-tuple-element.97), channel_id=1, source_target_pairs={{0,2},{2,0},{4,6},{6,4},{1,3},{3,1},{5,7},{7,5},{8,10},{10,8},{12,... | collective-permute-start | bytes 147464 | tf_op jit(solution)/shard_map/ppermute | solution.py:16
  81.3 4.2 %collective-permute-start.22 = (f32[32,384]{1,0:T(8,128)S(1)}, f32[32,384]{1,0:T(8,128)S(1)}, u32[]{:S(2)}, u32[]{:S(2)}) collective-permute-start(f32[32,384]{1,0:T(8,128)S(1)} %get-tuple-element.98), channel_id=1, source_target_pairs={{0,16},{8,24},{16,0},{24,8},{1,17},{9,25},{17,1},{25,9},{2,18},{10... | collective-permute-start | bytes 147464 | tf_op jit(solution)/shard_map/ppermute | solution.py:16
  82.9 4.1 %collective-permute-start.23 = (f32[32,384]{1,0:T(8,128)S(1)}, f32[32,384]{1,0:T(8,128)S(1)}, u32[]{:S(2)}, u32[]{:S(2)}) collective-permute-start(f32[32,384]{1,0:T(8,128)S(1)} %get-tuple-element.99), channel_id=1, source_target_pairs={{0,1},{1,0},{2,3},{3,2},{4,5},{5,4},{6,7},{7,6},{8,9},{9,8},{10,11... | collective-permute-start | bytes 147464 | tf_op jit(solution)/shard_map/ppermute | solution.py:16
  87.0 4.7 %collective-permute-start.24 = (f32[64,384]{1,0:T(8,128)S(1)}, f32[64,384]{1,0:T(8,128)S(1)}, u32[]{:S(2)}, u32[]{:S(2)}) collective-permute-start(f32[64,384]{1,0:T(8,128)S(1)} %pad_maximum_fusion.4), channel_id=1, source_target_pairs={{0,1},{1,0},{2,3},{3,2},{4,5},{5,4},{6,7},{7,6},{8,9},{9,8},{10,11... | collective-permute-start | bytes 294920 | tf_op jit(solution)/shard_map/ppermute | solution.py:16
  87.6 4.6 %collective-permute-start.25 = (f32[64,384]{1,0:T(8,128)S(1)}, f32[64,384]{1,0:T(8,128)S(1)}, u32[]{:S(2)}, u32[]{:S(2)}) collective-permute-start(f32[64,384]{1,0:T(8,128)S(1)} %pad_maximum_fusion.5), channel_id=1, source_target_pairs={{0,2},{2,0},{4,6},{6,4},{1,3},{3,1},{5,7},{7,5},{8,10},{10,8},{12,... | collective-permute-start | bytes 294920 | tf_op jit(solution)/shard_map/ppermute | solution.py:16
  89.5 4.9 %collective-permute-start.26 = (f32[64,384]{1,0:T(8,128)S(1)}, f32[64,384]{1,0:T(8,128)S(1)}, u32[]{:S(2)}, u32[]{:S(2)}) collective-permute-start(f32[64,384]{1,0:T(8,128)S(1)} %pad_maximum_fusion.6), channel_id=1, source_target_pairs={{0,16},{8,24},{16,0},{24,8},{1,17},{9,25},{17,1},{25,9},{2,18},{10... | collective-permute-start | bytes 294920 | tf_op jit(solution)/shard_map/ppermute | solution.py:16
  94.5 5.7 %collective-permute-start.27 = (f32[128,384]{1,0:T(8,128)S(1)}, f32[128,384]{1,0:T(8,128)S(1)}, u32[]{:S(2)}, u32[]{:S(2)}) collective-permute-start(f32[128,384]{1,0:T(8,128)S(1)} %pad_maximum_fusion), channel_id=1, source_target_pairs={{0,16},{8,24},{16,0},{24,8},{1,17},{9,25},{17,1},{25,9},{2,18},{10... | collective-permute-start | bytes 589832 | tf_op jit(solution)/shard_map/ppermute | solution.py:16
  95.2 5.7 %collective-permute-start.28 = (f32[128,384]{1,0:T(8,128)S(1)}, f32[128,384]{1,0:T(8,128)S(1)}, u32[]{:S(2)}, u32[]{:S(2)}) collective-permute-start(f32[128,384]{1,0:T(8,128)S(1)} %pad_maximum_fusion.1), channel_id=1, source_target_pairs={{0,1},{1,0},{2,3},{3,2},{4,5},{5,4},{6,7},{7,6},{8,9},{9,8},{10,11... | collective-permute-start | bytes 589832 | tf_op jit(solution)/shard_map/ppermute | solution.py:16
  96.7 5.7 %collective-permute-start.29 = (f32[128,384]{1,0:T(8,128)S(1)}, f32[128,384]{1,0:T(8,128)S(1)}, u32[]{:S(2)}, u32[]{:S(2)}) collective-permute-start(f32[128,384]{1,0:T(8,128)S(1)} %pad_maximum_fusion.2), channel_id=1, source_target_pairs={{0,2},{2,0},{4,6},{6,4},{1,3},{3,1},{5,7},{7,5},{8,10},{10,8},{12,... | collective-permute-start | bytes 589832 | tf_op jit(solution)/shard_map/ppermute | solution.py:16
  102.5 2.9 %collective-permute-start.30 = (f32[256,1152]{1,0:T(8,128)S(1)}, f32[256,1152]{1,0:T(8,128)S(1)}, u32[]{:S(2)}, u32[]{:S(2)}) collective-permute-start(f32[256,1152]{1,0:T(8,128)S(1)} %maximum_maximum_fusion.mine_ref), channel_id=1, source_target_pairs={{0,8},{8,0},{16,24},{24,16},{1,9},{9,1},{17,25},{25,17},{2,10},{10... | collective-permute-start | bytes 3538952 | tf_op jit(solution)/shard_map/ppermute | solution.py:16
  102.5 37.1 %collective-permute-start.31 = (f32[2,128,256]{2,1,0:T(8,128)S(1)}, f32[2,128,256]{2,1,0:T(8,128)S(1)}, u32[]{:S(2)}, u32[]{:S(2)}) collective-permute-start(f32[2,128,256]{2,1,0:T(8,128)S(1)} %slice.97.refs_0_), channel_id=1, source_target_pairs={{0,8},{8,0},{16,24},{24,16},{1,9},{9,1},{17,25},{25,17},{2,10},{10... | collective-permute-start | bytes 786440 | tf_op jit(solution)/shard_map/ppermute | solution.py:16
  103.0 36.6 %collective-permute-start.32 = (f32[2,128,256]{2,1,0:T(8,128)S(1)}, f32[2,128,256]{2,1,0:T(8,128)S(1)}, u32[]{:S(2)}, u32[]{:S(2)}) collective-permute-start(f32[2,128,256]{2,1,0:T(8,128)S(1)} %collective-permute-done.20.refs_2_), channel_id=1, source_target_pairs={{0,8},{8,0},{16,24},{24,16},{1,9},{9,1},{17,25},{25,17},{2,10},{10... | collective-permute-start | bytes 786440 | tf_op jit(solution)/shard_map/ppermute | solution.py:16
  103.1 36.5 %collective-permute-start.33 = (f32[2,384,256]{2,1,0:T(8,128)S(1)}, f32[2,384,256]{2,1,0:T(8,128)S(1)}, u32[]{:S(2)}, u32[]{:S(2)}) collective-permute-start(f32[2,384,256]{2,1,0:T(8,128)S(1)} %slice.96.refs_4_), channel_id=1, source_target_pairs={{0,16},{8,24},{16,0},{24,8},{1,17},{9,25},{17,1},{25,9},{2,18},{10... | collective-permute-start | bytes 2359304 | tf_op jit(solution)/shard_map/ppermute | solution.py:16
  104.3 35.6 %collective-permute-start.34 = (f32[2,384,256]{2,1,0:T(8,128)S(1)}, f32[2,384,256]{2,1,0:T(8,128)S(1)}, u32[]{:S(2)}, u32[]{:S(2)}) collective-permute-start(f32[2,384,256]{2,1,0:T(8,128)S(1)} %collective-permute-done.18.refs_5_), channel_id=1, source_target_pairs={{0,16},{8,24},{16,0},{24,8},{1,17},{9,25},{17,1},{25,9},{2,18},{10... | collective-permute-start | bytes 2359304 | tf_op jit(solution)/shard_map/ppermute | solution.py:16
  105.4 1.0 copy-start.5

commit v3 on v2

--- a/solution.py
+++ b/solution.py
@@ -392,43 +392,51 @@
             pltpu.VMEM((PIECES, chi, chi), jnp.bfloat16),
             pltpu.VMEM((chi, chi), jnp.float32),
         ],
-        compiler_params=pltpu.CompilerParams(vmem_limit_bytes=52 * 2**20),
+        compiler_params=pltpu.CompilerParams(vmem_limit_bytes=40 * 2**20),
         cost_estimate=pl.CostEstimate(flops=20 * 2 * chi**3, bytes_accessed=16 * chi**2, transcendentals=0),
     )(places, mine, other, left)
 
 
-def site_kernel(scale, slots, place_ref, weights_ref, own_ref, *refs):
-    *got_refs, out_ref = refs
+def site_kernel(scale, place_ref, weights_ref, own_ref, first_ref, second_ref, *refs):
+    out_ref = refs[-1]
     depth = own_ref.shape[1]
     mine = weights_ref[:, pl.ds(pl.multiple_of(place_ref[1] * depth, depth), depth)]
-    first = pl.multiple_of((place_ref[1] ^ 1) * depth, depth)
-    count = own_ref.shape[0] // slots
-    for slot in range(slots):
-        for i in range(count):
-            e = (place_ref[0] ^ slot) * count + i
-            total, at = dot(mine, own_ref[e]), first
-            for got_ref in got_refs[slot::slots]:
-                part = got_ref.shape[1]
-                total = total + dot(weights_ref[:, pl.ds(at, part)], got_ref[i].astype(jnp.bfloat16))
-                at = pl.multiple_of(at + part, BLOCK)
-            out_ref[e] = scale * total
-
-
-def make_site(weights, own, got, places, scale):
+    other = weights_ref[:, pl.ds(pl.multiple_of((place_ref[1] ^ 1) * depth, depth), depth)]
+    got = jnp.where(pl.program_id(0) == 0, first_ref[0], second_ref[0]).astype(jnp.bfloat16)
+    out_ref[0] = scale * (dot(mine, own_ref[0]) + dot(other, got))
+
+
+def make_site(weights, own, slots, got, places, scale, before):
     rows, chi = weights.shape
-    east, _, right = own.shape
-    whole = pl.BlockSpec(memory_space=pltpu.VMEM)
-    pieces = sum(got, [])
+    east, depth, right = own.shape
+    count = got[0].shape[0]
+    first, second = slots
+
+    def leg(s, i, place_ref):
+        return ((place_ref[0] ^ (first + s * (second - first))) * count + i, 0, 0)
+
+    piece = pl.BlockSpec((1, depth, right), lambda s, i, place_ref: (i, 0, 0))
     return pl.pallas_call(
-        functools.partial(site_kernel, scale, len(got[0])),
+        functools.partial(site_kernel, scale),
         out_shape=jax.ShapeDtypeStruct((east, rows, right), jnp.float32),
-        in_specs=[pl.BlockSpec(memory_space=pltpu.SMEM)] + [whole] * (2 + len(pieces)),
-        out_specs=whole,
-        compiler_params=pltpu.CompilerParams(vmem_limit_bytes=32 * 2**20),
+        grid_spec=pltpu.PrefetchScalarGridSpec(
+            num_scalar_prefetch=1,
+            grid=(2, count),
+            in_specs=[
+                pl.BlockSpec((rows, chi), lambda s, i, place_ref: (0, 0)),
+                pl.BlockSpec((1, depth, right), leg),
+                piece,
+                piece,
+            ]
+            + [pl.BlockSpec(memory_space=pl.ANY)] * len(before),
+            out_specs=pl.BlockSpec((1, rows, right), leg),
+        ),
+        input_output_aliases={5: 0} if before else {},
+        compiler_params=pltpu.CompilerParams(vmem_limit_bytes=24 * 2**20),
         cost_estimate=pl.CostEstimate(
-            flops=2 * rows * chi * east * right, bytes_accessed=8 * east * chi * right, transcendentals=0
+            flops=rows * chi * east * right, bytes_accessed=4 * east * chi * right, transcendentals=0
         ),
-    )(places, weights, own, *pieces)
+    )(places, weights, own, *got, *before)
 
 
 def shards(sizes, left_factor, boundary_site, double_layer):
@@ -473,31 +481,27 @@
     parts = [whole[:, i * third : (i + 1) * third] for i in range(3)]
     parts = reduce_parts(parts, orders, cut)
     whole = jnp.concatenate(parts, 1)
-    cut_depth = depth // 4
-    ahead = rep == 2 and right_parts == 1 and len(across) == 1 and far and cut_depth % BLOCK == 0
-    after = [got[0][:, cut_depth:]] if ahead else got
-    pairs = [[piece, swap(piece, core[0])] for piece in after]
+    pairs = [[piece, swap(piece, core[0])] for piece in got]
     whole, pairs = lax.optimization_barrier((whole, pairs))
-    for i, step in enumerate(far):
-        if ahead and i == 0:
-            early = got[0][:, :cut_depth]
-            other, crossed = swap_parts([whole, early], [step, across[0]])
-            early = gather_slots([(0, early), (across[0][2], crossed)], core)
-        else:
-            other = swap(whole, step)
-        whole = whole + other
+    for step in far:
+        whole = whole + swap(whole, step)
     parts = [whole[:, i * third : (i + 1) * third] for i in range(3)]
     parts = gather_parts(parts, orders, cut)
     whole = jnp.concatenate(parts, 1)
     other = swap(whole, core[0])
     pairs, whole = lax.optimization_barrier((pairs, whole))
-    got = [gather_slots(list(zip(range(2), pair)), across[::-1]) for pair in pairs]
+    halved = rep == 2 and right_parts == 1 and len(across) == 1
+    if halved:
+        crossed = swap(pairs[0][0], across[0])
 
     factor, weights = factorize(whole, other, left, places, row_count, chunk, scale)
-    if rep == 2 and right_parts == 1:
-        pieces = [[piece for _, piece in sorted(held, key=lambda pair: pair[0])] for held in ([early] if ahead else []) + got]
-        site_q = make_site(weights, own, pieces, places, scale)
+    if halved:
+        crossed, weights = lax.optimization_barrier((crossed, weights))
+        pair = [crossed, swap(crossed, core[0])]
+        site_q = make_site(weights, own, (0, 1), pairs[0], places, scale, [])
+        site_q = make_site(weights, own, (2, 3), pair, places, scale, [site_q])
     else:
+        got = [gather_slots(list(zip(range(2), pair)), across[::-1]) for pair in pairs]
         nothing = double_layer[0, 0] * 0.0
         site = jnp.zeros((east, chi, right), jnp.bfloat16)
         site = lax.dynamic_update_slice(site, own, (0, p * depth, 0))

time: 144 us -> 141 us (0.979)
  waiting for transfers between devices: 50.7 us -> 48.7 us
    pallas_call x1 -> x2, Pallas kernels: 3.43 us -> 6.01 us  [make_site(): pl.pallas_call(functools.partial(site_kernel, scale), out_shape=jax.Shape...]
    ppermute x35 -> x32, waiting for transfers between devices: 50.7 us -> 48.7 us  [swap(): return lax.ppermute(array, axis, [(i, i ^ distance) for i in range(size)])]
    unnamed x12 -> x8, local copies, waits for them, and re-layouts: 6.11 us -> 5.08 us
    ppermute x35 -> x32, starting transfers between devices: 33.3 us -> 32.6 us  [swap(): return lax.ppermute(array, axis, [(i, i ^ distance) for i in range(size)])]
  transfers between devices with their start and end apart: 35 -> 32, of which waited for: 24 -> 22; matrix products, arithmetic and copies ran while one was open for 0% -> 0% of each run, Pallas kernels for 28% -> 30%
where the time goes in v3:
time: 141 us
  Pallas kernels  51.5 us (37%)
  waiting for transfers between devices  48.7 us (35%)
  starting transfers between devices  32.6 us (23%)
  local copies, waits for them, and re-layouts  5.38 us (4%)
  other arithmetic  1.51 us (1%)
    ppermute x32, waiting for transfers between devices, swap(): return lax.ppermute(array, axis, [(i, i ^ distance) for i in range(size)])  48.7 us
    ppermute x32, starting transfers between devices, swap(): return lax.ppermute(array, axis, [(i, i ^ distance) for i in range(size)])  32.6 us
    pallas_call x1, Pallas kernels, factorize(): pl.pallas_call(functools.partial(factor_kernel, scale, chunk), out_shape=...  31.8 us
    pallas_call x2, Pallas kernels, absorb(): pl.pallas_call(functools.partial(absorb_kernel, east_parts), grid=(tiles,...  7.48 us
    pallas_call x1, Pallas kernels, gram_of_columns(): pl.pallas_call(functools.partial(gram_kernel, chi, chunk, width // 3, len...  6.17 us
    pallas_call x2, Pallas kernels, make_site(): pl.pallas_call(functools.partial(site_kernel, scale), out_shape=jax.Shape...  6.01 us
    unnamed x8, local copies, waits for them, and re-layouts  5.08 us
  transfers between devices with their start and end apart: 32, of which 22 were waited for; matrix products, arithmetic and copies ran while one was open for 0% of the time, Pallas kernels for 30%

profile of v3, /device:TPU:0, one launch (start us, length us, event | category | flops | bytes accessed | tf_op | source)
XLA Modules:
  0.0 140.6 jit_solution(189069910987955367)
XLA Ops:
  0.6 1.0 convert_element_type.3.refs_2_
  1.6 3.0 %collective-permute-start.1 = (f32[256,512]{1,0:T(8,128)S(1)}, f32[256,512]{1,0:T(8,128)S(1)}, u32[]{:S(2)}, u32[]{:S(2)}) collective-permute-start(f32[256,512]{1,0:T(8,128)S(1)} %convert_element_type.3.refs_2_), channel_id=1, source_target_pairs={{0,1},{1,0},{2,3},{3,2},{4,5},{5,4},{6,7},{7,6},{8,9},{9,8},{10,11... | collective-permute-start | bytes 1572872 | tf_op jit(solution)/shard_map/ppermute | solution.py:16
  4.7 1.5 %collective-permute-start.4 = (f32[256,512]{1,0:T(8,128)S(1)}, f32[256,512]{1,0:T(8,128)}, u32[]{:S(2)}, u32[]{:S(2)}) collective-permute-start(f32[256,512]{1,0:T(8,128)S(1)} %convert_element_type.3.refs_2_), channel_id=1, source_target_pairs={{0,16},{8,24},{16,0},{24,8},{1,17},{9,25},{17,1},{25,9},{2,18},{10... | collective-permute-start | bytes 1572872 | tf_op jit(solution)/shard_map/ppermute | solution.py:16
  6.2 2.2 %copy-done = bf16[512,16,256]{2,1,0:T(8,128)(2,1)S(1)} copy-done((bf16[512,16,256]{2,1,0:T(8,128)(2,1)S(1)}, bf16[512,16,256]{2,1,0:T(8,128)(2,1)}, u32[]{:S(2)}) %copy-start) | copy-done | bytes 4194328
  8.4 0.7 copy-done.2
  9.1 3.0 %shard_map.51 = f32[2,512,256]{2,1,0:T(8,128)S(1)} custom-call(s32[2]{0:T(128)S(1)} %pad_add_fusion.legs_ref, bf16[8192,256]{1,0:T(8,128)(2,1)S(1)} %bitcast.16, f32[16,16]{1,0:T(8,128)S(1)} %copy-done.2), custom_call_target="tpu_custom_call" | custom-call | flops 268435456 | bytes 16777216 | tf_op jit(solution)/shard_map/pallas_call | solution.py:118
  12.2 0.6 collective-permute-start
  12.7 4.7 %collective-permute-done.1.refs_3_ = f32[256,512]{1,0:T(8,128)S(1)} collective-permute-done((f32[256,512]{1,0:T(8,128)S(1)}, f32[256,512]{1,0:T(8,128)S(1)}, u32[]{:S(2)}, u32[]{:S(2)}) %collective-permute-start.1) | collective-permute-done | bytes 524320 | tf_op jit(solution)/shard_map/ppermute | solution.py:16
  17.4 2.0 %collective-permute-start.5 = (f32[256,512]{1,0:T(8,128)S(1)}, f32[256,512]{1,0:T(8,128)}, u32[]{:S(2)}, u32[]{:S(2)}) collective-permute-start(f32[256,512]{1,0:T(8,128)S(1)} %collective-permute-done.1.refs_3_), channel_id=1, source_target_pairs={{0,16},{8,24},{16,0},{24,8},{1,17},{9,25},{17,1},{25,9},{2,18},{10... | collective-permute-start | bytes 1572872 | tf_op jit(solution)/shard_map/ppermute | solution.py:16
  20.0 9.9 %collective-permute-done.5.refs_7_ = f32[256,512]{1,0:T(8,128)} collective-permute-done((f32[256,512]{1,0:T(8,128)S(1)}, f32[256,512]{1,0:T(8,128)}, u32[]{:S(2)}, u32[]{:S(2)}) %collective-permute-start.5) | collective-permute-done | bytes 524320 | tf_op jit(solution)/shard_map/ppermute | solution.py:16
  30.1 2.2 %copy-done.1 = bf16[512,16,256]{2,1,0:T(8,128)(2,1)S(1)} copy-done((bf16[512,16,256]{2,1,0:T(8,128)(2,1)S(1)}, bf16[512,16,256]{2,1,0:T(8,128)(2,1)}, u32[]{:S(2)}) %copy-start.1) | copy-done | bytes 4194328
  32.3 4.4 %shard_map.50.own_ref = bf16[8,512,256]{2,1,0:T(8,128)(2,1)S(1)} custom-call(s32[8]{0:T(128)S(1)} %stack.68.legs_ref, bf16[8192,256]{1,0:T(8,128)(2,1)S(1)} %bitcast.17, f32[16,16]{1,0:T(8,128)S(1)} %copy-done.3), custom_call_target="tpu_custom_call" | custom-call | flops 1073741824 | bytes 16777216 | tf_op jit(solution)/shard_map/pallas_call | solution.py:118
  36.8 2.3 %collective-permute-done.refs_1_.first_ref = f32[2,512,256]{2,1,0:T(8,128)S(1)} collective-permute-done((f32[2,512,256]{2,1,0:T(8,128)S(1)}, f32[2,512,256]{2,1,0:T(8,128)S(1)}, u32[]{:S(2)}, u32[]{:S(2)}) %collective-permute-start) | collective-permute-done | bytes 1048608 | tf_op jit(solution)/shard_map/ppermute | solution.py:16
  39.1 6.2 %shard_map.52 = (f32[256,1152]{1,0:T(8,128)S(1)}, f32[256,1152]{1,0:T(8,128)S(1)}, bf16[1024,1024]{1,0:T(8,128)(2,1)S(1)}) custom-call(s32[5]{0:T(128)S(1)} %stack.59.place_ref, bf16[2,512,256]{2,1,0:T(8,128)(2,1)S(1)} %constant_dynamic-slice_fusion.refs_0_, f32[2,512,256]{2,1,0:T(8,128)S(1)} %collective-permute-done.refs_1_.first_ref, ...), custom_call_target="tpu_custom_call" | custom-call | flops 2684354560 | bytes 12582912 | tf_op jit(solution)/shard_map/pallas_call | solution.py:174
  45.3 2.8 %collective-permute-done.8 = f32[256,1152]{1,0:T(8,128)S(1)} collective-permute-done((f32[256,1152]{1,0:T(8,128)S(1)}, f32[256,1152]{1,0:T(8,128)S(1)}, u32[]{:S(2)}, u32[]{:S(2)}) %collective-permute-start.8) | collective-permute-done | bytes 1179680 | tf_op jit(solution)/shard_map/ppermute | solution.py:16
  48.3 1.8 %collective-permute-start.10 = (f32[128,384]{1,0:T(8,128)S(1)}, f32[128,384]{1,0:T(8,128)S(1)}, u32[]{:S(2)}, u32[]{:S(2)}) collective-permute-start(f32[128,384]{1,0:T(8,128)S(1)} %get-tuple-element.72), channel_id=1, source_target_pairs={{0,1},{1,0},{2,3},{3,2},{4,5},{5,4},{6,7},{7,6},{8,9},{9,8},{10,11... | collective-permute-start | bytes 589832 | tf_op jit(solution)/shard_map/ppermute | solution.py:16
  50.2 1.6 %collective-permute-start.11 = (f32[128,384]{1,0:T(8,128)S(1)}, f32[128,384]{1,0:T(8,128)S(1)}, u32[]{:S(2)}, u32[]{:S(2)}) collective-permute-start(f32[128,384]{1,0:T(8,128)S(1)} %get-tuple-element.73), channel_id=1, source_target_pairs={{0,2},{2,0},{4,6},{6,4},{1,3},{3,1},{5,7},{7,5},{8,10},{10,8},{12,... | collective-permute-start | bytes 589832 | tf_op jit(solution)/shard_map/ppermute | solution.py:16
  51.7 1.5 %collective-permute-start.9 = (f32[128,384]{1,0:T(8,128)S(1)}, f32[128,384]{1,0:T(8,128)S(1)}, u32[]{:S(2)}, u32[]{:S(2)}) collective-permute-start(f32[128,384]{1,0:T(8,128)S(1)} %get-tuple-element.71), channel_id=1, source_target_pairs={{0,16},{8,24},{16,0},{24,8},{1,17},{9,25},{17,1},{25,9},{2,18},{10... | collective-permute-start | bytes 589832 | tf_op jit(solution)/shard_map/ppermute | solution.py:16
  53.2 2.1 %collective-permute-done.10 = f32[128,384]{1,0:T(8,128)S(1)} collective-permute-done((f32[128,384]{1,0:T(8,128)S(1)}, f32[128,384]{1,0:T(8,128)S(1)}, u32[]{:S(2)}, u32[]{:S(2)}) %collective-permute-start.10) | collective-permute-done | bytes 196640 | tf_op jit(solution)/shard_map/ppermute | solution.py:16
  55.4 1.5 %collective-permute-done.11 = f32[128,384]{1,0:T(8,128)S(1)} collective-permute-done((f32[128,384]{1,0:T(8,128)S(1)}, f32[128,384]{1,0:T(8,128)S(1)}, u32[]{:S(2)}, u32[]{:S(2)}) %collective-permute-start.11) | collective-permute-done | bytes 196640 | tf_op jit(solution)/shard_map/ppermute | solution.py:16
  56.8 1.3 collective-permute-done.9
  58.2 0.6 collective-permute-start.12
  59.1 1.6 %collective-permute-start.14 = (f32[64,384]{1,0:T(8,128)S(1)}, f32[64,384]{1,0:T(8,128)S(1)}, u32[]{:S(2)}, u32[]{:S(2)}) collective-permute-start(f32[64,384]{1,0:T(8,128)S(1)} %slice.102), channel_id=1, source_target_pairs={{0,16},{8,24},{16,0},{24,8},{1,17},{9,25},{17,1},{25,9},{2,18},{10... | collective-permute-start | bytes 294920 | tf_op jit(solution)/shard_map/ppermute | solution.py:16
  60.8 2.2 %collective-permute-done.12 = f32[64,384]{1,0:T(8,128)S(1)} collective-permute-done((f32[64,384]{1,0:T(8,128)S(1)}, f32[64,384]{1,0:T(8,128)S(1)}, u32[]{:S(2)}, u32[]{:S(2)}) %collective-permute-start.12) | collective-permute-done | bytes 98336 | tf_op jit(solution)/shard_map/ppermute | solution.py:16
  63.8 1.8 %collective-permute-start.15 = (f32[32,384]{1,0:T(8,128)S(1)}, f32[32,384]{1,0:T(8,128)S(1)}, u32[]{:S(2)}, u32[]{:S(2)}) collective-permute-start(f32[32,384]{1,0:T(8,128)S(1)} %slice.104), channel_id=1, source_target_pairs={{0,2},{2,0},{4,6},{6,4},{1,3},{3,1},{5,7},{7,5},{8,10},{10,8},{12,... | collective-permute-start | bytes 147464 | tf_op jit(solution)/shard_map/ppermute | solution.py:16
  65.6 1.5 %collective-permute-start.16 = (f32[32,384]{1,0:T(8,128)S(1)}, f32[32,384]{1,0:T(8,128)S(1)}, u32[]{:S(2)}, u32[]{:S(2)}) collective-permute-start(f32[32,384]{1,0:T(8,128)S(1)} %slice.106), channel_id=1, source_target_pairs={{0,16},{8,24},{16,0},{24,8},{1,17},{9,25},{17,1},{25,9},{2,18},{10... | collective-permute-start | bytes 147464 | tf_op jit(solution)/shard_map/ppermute | solution.py:16
  67.1 1.5 %collective-permute-start.17 = (f32[32,384]{1,0:T(8,128)S(1)}, f32[32,384]{1,0:T(8,128)S(1)}, u32[]{:S(2)}, u32[]{:S(2)}) collective-permute-start(f32[32,384]{1,0:T(8,128)S(1)} %slice.108), channel_id=1, source_target_pairs={{0,1},{1,0},{2,3},{3,2},{4,5},{5,4},{6,7},{7,6},{8,9},{9,8},{10,11... | collective-permute-start | bytes 147464 | tf_op jit(solution)/shard_map/ppermute | solution.py:16
  68.6 1.1 collective-permute-done.16
  69.7 1.5 %collective-permute-done.17 = f32[32,384]{1,0:T(8,128)S(1)} collective-permute-done((f32[32,384]{1,0:T(8,128)S(1)}, f32[32,384]{1,0:T(8,128)S(1)}, u32[]{:S(2)}, u32[]{:S(2)}) %collective-permute-start.17) | collective-permute-done | bytes 49184 | tf_op jit(solution)/shard_map/ppermute | solution.py:16
  71.3 2.7 %collective-permute-start.19 = (f32[32,1152]{1,0:T(8,128)S(1)}, f32[32,1152]{1,0:T(8,128)S(1)}, u32[]{:S(2)}, u32[]{:S(2)}) collective-permute-start(f32[32,1152]{1,0:T(8,128)S(1)} %pad_maximum_fusion.3), channel_id=1, source_target_pairs={{0,4},{2,6},{4,0},{6,2},{1,5},{3,7},{5,1},{7,3},{8,12},{10,14},{12... | collective-permute-start | bytes 442376 | tf_op jit(solution)/shard_map/ppermute | solution.py:16
  73.9 4.9 %collective-permute-done.19 = f32[32,1152]{1,0:T(8,128)S(1)} collective-permute-done((f32[32,1152]{1,0:T(8,128)S(1)}, f32[32,1152]{1,0:T(8,128)S(1)}, u32[]{:S(2)}, u32[]{:S(2)}) %collective-permute-start.19) | collective-permute-done | bytes 147488 | tf_op jit(solution)/shard_map/ppermute | solution.py:16
  79.4 1.7 %collective-permute-start.22 = (f32[32,384]{1,0:T(8,128)S(1)}, f32[32,384]{1,0:T(8,128)S(1)}, u32[]{:S(2)}, u32[]{:S(2)}) collective-permute-start(f32[32,384]{1,0:T(8,128)S(1)} %get-tuple-element.94), channel_id=1, source_target_pairs={{0,1},{1,0},{2,3},{3,2},{4,5},{5,4},{6,7},{7,6},{8,9},{9,8},{10,11... | collective-permute-start | bytes 147464 | tf_op jit(solution)/shard_map/ppermute | solution.py:16
  81.1 2.0 %collective-permute-done.20 = f32[32,384]{1,0:T(8,128)S(1)} collective-permute-done((f32[32,384]{1,0:T(8,128)S(1)}, f32[32,384]{1,0:T(8,128)S(1)}, u32[]{:S(2)}, u32[]{:S(2)}) %collective-permute-start.20) | collective-permute-done | bytes 49184 | tf_op jit(solution)/shard_map/ppermute | solution.py:16
  83.0 0.5 collective-permute-done.21
  83.6 1.7 %collective-permute-start.23 = (f32[64,384]{1,0:T(8,128)S(1)}, f32[64,384]{1,0:T(8,128)S(1)}, u32[]{:S(2)}, u32[]{:S(2)}) collective-permute-start(f32[64,384]{1,0:T(8,128)S(1)} %pad_maximum_fusion.4), channel_id=1, source_target_pairs={{0,1},{1,0},{2,3},{3,2},{4,5},{5,4},{6,7},{7,6},{8,9},{9,8},{10,11... | collective-permute-start | bytes 294920 | tf_op jit(solution)/shard_map/ppermute | solution.py:16
  85.3 1.9 %collective-permute-start.24 = (f32[64,384]{1,0:T(8,128)S(1)}, f32[64,384]{1,0:T(8,128)S(1)}, u32[]{:S(2)}, u32[]{:S(2)}) collective-permute-start(f32[64,384]{1,0:T(8,128)S(1)} %pad_maximum_fusion.5), channel_id=1, source_target_pairs={{0,2},{2,0},{4,6},{6,4},{1,3},{3,1},{5,7},{7,5},{8,10},{10,8},{12,... | collective-permute-start | bytes 294920 | tf_op jit(solution)/shard_map/ppermute | solution.py:16
  87.2 1.5 %collective-permute-start.25 = (f32[64,384]{1,0:T(8,128)S(1)}, f32[64,384]{1,0:T(8,128)S(1)}, u32[]{:S(2)}, u32[]{:S(2)}) collective-permute-start(f32[64,384]{1,0:T(8,128)S(1)} %pad_maximum_fusion.6), channel_id=1, source_target_pairs={{0,16},{8,24},{16,0},{24,8},{1,17},{9,25},{17,1},{25,9},{2,18},{10... | collective-permute-start | bytes 294920 | tf_op jit(solution)/shard_map/ppermute | solution.py:16
  88.7 0.6 collective-permute-done.23
  89.3 1.5 %collective-permute-done.24 = f32[64,384]{1,0:T(8,128)S(1)} collective-permute-done((f32[64,384]{1,0:T(8,128)S(1)}, f32[64,384]{1,0:T(8,128)S(1)}, u32[]{:S(2)}, u32[]{:S(2)}) %collective-permute-start.24) | collective-permute-done | bytes 98336 | tf_op jit(solution)/shard_map/ppermute | solution.py:16
  90.7 1.1 collective-permute-done.25
  91.9 1.5 %collective-permute-start.26 = (f32[128,384]{1,0:T(8,128)S(1)}, f32[128,384]{1,0:T(8,128)S(1)}, u32[]{:S(2)}, u32[]{:S(2)}) collective-permute-start(f32[128,384]{1,0:T(8,128)S(1)} %pad_maximum_fusion), channel_id=1, source_target_pairs={{0,16},{8,24},{16,0},{24,8},{1,17},{9,25},{17,1},{25,9},{2,18},{10... | collective-permute-start | bytes 589832 | tf_op jit(solution)/shard_map/ppermute | solution.py:16
  93.5 0.5 collective-permute-start.27
  94.0 3.6 %collective-permute-done.26 = f32[128,384]{1,0:T(8,128)S(1)} collective-permute-done((f32[128,384]{1,0:T(8,128)S(1)}, f32[128,384]{1,0:T(8,128)S(1)}, u32[]{:S(2)}, u32[]{:S(2)}) %collective-permute-start.26) | collective-permute-done | bytes 196640 | tf_op jit(solution)/shard_map/ppermute | solution.py:16
  97.6 1.5 %collective-permute-done.27 = f32[128,384]{1,0:T(8,128)S(1)} collective-permute-done((f32[128,384]{1,0:T(8,128)S(1)}, f32[128,384]{1,0:T(8,128)S(1)}, u32[]{:S(2)}, u32[]{:S(2)}) %collective-permute-start.27) | collective-permute-done | bytes 196640 | tf_op jit(solution)/shard_map/ppermute | solution.py:16
  100.3 2.4 %collective-permute-done.30.other_ref = f32[256,1152]{1,0:T(8,128)S(1)} collective-permute-done((f32[256,1152]{1,0:T(8,128)S(1)}, f32[256,1152]{1,0:T(8,128)S(1)}, u32[]{:S(2)}, u32[]{:S(2)}) %collective-permute-start.30) | collective-permute-done | bytes 1179680 | tf_op jit(solution)/shard_map/ppermute | solution.py:16
  102.6 31.8 %shard_map.53 = (f32[256,1024]{1,0:T(8,128)}, bf16[256,1024]{1,0:T(8,128)(2,1)S(1)}) custom-call(s32[5]{0:T(128)S(1)} %stack.59.place_ref, f32[256,1152]{1,0:T(8,128)S(1)} %maximum_maximum_fusion.mine_ref, f32[256,1152]{1,0:T(8,128)S(1)} %collective-permute-done.30.other_ref, bf16[1024,1024]{1,0:T(8,128)(2,1)S(1)} %get-tuple-element.112.left), custom_call_target="tpu_custom_call" | custom-call | flops 42949672960 | bytes 16777216 | tf_op jit(solution)/shard_map/pallas_call | solution.py:376
  134.6 3.0 %shard_map.54.refs_0_ = f32[8,256,256]{2,1,0:T(8,128)} custom-call(s32[5]{0:T(128)S(1)} %stack.59.place_ref, bf16[256,1024]{1,0:T(8,128)(2,1)S(1)} %get-tuple-element.114.weights_ref, bf16[8,512,256]{2,1,0:T(8,128)(2,1)S(1)} %shard_map.50.own_ref, f32[2,512,256]{2,1,0:T(8,128)S(1)} %collective-permute-done.refs_1_.first_ref, ...), custom_call_target="tpu_custom_call" | custom-call | flops 536870912 | bytes 8388608 | tf_op jit(solution)/shard_map/pallas_call | solution.py:419
  137.6 3.0 %shard_map.55 = f32[8,256,256]{2,1,0:T(8,128)} custom-call(s32[5]{0:T(128)S(1)} %stack.59.place_ref, bf16[256,1024]{1,0:T(8,128)(2,1)S(1)} %get-tuple-element.114.weights_ref, bf16[8,512,256]{2,1,0:T(8,128)(2,1)S(1)} %shard_map.50.own_ref, f32[2,512,256]{2,1,0:T(8,128)S(1)} %collective-permute-done.29.first_ref, ...), custom_call_target="tpu_custom_call", output_to_operand_aliasing={{}: (5, {})} | custom-call | flops 536870912 | bytes 8388608 | tf_op jit(solution)/shard_map/pallas_call | solution.py:419
  (59 shorter events, 4.3 us)
Async XLA Ops:
  1.6 15.8 %collective-permute-start.1 = (f32[256,512]{1,0:T(8,128)S(1)}, f32[256,512]{1,0:T(8,128)S(1)}, u32[]{:S(2)}, u32[]{:S(2)}) collective-permute-start(f32[256,512]{1,0:T(8,128)S(1)} %convert_element_type.3.refs_2_), channel_id=1, source_target_pairs={{0,1},{1,0},{2,3},{3,2},{4,5},{5,4},{6,7},{7,6},{8,9},{9,8},{10,11... | collective-permute-start | bytes 1572872 | tf_op jit(solution)/shard_map/ppermute | solution.py:16
  4.7 15.3 %collective-permute-start.4 = (f32[256,512]{1,0:T(8,128)S(1)}, f32[256,512]{1,0:T(8,128)}, u32[]{:S(2)}, u32[]{:S(2)}) collective-permute-start(f32[256,512]{1,0:T(8,128)S(1)} %convert_element_type.3.refs_2_), channel_id=1, source_target_pairs={{0,16},{8,24},{16,0},{24,8},{1,17},{9,25},{17,1},{25,9},{2,18},{10... | collective-permute-start | bytes 1572872 | tf_op jit(solution)/shard_map/ppermute | solution.py:16
  6.2 2.2 %copy-start = (bf16[512,16,256]{2,1,0:T(8,128)(2,1)S(1)}, bf16[512,16,256]{2,1,0:T(8,128)(2,1)}, u32[]{:S(2)}) copy-start(bf16[512,16,256]{2,1,0:T(8,128)(2,1)} %param.4) | copy-start | bytes 12582916
  8.4 0.7 copy-start.2
  9.1 21.0 %copy-start.3 = (f32[16,16]{1,0:T(8,128)S(1)}, f32[16,16]{1,0:T(8,128)}, u32[]{:S(2)}) copy-start(f32[16,16]{1,0:T(8,128)} %double_ref.3) | copy-start | bytes 3076
  12.2 26.9 %collective-permute-start = (f32[2,512,256]{2,1,0:T(8,128)S(1)}, f32[2,512,256]{2,1,0:T(8,128)S(1)}, u32[]{:S(2)}, u32[]{:S(2)}) collective-permute-start(f32[2,512,256]{2,1,0:T(8,128)S(1)} %shard_map.51), channel_id=1, source_target_pairs={{0,1},{1,0},{2,3},{3,2},{4,5},{5,4},{6,7},{7,6},{8,9},{9,8},{10,11... | collective-permute-start | bytes 3145736 | tf_op jit(solution)/shard_map/ppermute | solution.py:16
  17.4 12.5 %collective-permute-start.5 = (f32[256,512]{1,0:T(8,128)S(1)}, f32[256,512]{1,0:T(8,128)}, u32[]{:S(2)}, u32[]{:S(2)}) collective-permute-start(f32[256,512]{1,0:T(8,128)S(1)} %collective-permute-done.1.refs_3_), channel_id=1, source_target_pairs={{0,16},{8,24},{16,0},{24,8},{1,17},{9,25},{17,1},{25,9},{2,18},{10... | collective-permute-start | bytes 1572872 | tf_op jit(solution)/shard_map/ppermute | solution.py:16
  19.5 17.3 %collective-permute-start.2 = (f32[256,512]{1,0:T(8,128)S(1)}, f32[256,512]{1,0:T(8,128)}, u32[]{:S(2)}, u32[]{:S(2)}) collective-permute-start(f32[256,512]{1,0:T(8,128)S(1)} %convert_element_type.3.refs_2_), channel_id=1, source_target_pairs={{0,8},{8,0},{16,24},{24,16},{1,9},{9,1},{17,25},{25,17},{2,10},{10... | collective-permute-start | bytes 1572872 | tf_op jit(solution)/shard_map/ppermute | solution.py:16
  19.5 19.6 %collective-permute-start.3 = (f32[256,512]{1,0:T(8,128)S(1)}, f32[256,512]{1,0:T(8,128)}, u32[]{:S(2)}, u32[]{:S(2)}) collective-permute-start(f32[256,512]{1,0:T(8,128)S(1)} %collective-permute-done.1.refs_3_), channel_id=1, source_target_pairs={{0,8},{8,0},{16,24},{24,16},{1,9},{9,1},{17,25},{25,17},{2,10},{10... | collective-permute-start | bytes 1572872 | tf_op jit(solution)/shard_map/ppermute | solution.py:16
  20.0 19.1 %collective-permute-start.6 = (f32[256,512]{1,0:T(8,128)}, f32[256,512]{1,0:T(8,128)}, u32[]{:S(2)}, u32[]{:S(2)}) collective-permute-start(f32[256,512]{1,0:T(8,128)} %collective-permute-done.4.refs_6_), channel_id=1, source_target_pairs={{0,8},{8,0},{16,24},{24,16},{1,9},{9,1},{17,25},{25,17},{2,10},{10... | collective-permute-start | bytes 1572872 | tf_op jit(solution)/shard_map/ppermute | solution.py:16
  29.9 9.2 %collective-permute-start.7 = (f32[256,512]{1,0:T(8,128)}, f32[256,512]{1,0:T(8,128)}, u32[]{:S(2)}, u32[]{:S(2)}) collective-permute-start(f32[256,512]{1,0:T(8,128)} %collective-permute-done.5.refs_7_), channel_id=1, source_target_pairs={{0,8},{8,0},{16,24},{24,16},{1,9},{9,1},{17,25},{25,17},{2,10},{10... | collective-permute-start | bytes 1572872 | tf_op jit(solution)/shard_map/ppermute | solution.py:16
  30.1 2.2 %copy-start.1 = (bf16[512,16,256]{2,1,0:T(8,128)(2,1)S(1)}, bf16[512,16,256]{2,1,0:T(8,128)(2,1)}, u32[]{:S(2)}) copy-start(bf16[512,16,256]{2,1,0:T(8,128)(2,1)} %param.4) | copy-start | bytes 12582916
  45.3 2.9 %collective-permute-start.8 = (f32[256,1152]{1,0:T(8,128)S(1)}, f32[256,1152]{1,0:T(8,128)S(1)}, u32[]{:S(2)}, u32[]{:S(2)}) collective-permute-start(f32[256,1152]{1,0:T(8,128)S(1)} %get-tuple-element.70), channel_id=1, source_target_pairs={{0,8},{8,0},{16,24},{24,16},{1,9},{9,1},{17,25},{25,17},{2,10},{10... | collective-permute-start | bytes 3538952 | tf_op jit(solution)/shard_map/ppermute | solution.py:16
  48.3 7.0 %collective-permute-start.10 = (f32[128,384]{1,0:T(8,128)S(1)}, f32[128,384]{1,0:T(8,128)S(1)}, u32[]{:S(2)}, u32[]{:S(2)}) collective-permute-start(f32[128,384]{1,0:T(8,128)S(1)} %get-tuple-element.72), channel_id=1, source_target_pairs={{0,1},{1,0},{2,3},{3,2},{4,5},{5,4},{6,7},{7,6},{8,9},{9,8},{10,11... | collective-permute-start | bytes 589832 | tf_op jit(solution)/shard_map/ppermute | solution.py:16
  50.2 6.7 %collective-permute-start.11 = (f32[128,384]{1,0:T(8,128)S(1)}, f32[128,384]{1,0:T(8,128)S(1)}, u32[]{:S(2)}, u32[]{:S(2)}) collective-permute-start(f32[128,384]{1,0:T(8,128)S(1)} %get-tuple-element.73), channel_id=1, source_target_pairs={{0,2},{2,0},{4,6},{6,4},{1,3},{3,1},{5,7},{7,5},{8,10},{10,8},{12,... | collective-permute-start | bytes 589832 | tf_op jit(solution)/shard_map/ppermute | solution.py:16
  51.7 6.4 %collective-permute-start.9 = (f32[128,384]{1,0:T(8,128)S(1)}, f32[128,384]{1,0:T(8,128)S(1)}, u32[]{:S(2)}, u32[]{:S(2)}) collective-permute-start(f32[128,384]{1,0:T(8,128)S(1)} %get-tuple-element.71), channel_id=1, source_target_pairs={{0,16},{8,24},{16,0},{24,8},{1,17},{9,25},{17,1},{25,9},{2,18},{10... | collective-permute-start | bytes 589832 | tf_op jit(solution)/shard_map/ppermute | solution.py:16
  58.2 4.7 %collective-permute-start.12 = (f32[64,384]{1,0:T(8,128)S(1)}, f32[64,384]{1,0:T(8,128)S(1)}, u32[]{:S(2)}, u32[]{:S(2)}) collective-permute-start(f32[64,384]{1,0:T(8,128)S(1)} %slice.98), channel_id=1, source_target_pairs={{0,1},{1,0},{2,3},{3,2},{4,5},{5,4},{6,7},{7,6},{8,9},{9,8},{10,11... | collective-permute-start | bytes 294920 | tf_op jit(solution)/shard_map/ppermute | solution.py:16
  58.8 4.6 %collective-permute-start.13 = (f32[64,384]{1,0:T(8,128)S(1)}, f32[64,384]{1,0:T(8,128)S(1)}, u32[]{:S(2)}, u32[]{:S(2)}) collective-permute-start(f32[64,384]{1,0:T(8,128)S(1)} %slice.100), channel_id=1, source_target_pairs={{0,2},{2,0},{4,6},{6,4},{1,3},{3,1},{5,7},{7,5},{8,10},{10,8},{12,... | collective-permute-start | bytes 294920 | tf_op jit(solution)/shard_map/ppermute | solution.py:16
  59.1 4.6 %collective-permute-start.14 = (f32[64,384]{1,0:T(8,128)S(1)}, f32[64,384]{1,0:T(8,128)S(1)}, u32[]{:S(2)}, u32[]{:S(2)}) collective-permute-start(f32[64,384]{1,0:T(8,128)S(1)} %slice.102), channel_id=1, source_target_pairs={{0,16},{8,24},{16,0},{24,8},{1,17},{9,25},{17,1},{25,9},{2,18},{10... | collective-permute-start | bytes 294920 | tf_op jit(solution)/shard_map/ppermute | solution.py:16
  60.7 10.5 %collective-permute-start.18 = (f32[2,512,256]{2,1,0:T(8,128)S(1)}, f32[2,512,256]{2,1,0:T(8,128)S(1)}, u32[]{:S(2)}, u32[]{:S(2)}) collective-permute-start(f32[2,512,256]{2,1,0:T(8,128)S(1)} %collective-permute-done.refs_1_.first_ref), channel_id=1, source_target_pairs={{0,8},{8,0},{16,24},{24,16},{1,9},{9,1},{17,25},{25,17},{2,10},{10... | collective-permute-start | bytes 3145736 | tf_op jit(solution)/shard_map/ppermute | solution.py:16
  63.8 4.8 %collective-permute-start.15 = (f32[32,384]{1,0:T(8,128)S(1)}, f32[32,384]{1,0:T(8,128)S(1)}, u32[]{:S(2)}, u32[]{:S(2)}) collective-permute-start(f32[32,384]{1,0:T(8,128)S(1)} %slice.104), channel_id=1, source_target_pairs={{0,2},{2,0},{4,6},{6,4},{1,3},{3,1},{5,7},{7,5},{8,10},{10,8},{12,... | collective-permute-start | bytes 147464 | tf_op jit(solution)/shard_map/ppermute | solution.py:16
  65.6 4.1 %collective-permute-start.16 = (f32[32,384]{1,0:T(8,128)S(1)}, f32[32,384]{1,0:T(8,128)S(1)}, u32[]{:S(2)}, u32[]{:S(2)}) collective-permute-start(f32[32,384]{1,0:T(8,128)S(1)} %slice.106), channel_id=1, source_target_pairs={{0,16},{8,24},{16,0},{24,8},{1,17},{9,25},{17,1},{25,9},{2,18},{10... | collective-permute-start | bytes 147464 | tf_op jit(solution)/shard_map/ppermute | solution.py:16
  67.1 4.1 %collective-permute-start.17 = (f32[32,384]{1,0:T(8,128)S(1)}, f32[32,384]{1,0:T(8,128)S(1)}, u32[]{:S(2)}, u32[]{:S(2)}) collective-permute-start(f32[32,384]{1,0:T(8,128)S(1)} %slice.108), channel_id=1, source_target_pairs={{0,1},{1,0},{2,3},{3,2},{4,5},{5,4},{6,7},{7,6},{8,9},{9,8},{10,11... | collective-permute-start | bytes 147464 | tf_op jit(solution)/shard_map/ppermute | solution.py:16
  71.3 7.6 %collective-permute-start.19 = (f32[32,1152]{1,0:T(8,128)S(1)}, f32[32,1152]{1,0:T(8,128)S(1)}, u32[]{:S(2)}, u32[]{:S(2)}) collective-permute-start(f32[32,1152]{1,0:T(8,128)S(1)} %pad_maximum_fusion.3), channel_id=1, source_target_pairs={{0,4},{2,6},{4,0},{6,2},{1,5},{3,7},{5,1},{7,3},{8,12},{10,14},{12... | collective-permute-start | bytes 442376 | tf_op jit(solution)/shard_map/ppermute | solution.py:16
  78.9 4.2 %collective-permute-start.20 = (f32[32,384]{1,0:T(8,128)S(1)}, f32[32,384]{1,0:T(8,128)S(1)}, u32[]{:S(2)}, u32[]{:S(2)}) collective-permute-start(f32[32,384]{1,0:T(8,128)S(1)} %get-tuple-element.92), channel_id=1, source_target_pairs={{0,2},{2,0},{4,6},{6,4},{1,3},{3,1},{5,7},{7,5},{8,10},{10,8},{12,... | collective-permute-start | bytes 147464 | tf_op jit(solution)/shard_map/ppermute | solution.py:16
  79.0 4.6 %collective-permute-start.21 = (f32[32,384]{1,0:T(8,128)S(1)}, f32[32,384]{1,0:T(8,128)S(1)}, u32[]{:S(2)}, u32[]{:S(2)}) collective-permute-start(f32[32,384]{1,0:T(8,128)S(1)} %get-tuple-element.93), channel_id=1, source_target_pairs={{0,16},{8,24},{16,0},{24,8},{1,17},{9,25},{17,1},{25,9},{2,18},{10... | collective-permute-start | bytes 147464 | tf_op jit(solution)/shard_map/ppermute | solution.py:16
  79.4 4.2 %collective-permute-start.22 = (f32[32,384]{1,0:T(8,128)S(1)}, f32[32,384]{1,0:T(8,128)S(1)}, u32[]{:S(2)}, u32[]{:S(2)}) collective-permute-start(f32[32,384]{1,0:T(8,128)S(1)} %get-tuple-element.94), channel_id=1, source_target_pairs={{0,1},{1,0},{2,3},{3,2},{4,5},{5,4},{6,7},{7,6},{8,9},{9,8},{10,11... | collective-permute-start | bytes 147464 | tf_op jit(solution)/shard_map/ppermute | solution.py:16
  83.6 5.6 %collective-permute-start.23 = (f32[64,384]{1,0:T(8,128)S(1)}, f32[64,384]{1,0:T(8,128)S(1)}, u32[]{:S(2)}, u32[]{:S(2)}) collective-permute-start(f32[64,384]{1,0:T(8,128)S(1)} %pad_maximum_fusion.4), channel_id=1, source_target_pairs={{0,1},{1,0},{2,3},{3,2},{4,5},{5,4},{6,7},{7,6},{8,9},{9,8},{10,11... | collective-permute-start | bytes 294920 | tf_op jit(solution)/shard_map/ppermute | solution.py:16
  85.3 5.5 %collective-permute-start.24 = (f32[64,384]{1,0:T(8,128)S(1)}, f32[64,384]{1,0:T(8,128)S(1)}, u32[]{:S(2)}, u32[]{:S(2)}) collective-permute-start(f32[64,384]{1,0:T(8,128)S(1)} %pad_maximum_fusion.5), channel_id=1, source_target_pairs={{0,2},{2,0},{4,6},{6,4},{1,3},{3,1},{5,7},{7,5},{8,10},{10,8},{12,... | collective-permute-start | bytes 294920 | tf_op jit(solution)/shard_map/ppermute | solution.py:16
  87.2 4.6 %collective-permute-start.25 = (f32[64,384]{1,0:T(8,128)S(1)}, f32[64,384]{1,0:T(8,128)S(1)}, u32[]{:S(2)}, u32[]{:S(2)}) collective-permute-start(f32[64,384]{1,0:T(8,128)S(1)} %pad_maximum_fusion.6), channel_id=1, source_target_pairs={{0,16},{8,24},{16,0},{24,8},{1,17},{9,25},{17,1},{25,9},{2,18},{10... | collective-permute-start | bytes 294920 | tf_op jit(solution)/shard_map/ppermute | solution.py:16
  91.9 5.7 %collective-permute-start.26 = (f32[128,384]{1,0:T(8,128)S(1)}, f32[128,384]{1,0:T(8,128)S(1)}, u32[]{:S(2)}, u32[]{:S(2)}) collective-permute-start(f32[128,384]{1,0:T(8,128)S(1)} %pad_maximum_fusion), channel_id=1, source_target_pairs={{0,16},{8,24},{16,0},{24,8},{1,17},{9,25},{17,1},{25,9},{2,18},{10... | collective-permute-start | bytes 589832 | tf_op jit(solution)/shard_map/ppermute | solution.py:16
  93.5 5.7 %collective-permute-start.27 = (f32[128,384]{1,0:T(8,128)S(1)}, f32[128,384]{1,0:T(8,128)S(1)}, u32[]{:S(2)}, u32[]{:S(2)}) collective-permute-start(f32[128,384]{1,0:T(8,128)S(1)} %pad_maximum_fusion.1), channel_id=1, source_target_pairs={{0,1},{1,0},{2,3},{3,2},{4,5},{5,4},{6,7},{7,6},{8,9},{9,8},{10,11... | collective-permute-start | bytes 589832 | tf_op jit(solution)/shard_map/ppermute | solution.py:16
  94.0 5.7 %collective-permute-start.28 = (f32[128,384]{1,0:T(8,128)S(1)}, f32[128,384]{1,0:T(8,128)S(1)}, u32[]{:S(2)}, u32[]{:S(2)}) collective-permute-start(f32[128,384]{1,0:T(8,128)S(1)} %pad_maximum_fusion.2), channel_id=1, source_target_pairs={{0,2},{2,0},{4,6},{6,4},{1,3},{3,1},{5,7},{7,5},{8,10},{10,8},{12,... | collective-permute-start | bytes 589832 | tf_op jit(solution)/shard_map/ppermute | solution.py:16
  99.7 2.9 %collective-permute-start.30 = (f32[256,1152]{1,0:T(8,128)S(1)}, f32[256,1152]{1,0:T(8,128)S(1)}, u32[]{:S(2)}, u32[]{:S(2)}) collective-permute-start(f32[256,1152]{1,0:T(8,128)S(1)} %maximum_maximum_fusion.mine_ref), channel_id=1, source_target_pairs={{0,8},{8,0},{16,24},{24,16},{1,9},{9,1},{17,25},{25,17},{2,10},{10... | collective-permute-start | bytes 3538952 | tf_op jit(solution)/shard_map/ppermute | solution.py:16
  99.8 34.7 %collective-permute-start.29 = (f32[2,512,256]{2,1,0:T(8,128)S(1)}, f32[2,512,256]{2,1,0:T(8,128)S(1)}, u32[]{:S(2)}, u32[]{:S(2)}) collective-permute-start(f32[2,512,256]{2,1,0:T(8,128)S(1)} %collective-permute-done.refs_1_.first_ref), channel_id=1, source_target_pairs={{0,16},{8,24},{16,0},{24,8},{1,17},{9,25},{17,1},{25,9},{2,18},{10... | collective-permute-start | bytes 3145736 | tf_op jit(solution)/shard_map/ppermute | solution.py:16
  134.5 3.2 %collective-permute-start.31 = (f32[2,512,256]{2,1,0:T(8,128)S(1)}, f32[2,512,256]{2,1,0:T(8,128)S(1)}, u32[]{:S(2)}, u32[]{:S(2)}) collective-permute-start(f32[2,512,256]{2,1,0:T(8,128)S(1)} %collective-permute-done.29.first_ref), channel_id=1, source_target_pairs={{0,8},{8,0},{16,24},{24,16},{1,9},{9,1},{17,25},{25,17},{2,10},{10... | collective-permute-start | bytes 3145736 | tf_op jit(solution)/shard_map/ppermute | solution.py:16

commit v4 on v3

--- a/solution.py
+++ b/solution.py
@@ -178,7 +178,7 @@
         in_specs=[pl.BlockSpec(memory_space=pltpu.SMEM)] + [whole] * (len(blocks) + len(left_blocks)),
         out_specs=[whole, whole, whole],
         scratch_shapes=[pltpu.VMEM((chi, count * right), jnp.bfloat16)] * 3 + [pltpu.VMEM((rows, width), jnp.float32)],
-        compiler_params=pltpu.CompilerParams(vmem_limit_bytes=40 * 2**20),
+        compiler_params=pltpu.CompilerParams(vmem_limit_bytes=26 * 2**20),
         cost_estimate=pl.CostEstimate(
             flops=5 * chi * chi * count * right, bytes_accessed=12 * chi * chi, transcendentals=0
         ),

time: 141 us -> 141 us (level)
  no operation moved by 1% of the time
where the time goes in v4:
time: 141 us; the launch traced here: 140 us
  Pallas kernels  51.4 us (36%)
  waiting for transfers between devices  48.7 us (35%)
  starting transfers between devices  32.7 us (23%)
  local copies, waits for them, and re-layouts  5.38 us (4%)
  other arithmetic  1.5 us (1%)
    ppermute x32, waiting for transfers between devices, swap(): return lax.ppermute(array, axis, [(i, i ^ distance) for i in range(size)])  48.7 us
    ppermute x32, starting transfers between devices, swap(): return lax.ppermute(array, axis, [(i, i ^ distance) for i in range(size)])  32.7 us
    pallas_call x1, Pallas kernels, factorize(): pl.pallas_call(functools.partial(factor_kernel, scale, chunk), out_shape=...  31.7 us
    pallas_call x2, Pallas kernels, absorb(): pl.pallas_call(functools.partial(absorb_kernel, east_parts), grid=(tiles,...  7.48 us
    pallas_call x1, Pallas kernels, gram_of_columns(): pl.pallas_call(functools.partial(gram_kernel, chi, chunk, width // 3, len...  6.13 us
    pallas_call x2, Pallas kernels, make_site(): pl.pallas_call(functools.partial(site_kernel, scale), out_shape=jax.Shape...  6.01 us
    unnamed x8, local copies, waits for them, and re-layouts  5.08 us
  transfers between devices with their start and end apart: 32, of which 22 were waited for; matrix products, arithmetic and copies ran while one was open for 0% of the time, Pallas kernels for 30%

profile of v4, /device:TPU:0, one launch (start us, length us, event | category | flops | bytes accessed | tf_op | source)
XLA Modules:
  0.0 140.5 jit_solution(7439006137292117512)
XLA Ops:
  0.6 1.0 convert_element_type.3.refs_2_
  1.6 3.0 %collective-permute-start.1 = (f32[256,512]{1,0:T(8,128)S(1)}, f32[256,512]{1,0:T(8,128)S(1)}, u32[]{:S(2)}, u32[]{:S(2)}) collective-permute-start(f32[256,512]{1,0:T(8,128)S(1)} %convert_element_type.3.refs_2_), channel_id=1, source_target_pairs={{0,1},{1,0},{2,3},{3,2},{4,5},{5,4},{6,7},{7,6},{8,9},{9,8},{10,11... | collective-permute-start | bytes 1572872 | tf_op jit(solution)/shard_map/ppermute | solution.py:16
  4.7 1.5 %collective-permute-start.4 = (f32[256,512]{1,0:T(8,128)S(1)}, f32[256,512]{1,0:T(8,128)}, u32[]{:S(2)}, u32[]{:S(2)}) collective-permute-start(f32[256,512]{1,0:T(8,128)S(1)} %convert_element_type.3.refs_2_), channel_id=1, source_target_pairs={{0,16},{8,24},{16,0},{24,8},{1,17},{9,25},{17,1},{25,9},{2,18},{10... | collective-permute-start | bytes 1572872 | tf_op jit(solution)/shard_map/ppermute | solution.py:16
  6.2 2.2 %copy-done = bf16[512,16,256]{2,1,0:T(8,128)(2,1)S(1)} copy-done((bf16[512,16,256]{2,1,0:T(8,128)(2,1)S(1)}, bf16[512,16,256]{2,1,0:T(8,128)(2,1)}, u32[]{:S(2)}) %copy-start) | copy-done | bytes 4194328
  8.4 0.7 copy-done.2
  9.1 3.0 %shard_map.51 = f32[2,512,256]{2,1,0:T(8,128)S(1)} custom-call(s32[2]{0:T(128)S(1)} %pad_add_fusion.legs_ref, bf16[8192,256]{1,0:T(8,128)(2,1)S(1)} %bitcast.16, f32[16,16]{1,0:T(8,128)S(1)} %copy-done.2), custom_call_target="tpu_custom_call" | custom-call | flops 268435456 | bytes 16777216 | tf_op jit(solution)/shard_map/pallas_call | solution.py:118
  12.2 0.6 collective-permute-start
  12.7 4.7 %collective-permute-done.1.refs_3_ = f32[256,512]{1,0:T(8,128)S(1)} collective-permute-done((f32[256,512]{1,0:T(8,128)S(1)}, f32[256,512]{1,0:T(8,128)S(1)}, u32[]{:S(2)}, u32[]{:S(2)}) %collective-permute-start.1) | collective-permute-done | bytes 524320 | tf_op jit(solution)/shard_map/ppermute | solution.py:16
  17.4 2.0 %collective-permute-start.5 = (f32[256,512]{1,0:T(8,128)S(1)}, f32[256,512]{1,0:T(8,128)}, u32[]{:S(2)}, u32[]{:S(2)}) collective-permute-start(f32[256,512]{1,0:T(8,128)S(1)} %collective-permute-done.1.refs_3_), channel_id=1, source_target_pairs={{0,16},{8,24},{16,0},{24,8},{1,17},{9,25},{17,1},{25,9},{2,18},{10... | collective-permute-start | bytes 1572872 | tf_op jit(solution)/shard_map/ppermute | solution.py:16
  19.5 0.5 collective-permute-start.3
  20.0 9.9 %collective-permute-done.5.refs_7_ = f32[256,512]{1,0:T(8,128)} collective-permute-done((f32[256,512]{1,0:T(8,128)S(1)}, f32[256,512]{1,0:T(8,128)}, u32[]{:S(2)}, u32[]{:S(2)}) %collective-permute-start.5) | collective-permute-done | bytes 524320 | tf_op jit(solution)/shard_map/ppermute | solution.py:16
  30.1 2.2 %copy-done.1 = bf16[512,16,256]{2,1,0:T(8,128)(2,1)S(1)} copy-done((bf16[512,16,256]{2,1,0:T(8,128)(2,1)S(1)}, bf16[512,16,256]{2,1,0:T(8,128)(2,1)}, u32[]{:S(2)}) %copy-start.1) | copy-done | bytes 4194328
  32.3 4.4 %shard_map.50.own_ref = bf16[8,512,256]{2,1,0:T(8,128)(2,1)S(1)} custom-call(s32[8]{0:T(128)S(1)} %stack.68.legs_ref, bf16[8192,256]{1,0:T(8,128)(2,1)S(1)} %bitcast.17, f32[16,16]{1,0:T(8,128)S(1)} %copy-done.3), custom_call_target="tpu_custom_call" | custom-call | flops 1073741824 | bytes 16777216 | tf_op jit(solution)/shard_map/pallas_call | solution.py:118
  36.8 2.3 %collective-permute-done.refs_1_.first_ref = f32[2,512,256]{2,1,0:T(8,128)S(1)} collective-permute-done((f32[2,512,256]{2,1,0:T(8,128)S(1)}, f32[2,512,256]{2,1,0:T(8,128)S(1)}, u32[]{:S(2)}, u32[]{:S(2)}) %collective-permute-start) | collective-permute-done | bytes 1048608 | tf_op jit(solution)/shard_map/ppermute | solution.py:16
  39.1 6.1 %shard_map.52 = (f32[256,1152]{1,0:T(8,128)S(1)}, f32[256,1152]{1,0:T(8,128)S(1)}, bf16[1024,1024]{1,0:T(8,128)(2,1)S(1)}) custom-call(s32[5]{0:T(128)S(1)} %stack.59.place_ref, bf16[2,512,256]{2,1,0:T(8,128)(2,1)S(1)} %constant_dynamic-slice_fusion.refs_0_, f32[2,512,256]{2,1,0:T(8,128)S(1)} %collective-permute-done.refs_1_.first_ref, ...), custom_call_target="tpu_custom_call" | custom-call | flops 2684354560 | bytes 12582912 | tf_op jit(solution)/shard_map/pallas_call | solution.py:174
  45.3 2.8 %collective-permute-done.8 = f32[256,1152]{1,0:T(8,128)S(1)} collective-permute-done((f32[256,1152]{1,0:T(8,128)S(1)}, f32[256,1152]{1,0:T(8,128)S(1)}, u32[]{:S(2)}, u32[]{:S(2)}) %collective-permute-start.8) | collective-permute-done | bytes 1179680 | tf_op jit(solution)/shard_map/ppermute | solution.py:16
  48.3 1.8 %collective-permute-start.10 = (f32[128,384]{1,0:T(8,128)S(1)}, f32[128,384]{1,0:T(8,128)S(1)}, u32[]{:S(2)}, u32[]{:S(2)}) collective-permute-start(f32[128,384]{1,0:T(8,128)S(1)} %get-tuple-element.72), channel_id=1, source_target_pairs={{0,1},{1,0},{2,3},{3,2},{4,5},{5,4},{6,7},{7,6},{8,9},{9,8},{10,11... | collective-permute-start | bytes 589832 | tf_op jit(solution)/shard_map/ppermute | solution.py:16
  50.1 1.6 %collective-permute-start.11 = (f32[128,384]{1,0:T(8,128)S(1)}, f32[128,384]{1,0:T(8,128)S(1)}, u32[]{:S(2)}, u32[]{:S(2)}) collective-permute-start(f32[128,384]{1,0:T(8,128)S(1)} %get-tuple-element.73), channel_id=1, source_target_pairs={{0,2},{2,0},{4,6},{6,4},{1,3},{3,1},{5,7},{7,5},{8,10},{10,8},{12,... | collective-permute-start | bytes 589832 | tf_op jit(solution)/shard_map/ppermute | solution.py:16
  51.7 1.5 %collective-permute-start.9 = (f32[128,384]{1,0:T(8,128)S(1)}, f32[128,384]{1,0:T(8,128)S(1)}, u32[]{:S(2)}, u32[]{:S(2)}) collective-permute-start(f32[128,384]{1,0:T(8,128)S(1)} %get-tuple-element.71), channel_id=1, source_target_pairs={{0,16},{8,24},{16,0},{24,8},{1,17},{9,25},{17,1},{25,9},{2,18},{10... | collective-permute-start | bytes 589832 | tf_op jit(solution)/shard_map/ppermute | solution.py:16
  53.2 2.1 %collective-permute-done.10 = f32[128,384]{1,0:T(8,128)S(1)} collective-permute-done((f32[128,384]{1,0:T(8,128)S(1)}, f32[128,384]{1,0:T(8,128)S(1)}, u32[]{:S(2)}, u32[]{:S(2)}) %collective-permute-start.10) | collective-permute-done | bytes 196640 | tf_op jit(solution)/shard_map/ppermute | solution.py:16
  55.3 1.5 %collective-permute-done.11 = f32[128,384]{1,0:T(8,128)S(1)} collective-permute-done((f32[128,384]{1,0:T(8,128)S(1)}, f32[128,384]{1,0:T(8,128)S(1)}, u32[]{:S(2)}, u32[]{:S(2)}) %collective-permute-start.11) | collective-permute-done | bytes 196640 | tf_op jit(solution)/shard_map/ppermute | solution.py:16
  56.8 1.3 collective-permute-done.9
  58.2 0.6 collective-permute-start.12
  59.1 1.6 %collective-permute-start.14 = (f32[64,384]{1,0:T(8,128)S(1)}, f32[64,384]{1,0:T(8,128)S(1)}, u32[]{:S(2)}, u32[]{:S(2)}) collective-permute-start(f32[64,384]{1,0:T(8,128)S(1)} %slice.102), channel_id=1, source_target_pairs={{0,16},{8,24},{16,0},{24,8},{1,17},{9,25},{17,1},{25,9},{2,18},{10... | collective-permute-start | bytes 294920 | tf_op jit(solution)/shard_map/ppermute | solution.py:16
  60.7 2.2 %collective-permute-done.12 = f32[64,384]{1,0:T(8,128)S(1)} collective-permute-done((f32[64,384]{1,0:T(8,128)S(1)}, f32[64,384]{1,0:T(8,128)S(1)}, u32[]{:S(2)}, u32[]{:S(2)}) %collective-permute-start.12) | collective-permute-done | bytes 98336 | tf_op jit(solution)/shard_map/ppermute | solution.py:16
  63.8 1.8 %collective-permute-start.15 = (f32[32,384]{1,0:T(8,128)S(1)}, f32[32,384]{1,0:T(8,128)S(1)}, u32[]{:S(2)}, u32[]{:S(2)}) collective-permute-start(f32[32,384]{1,0:T(8,128)S(1)} %slice.104), channel_id=1, source_target_pairs={{0,2},{2,0},{4,6},{6,4},{1,3},{3,1},{5,7},{7,5},{8,10},{10,8},{12,... | collective-permute-start | bytes 147464 | tf_op jit(solution)/shard_map/ppermute | solution.py:16
  65.5 1.5 %collective-permute-start.16 = (f32[32,384]{1,0:T(8,128)S(1)}, f32[32,384]{1,0:T(8,128)S(1)}, u32[]{:S(2)}, u32[]{:S(2)}) collective-permute-start(f32[32,384]{1,0:T(8,128)S(1)} %slice.106), channel_id=1, source_target_pairs={{0,16},{8,24},{16,0},{24,8},{1,17},{9,25},{17,1},{25,9},{2,18},{10... | collective-permute-start | bytes 147464 | tf_op jit(solution)/shard_map/ppermute | solution.py:16
  67.0 1.5 %collective-permute-start.17 = (f32[32,384]{1,0:T(8,128)S(1)}, f32[32,384]{1,0:T(8,128)S(1)}, u32[]{:S(2)}, u32[]{:S(2)}) collective-permute-start(f32[32,384]{1,0:T(8,128)S(1)} %slice.108), channel_id=1, source_target_pairs={{0,1},{1,0},{2,3},{3,2},{4,5},{5,4},{6,7},{7,6},{8,9},{9,8},{10,11... | collective-permute-start | bytes 147464 | tf_op jit(solution)/shard_map/ppermute | solution.py:16
  68.6 1.1 collective-permute-done.16
  69.6 1.5 %collective-permute-done.17 = f32[32,384]{1,0:T(8,128)S(1)} collective-permute-done((f32[32,384]{1,0:T(8,128)S(1)}, f32[32,384]{1,0:T(8,128)S(1)}, u32[]{:S(2)}, u32[]{:S(2)}) %collective-permute-start.17) | collective-permute-done | bytes 49184 | tf_op jit(solution)/shard_map/ppermute | solution.py:16
  71.2 2.7 %collective-permute-start.19 = (f32[32,1152]{1,0:T(8,128)S(1)}, f32[32,1152]{1,0:T(8,128)S(1)}, u32[]{:S(2)}, u32[]{:S(2)}) collective-permute-start(f32[32,1152]{1,0:T(8,128)S(1)} %pad_maximum_fusion.3), channel_id=1, source_target_pairs={{0,4},{2,6},{4,0},{6,2},{1,5},{3,7},{5,1},{7,3},{8,12},{10,14},{12... | collective-permute-start | bytes 442376 | tf_op jit(solution)/shard_map/ppermute | solution.py:16
  73.9 4.9 %collective-permute-done.19 = f32[32,1152]{1,0:T(8,128)S(1)} collective-permute-done((f32[32,1152]{1,0:T(8,128)S(1)}, f32[32,1152]{1,0:T(8,128)S(1)}, u32[]{:S(2)}, u32[]{:S(2)}) %collective-permute-start.19) | collective-permute-done | bytes 147488 | tf_op jit(solution)/shard_map/ppermute | solution.py:16
  79.4 1.7 %collective-permute-start.22 = (f32[32,384]{1,0:T(8,128)S(1)}, f32[32,384]{1,0:T(8,128)S(1)}, u32[]{:S(2)}, u32[]{:S(2)}) collective-permute-start(f32[32,384]{1,0:T(8,128)S(1)} %get-tuple-element.94), channel_id=1, source_target_pairs={{0,1},{1,0},{2,3},{3,2},{4,5},{5,4},{6,7},{7,6},{8,9},{9,8},{10,11... | collective-permute-start | bytes 147464 | tf_op jit(solution)/shard_map/ppermute | solution.py:16
  81.0 2.0 %collective-permute-done.20 = f32[32,384]{1,0:T(8,128)S(1)} collective-permute-done((f32[32,384]{1,0:T(8,128)S(1)}, f32[32,384]{1,0:T(8,128)S(1)}, u32[]{:S(2)}, u32[]{:S(2)}) %collective-permute-start.20) | collective-permute-done | bytes 49184 | tf_op jit(solution)/shard_map/ppermute | solution.py:16
  83.0 0.5 collective-permute-done.21
  83.6 1.7 %collective-permute-start.23 = (f32[64,384]{1,0:T(8,128)S(1)}, f32[64,384]{1,0:T(8,128)S(1)}, u32[]{:S(2)}, u32[]{:S(2)}) collective-permute-start(f32[64,384]{1,0:T(8,128)S(1)} %pad_maximum_fusion.4), channel_id=1, source_target_pairs={{0,1},{1,0},{2,3},{3,2},{4,5},{5,4},{6,7},{7,6},{8,9},{9,8},{10,11... | collective-permute-start | bytes 294920 | tf_op jit(solution)/shard_map/ppermute | solution.py:16
  85.2 1.9 %collective-permute-start.24 = (f32[64,384]{1,0:T(8,128)S(1)}, f32[64,384]{1,0:T(8,128)S(1)}, u32[]{:S(2)}, u32[]{:S(2)}) collective-permute-start(f32[64,384]{1,0:T(8,128)S(1)} %pad_maximum_fusion.5), channel_id=1, source_target_pairs={{0,2},{2,0},{4,6},{6,4},{1,3},{3,1},{5,7},{7,5},{8,10},{10,8},{12,... | collective-permute-start | bytes 294920 | tf_op jit(solution)/shard_map/ppermute | solution.py:16
  87.2 1.5 %collective-permute-start.25 = (f32[64,384]{1,0:T(8,128)S(1)}, f32[64,384]{1,0:T(8,128)S(1)}, u32[]{:S(2)}, u32[]{:S(2)}) collective-permute-start(f32[64,384]{1,0:T(8,128)S(1)} %pad_maximum_fusion.6), channel_id=1, source_target_pairs={{0,16},{8,24},{16,0},{24,8},{1,17},{9,25},{17,1},{25,9},{2,18},{10... | collective-permute-start | bytes 294920 | tf_op jit(solution)/shard_map/ppermute | solution.py:16
  88.7 0.5 collective-permute-done.23
  89.2 1.5 %collective-permute-done.24 = f32[64,384]{1,0:T(8,128)S(1)} collective-permute-done((f32[64,384]{1,0:T(8,128)S(1)}, f32[64,384]{1,0:T(8,128)S(1)}, u32[]{:S(2)}, u32[]{:S(2)}) %collective-permute-start.24) | collective-permute-done | bytes 98336 | tf_op jit(solution)/shard_map/ppermute | solution.py:16
  90.7 1.1 collective-permute-done.25
  91.8 1.6 %collective-permute-start.26 = (f32[128,384]{1,0:T(8,128)S(1)}, f32[128,384]{1,0:T(8,128)S(1)}, u32[]{:S(2)}, u32[]{:S(2)}) collective-permute-start(f32[128,384]{1,0:T(8,128)S(1)} %pad_maximum_fusion), channel_id=1, source_target_pairs={{0,16},{8,24},{16,0},{24,8},{1,17},{9,25},{17,1},{25,9},{2,18},{10... | collective-permute-start | bytes 589832 | tf_op jit(solution)/shard_map/ppermute | solution.py:16
  94.0 3.6 %collective-permute-done.26 = f32[128,384]{1,0:T(8,128)S(1)} collective-permute-done((f32[128,384]{1,0:T(8,128)S(1)}, f32[128,384]{1,0:T(8,128)S(1)}, u32[]{:S(2)}, u32[]{:S(2)}) %collective-permute-start.26) | collective-permute-done | bytes 196640 | tf_op jit(solution)/shard_map/ppermute | solution.py:16
  97.6 1.5 %collective-permute-done.27 = f32[128,384]{1,0:T(8,128)S(1)} collective-permute-done((f32[128,384]{1,0:T(8,128)S(1)}, f32[128,384]{1,0:T(8,128)S(1)}, u32[]{:S(2)}, u32[]{:S(2)}) %collective-permute-start.27) | collective-permute-done | bytes 196640 | tf_op jit(solution)/shard_map/ppermute | solution.py:16
  100.2 2.4 %collective-permute-done.30.other_ref = f32[256,1152]{1,0:T(8,128)S(1)} collective-permute-done((f32[256,1152]{1,0:T(8,128)S(1)}, f32[256,1152]{1,0:T(8,128)S(1)}, u32[]{:S(2)}, u32[]{:S(2)}) %collective-permute-start.30) | collective-permute-done | bytes 1179680 | tf_op jit(solution)/shard_map/ppermute | solution.py:16
  102.6 31.7 %shard_map.53 = (f32[256,1024]{1,0:T(8,128)}, bf16[256,1024]{1,0:T(8,128)(2,1)S(1)}) custom-call(s32[5]{0:T(128)S(1)} %stack.59.place_ref, f32[256,1152]{1,0:T(8,128)S(1)} %maximum_maximum_fusion.mine_ref, f32[256,1152]{1,0:T(8,128)S(1)} %collective-permute-done.30.other_ref, bf16[1024,1024]{1,0:T(8,128)(2,1)S(1)} %get-tuple-element.112.left), custom_call_target="tpu_custom_call" | custom-call | flops 42949672960 | bytes 16777216 | tf_op jit(solution)/shard_map/pallas_call | solution.py:376
  134.5 3.0 %shard_map.54.refs_0_ = f32[8,256,256]{2,1,0:T(8,128)} custom-call(s32[5]{0:T(128)S(1)} %stack.59.place_ref, bf16[256,1024]{1,0:T(8,128)(2,1)S(1)} %get-tuple-element.114.weights_ref, bf16[8,512,256]{2,1,0:T(8,128)(2,1)S(1)} %shard_map.50.own_ref, f32[2,512,256]{2,1,0:T(8,128)S(1)} %collective-permute-done.refs_1_.first_ref, ...), custom_call_target="tpu_custom_call" | custom-call | flops 536870912 | bytes 8388608 | tf_op jit(solution)/shard_map/pallas_call | solution.py:419
  137.5 3.0 %shard_map.55 = f32[8,256,256]{2,1,0:T(8,128)} custom-call(s32[5]{0:T(128)S(1)} %stack.59.place_ref, bf16[256,1024]{1,0:T(8,128)(2,1)S(1)} %get-tuple-element.114.weights_ref, bf16[8,512,256]{2,1,0:T(8,128)(2,1)S(1)} %shard_map.50.own_ref, f32[2,512,256]{2,1,0:T(8,128)S(1)} %collective-permute-done.29.first_ref, ...), custom_call_target="tpu_custom_call", output_to_operand_aliasing={{}: (5, {})} | custom-call | flops 536870912 | bytes 8388608 | tf_op jit(solution)/shard_map/pallas_call | solution.py:419
  (59 shorter events, 4.3 us)
Async XLA Ops:
  1.6 15.8 %collective-permute-start.1 = (f32[256,512]{1,0:T(8,128)S(1)}, f32[256,512]{1,0:T(8,128)S(1)}, u32[]{:S(2)}, u32[]{:S(2)}) collective-permute-start(f32[256,512]{1,0:T(8,128)S(1)} %convert_element_type.3.refs_2_), channel_id=1, source_target_pairs={{0,1},{1,0},{2,3},{3,2},{4,5},{5,4},{6,7},{7,6},{8,9},{9,8},{10,11... | collective-permute-start | bytes 1572872 | tf_op jit(solution)/shard_map/ppermute | solution.py:16
  4.7 15.3 %collective-permute-start.4 = (f32[256,512]{1,0:T(8,128)S(1)}, f32[256,512]{1,0:T(8,128)}, u32[]{:S(2)}, u32[]{:S(2)}) collective-permute-start(f32[256,512]{1,0:T(8,128)S(1)} %convert_element_type.3.refs_2_), channel_id=1, source_target_pairs={{0,16},{8,24},{16,0},{24,8},{1,17},{9,25},{17,1},{25,9},{2,18},{10... | collective-permute-start | bytes 1572872 | tf_op jit(solution)/shard_map/ppermute | solution.py:16
  6.2 2.2 %copy-start = (bf16[512,16,256]{2,1,0:T(8,128)(2,1)S(1)}, bf16[512,16,256]{2,1,0:T(8,128)(2,1)}, u32[]{:S(2)}) copy-start(bf16[512,16,256]{2,1,0:T(8,128)(2,1)} %param.4) | copy-start | bytes 12582916
  8.4 0.7 copy-start.2
  9.1 21.0 %copy-start.3 = (f32[16,16]{1,0:T(8,128)S(1)}, f32[16,16]{1,0:T(8,128)}, u32[]{:S(2)}) copy-start(f32[16,16]{1,0:T(8,128)} %double_ref.3) | copy-start | bytes 3076
  12.2 26.9 %collective-permute-start = (f32[2,512,256]{2,1,0:T(8,128)S(1)}, f32[2,512,256]{2,1,0:T(8,128)S(1)}, u32[]{:S(2)}, u32[]{:S(2)}) collective-permute-start(f32[2,512,256]{2,1,0:T(8,128)S(1)} %shard_map.51), channel_id=1, source_target_pairs={{0,1},{1,0},{2,3},{3,2},{4,5},{5,4},{6,7},{7,6},{8,9},{9,8},{10,11... | collective-permute-start | bytes 3145736 | tf_op jit(solution)/shard_map/ppermute | solution.py:16
  17.4 12.5 %collective-permute-start.5 = (f32[256,512]{1,0:T(8,128)S(1)}, f32[256,512]{1,0:T(8,128)}, u32[]{:S(2)}, u32[]{:S(2)}) collective-permute-start(f32[256,512]{1,0:T(8,128)S(1)} %collective-permute-done.1.refs_3_), channel_id=1, source_target_pairs={{0,16},{8,24},{16,0},{24,8},{1,17},{9,25},{17,1},{25,9},{2,18},{10... | collective-permute-start | bytes 1572872 | tf_op jit(solution)/shard_map/ppermute | solution.py:16
  19.5 17.3 %collective-permute-start.2 = (f32[256,512]{1,0:T(8,128)S(1)}, f32[256,512]{1,0:T(8,128)}, u32[]{:S(2)}, u32[]{:S(2)}) collective-permute-start(f32[256,512]{1,0:T(8,128)S(1)} %convert_element_type.3.refs_2_), channel_id=1, source_target_pairs={{0,8},{8,0},{16,24},{24,16},{1,9},{9,1},{17,25},{25,17},{2,10},{10... | collective-permute-start | bytes 1572872 | tf_op jit(solution)/shard_map/ppermute | solution.py:16
  19.5 19.6 %collective-permute-start.3 = (f32[256,512]{1,0:T(8,128)S(1)}, f32[256,512]{1,0:T(8,128)}, u32[]{:S(2)}, u32[]{:S(2)}) collective-permute-start(f32[256,512]{1,0:T(8,128)S(1)} %collective-permute-done.1.refs_3_), channel_id=1, source_target_pairs={{0,8},{8,0},{16,24},{24,16},{1,9},{9,1},{17,25},{25,17},{2,10},{10... | collective-permute-start | bytes 1572872 | tf_op jit(solution)/shard_map/ppermute | solution.py:16
  20.0 19.1 %collective-permute-start.6 = (f32[256,512]{1,0:T(8,128)}, f32[256,512]{1,0:T(8,128)}, u32[]{:S(2)}, u32[]{:S(2)}) collective-permute-start(f32[256,512]{1,0:T(8,128)} %collective-permute-done.4.refs_6_), channel_id=1, source_target_pairs={{0,8},{8,0},{16,24},{24,16},{1,9},{9,1},{17,25},{25,17},{2,10},{10... | collective-permute-start | bytes 1572872 | tf_op jit(solution)/shard_map/ppermute | solution.py:16
  29.9 9.2 %collective-permute-start.7 = (f32[256,512]{1,0:T(8,128)}, f32[256,512]{1,0:T(8,128)}, u32[]{:S(2)}, u32[]{:S(2)}) collective-permute-start(f32[256,512]{1,0:T(8,128)} %collective-permute-done.5.refs_7_), channel_id=1, source_target_pairs={{0,8},{8,0},{16,24},{24,16},{1,9},{9,1},{17,25},{25,17},{2,10},{10... | collective-permute-start | bytes 1572872 | tf_op jit(solution)/shard_map/ppermute | solution.py:16
  30.1 2.2 %copy-start.1 = (bf16[512,16,256]{2,1,0:T(8,128)(2,1)S(1)}, bf16[512,16,256]{2,1,0:T(8,128)(2,1)}, u32[]{:S(2)}) copy-start(bf16[512,16,256]{2,1,0:T(8,128)(2,1)} %param.4) | copy-start | bytes 12582916
  45.2 2.9 %collective-permute-start.8 = (f32[256,1152]{1,0:T(8,128)S(1)}, f32[256,1152]{1,0:T(8,128)S(1)}, u32[]{:S(2)}, u32[]{:S(2)}) collective-permute-start(f32[256,1152]{1,0:T(8,128)S(1)} %get-tuple-element.70), channel_id=1, source_target_pairs={{0,8},{8,0},{16,24},{24,16},{1,9},{9,1},{17,25},{25,17},{2,10},{10... | collective-permute-start | bytes 3538952 | tf_op jit(solution)/shard_map/ppermute | solution.py:16
  48.3 7.0 %collective-permute-start.10 = (f32[128,384]{1,0:T(8,128)S(1)}, f32[128,384]{1,0:T(8,128)S(1)}, u32[]{:S(2)}, u32[]{:S(2)}) collective-permute-start(f32[128,384]{1,0:T(8,128)S(1)} %get-tuple-element.72), channel_id=1, source_target_pairs={{0,1},{1,0},{2,3},{3,2},{4,5},{5,4},{6,7},{7,6},{8,9},{9,8},{10,11... | collective-permute-start | bytes 589832 | tf_op jit(solution)/shard_map/ppermute | solution.py:16
  50.1 6.7 %collective-permute-start.11 = (f32[128,384]{1,0:T(8,128)S(1)}, f32[128,384]{1,0:T(8,128)S(1)}, u32[]{:S(2)}, u32[]{:S(2)}) collective-permute-start(f32[128,384]{1,0:T(8,128)S(1)} %get-tuple-element.73), channel_id=1, source_target_pairs={{0,2},{2,0},{4,6},{6,4},{1,3},{3,1},{5,7},{7,5},{8,10},{10,8},{12,... | collective-permute-start | bytes 589832 | tf_op jit(solution)/shard_map/ppermute | solution.py:16
  51.7 6.4 %collective-permute-start.9 = (f32[128,384]{1,0:T(8,128)S(1)}, f32[128,384]{1,0:T(8,128)S(1)}, u32[]{:S(2)}, u32[]{:S(2)}) collective-permute-start(f32[128,384]{1,0:T(8,128)S(1)} %get-tuple-element.71), channel_id=1, source_target_pairs={{0,16},{8,24},{16,0},{24,8},{1,17},{9,25},{17,1},{25,9},{2,18},{10... | collective-permute-start | bytes 589832 | tf_op jit(solution)/shard_map/ppermute | solution.py:16
  58.2 4.7 %collective-permute-start.12 = (f32[64,384]{1,0:T(8,128)S(1)}, f32[64,384]{1,0:T(8,128)S(1)}, u32[]{:S(2)}, u32[]{:S(2)}) collective-permute-start(f32[64,384]{1,0:T(8,128)S(1)} %slice.98), channel_id=1, source_target_pairs={{0,1},{1,0},{2,3},{3,2},{4,5},{5,4},{6,7},{7,6},{8,9},{9,8},{10,11... | collective-permute-start | bytes 294920 | tf_op jit(solution)/shard_map/ppermute | solution.py:16
  58.8 4.6 %collective-permute-start.13 = (f32[64,384]{1,0:T(8,128)S(1)}, f32[64,384]{1,0:T(8,128)S(1)}, u32[]{:S(2)}, u32[]{:S(2)}) collective-permute-start(f32[64,384]{1,0:T(8,128)S(1)} %slice.100), channel_id=1, source_target_pairs={{0,2},{2,0},{4,6},{6,4},{1,3},{3,1},{5,7},{7,5},{8,10},{10,8},{12,... | collective-permute-start | bytes 294920 | tf_op jit(solution)/shard_map/ppermute | solution.py:16
  59.1 4.6 %collective-permute-start.14 = (f32[64,384]{1,0:T(8,128)S(1)}, f32[64,384]{1,0:T(8,128)S(1)}, u32[]{:S(2)}, u32[]{:S(2)}) collective-permute-start(f32[64,384]{1,0:T(8,128)S(1)} %slice.102), channel_id=1, source_target_pairs={{0,16},{8,24},{16,0},{24,8},{1,17},{9,25},{17,1},{25,9},{2,18},{10... | collective-permute-start | bytes 294920 | tf_op jit(solution)/shard_map/ppermute | solution.py:16
  60.7 10.5 %collective-permute-start.18 = (f32[2,512,256]{2,1,0:T(8,128)S(1)}, f32[2,512,256]{2,1,0:T(8,128)S(1)}, u32[]{:S(2)}, u32[]{:S(2)}) collective-permute-start(f32[2,512,256]{2,1,0:T(8,128)S(1)} %collective-permute-done.refs_1_.first_ref), channel_id=1, source_target_pairs={{0,8},{8,0},{16,24},{24,16},{1,9},{9,1},{17,25},{25,17},{2,10},{10... | collective-permute-start | bytes 3145736 | tf_op jit(solution)/shard_map/ppermute | solution.py:16
  63.8 4.8 %collective-permute-start.15 = (f32[32,384]{1,0:T(8,128)S(1)}, f32[32,384]{1,0:T(8,128)S(1)}, u32[]{:S(2)}, u32[]{:S(2)}) collective-permute-start(f32[32,384]{1,0:T(8,128)S(1)} %slice.104), channel_id=1, source_target_pairs={{0,2},{2,0},{4,6},{6,4},{1,3},{3,1},{5,7},{7,5},{8,10},{10,8},{12,... | collective-permute-start | bytes 147464 | tf_op jit(solution)/shard_map/ppermute | solution.py:16
  65.5 4.1 %collective-permute-start.16 = (f32[32,384]{1,0:T(8,128)S(1)}, f32[32,384]{1,0:T(8,128)S(1)}, u32[]{:S(2)}, u32[]{:S(2)}) collective-permute-start(f32[32,384]{1,0:T(8,128)S(1)} %slice.106), channel_id=1, source_target_pairs={{0,16},{8,24},{16,0},{24,8},{1,17},{9,25},{17,1},{25,9},{2,18},{10... | collective-permute-start | bytes 147464 | tf_op jit(solution)/shard_map/ppermute | solution.py:16
  67.0 4.1 %collective-permute-start.17 = (f32[32,384]{1,0:T(8,128)S(1)}, f32[32,384]{1,0:T(8,128)S(1)}, u32[]{:S(2)}, u32[]{:S(2)}) collective-permute-start(f32[32,384]{1,0:T(8,128)S(1)} %slice.108), channel_id=1, source_target_pairs={{0,1},{1,0},{2,3},{3,2},{4,5},{5,4},{6,7},{7,6},{8,9},{9,8},{10,11... | collective-permute-start | bytes 147464 | tf_op jit(solution)/shard_map/ppermute | solution.py:16
  71.2 7.6 %collective-permute-start.19 = (f32[32,1152]{1,0:T(8,128)S(1)}, f32[32,1152]{1,0:T(8,128)S(1)}, u32[]{:S(2)}, u32[]{:S(2)}) collective-permute-start(f32[32,1152]{1,0:T(8,128)S(1)} %pad_maximum_fusion.3), channel_id=1, source_target_pairs={{0,4},{2,6},{4,0},{6,2},{1,5},{3,7},{5,1},{7,3},{8,12},{10,14},{12... | collective-permute-start | bytes 442376 | tf_op jit(solution)/shard_map/ppermute | solution.py:16
  78.8 4.2 %collective-permute-start.20 = (f32[32,384]{1,0:T(8,128)S(1)}, f32[32,384]{1,0:T(8,128)S(1)}, u32[]{:S(2)}, u32[]{:S(2)}) collective-permute-start(f32[32,384]{1,0:T(8,128)S(1)} %get-tuple-element.92), channel_id=1, source_target_pairs={{0,2},{2,0},{4,6},{6,4},{1,3},{3,1},{5,7},{7,5},{8,10},{10,8},{12,... | collective-permute-start | bytes 147464 | tf_op jit(solution)/shard_map/ppermute | solution.py:16
  78.9 4.6 %collective-permute-start.21 = (f32[32,384]{1,0:T(8,128)S(1)}, f32[32,384]{1,0:T(8,128)S(1)}, u32[]{:S(2)}, u32[]{:S(2)}) collective-permute-start(f32[32,384]{1,0:T(8,128)S(1)} %get-tuple-element.93), channel_id=1, source_target_pairs={{0,16},{8,24},{16,0},{24,8},{1,17},{9,25},{17,1},{25,9},{2,18},{10... | collective-permute-start | bytes 147464 | tf_op jit(solution)/shard_map/ppermute | solution.py:16
  79.4 4.2 %collective-permute-start.22 = (f32[32,384]{1,0:T(8,128)S(1)}, f32[32,384]{1,0:T(8,128)S(1)}, u32[]{:S(2)}, u32[]{:S(2)}) collective-permute-start(f32[32,384]{1,0:T(8,128)S(1)} %get-tuple-element.94), channel_id=1, source_target_pairs={{0,1},{1,0},{2,3},{3,2},{4,5},{5,4},{6,7},{7,6},{8,9},{9,8},{10,11... | collective-permute-start | bytes 147464 | tf_op jit(solution)/shard_map/ppermute | solution.py:16
  83.6 5.7 %collective-permute-start.23 = (f32[64,384]{1,0:T(8,128)S(1)}, f32[64,384]{1,0:T(8,128)S(1)}, u32[]{:S(2)}, u32[]{:S(2)}) collective-permute-start(f32[64,384]{1,0:T(8,128)S(1)} %pad_maximum_fusion.4), channel_id=1, source_target_pairs={{0,1},{1,0},{2,3},{3,2},{4,5},{5,4},{6,7},{7,6},{8,9},{9,8},{10,11... | collective-permute-start | bytes 294920 | tf_op jit(solution)/shard_map/ppermute | solution.py:16
  85.2 5.5 %collective-permute-start.24 = (f32[64,384]{1,0:T(8,128)S(1)}, f32[64,384]{1,0:T(8,128)S(1)}, u32[]{:S(2)}, u32[]{:S(2)}) collective-permute-start(f32[64,384]{1,0:T(8,128)S(1)} %pad_maximum_fusion.5), channel_id=1, source_target_pairs={{0,2},{2,0},{4,6},{6,4},{1,3},{3,1},{5,7},{7,5},{8,10},{10,8},{12,... | collective-permute-start | bytes 294920 | tf_op jit(solution)/shard_map/ppermute | solution.py:16
  87.2 4.6 %collective-permute-start.25 = (f32[64,384]{1,0:T(8,128)S(1)}, f32[64,384]{1,0:T(8,128)S(1)}, u32[]{:S(2)}, u32[]{:S(2)}) collective-permute-start(f32[64,384]{1,0:T(8,128)S(1)} %pad_maximum_fusion.6), channel_id=1, source_target_pairs={{0,16},{8,24},{16,0},{24,8},{1,17},{9,25},{17,1},{25,9},{2,18},{10... | collective-permute-start | bytes 294920 | tf_op jit(solution)/shard_map/ppermute | solution.py:16
  91.8 5.7 %collective-permute-start.26 = (f32[128,384]{1,0:T(8,128)S(1)}, f32[128,384]{1,0:T(8,128)S(1)}, u32[]{:S(2)}, u32[]{:S(2)}) collective-permute-start(f32[128,384]{1,0:T(8,128)S(1)} %pad_maximum_fusion), channel_id=1, source_target_pairs={{0,16},{8,24},{16,0},{24,8},{1,17},{9,25},{17,1},{25,9},{2,18},{10... | collective-permute-start | bytes 589832 | tf_op jit(solution)/shard_map/ppermute | solution.py:16
  93.4 5.7 %collective-permute-start.27 = (f32[128,384]{1,0:T(8,128)S(1)}, f32[128,384]{1,0:T(8,128)S(1)}, u32[]{:S(2)}, u32[]{:S(2)}) collective-permute-start(f32[128,384]{1,0:T(8,128)S(1)} %pad_maximum_fusion.1), channel_id=1, source_target_pairs={{0,1},{1,0},{2,3},{3,2},{4,5},{5,4},{6,7},{7,6},{8,9},{9,8},{10,11... | collective-permute-start | bytes 589832 | tf_op jit(solution)/shard_map/ppermute | solution.py:16
  93.9 5.7 %collective-permute-start.28 = (f32[128,384]{1,0:T(8,128)S(1)}, f32[128,384]{1,0:T(8,128)S(1)}, u32[]{:S(2)}, u32[]{:S(2)}) collective-permute-start(f32[128,384]{1,0:T(8,128)S(1)} %pad_maximum_fusion.2), channel_id=1, source_target_pairs={{0,2},{2,0},{4,6},{6,4},{1,3},{3,1},{5,7},{7,5},{8,10},{10,8},{12,... | collective-permute-start | bytes 589832 | tf_op jit(solution)/shard_map/ppermute | solution.py:16
  99.7 2.9 %collective-permute-start.30 = (f32[256,1152]{1,0:T(8,128)S(1)}, f32[256,1152]{1,0:T(8,128)S(1)}, u32[]{:S(2)}, u32[]{:S(2)}) collective-permute-start(f32[256,1152]{1,0:T(8,128)S(1)} %maximum_maximum_fusion.mine_ref), channel_id=1, source_target_pairs={{0,8},{8,0},{16,24},{24,16},{1,9},{9,1},{17,25},{25,17},{2,10},{10... | collective-permute-start | bytes 3538952 | tf_op jit(solution)/shard_map/ppermute | solution.py:16
  99.7 34.6 %collective-permute-start.29 = (f32[2,512,256]{2,1,0:T(8,128)S(1)}, f32[2,512,256]{2,1,0:T(8,128)S(1)}, u32[]{:S(2)}, u32[]{:S(2)}) collective-permute-start(f32[2,512,256]{2,1,0:T(8,128)S(1)} %collective-permute-done.refs_1_.first_ref), channel_id=1, source_target_pairs={{0,16},{8,24},{16,0},{24,8},{1,17},{9,25},{17,1},{25,9},{2,18},{10... | collective-permute-start | bytes 3145736 | tf_op jit(solution)/shard_map/ppermute | solution.py:16
  134.3 3.2 %collective-permute-start.31 = (f32[2,512,256]{2,1,0:T(8,128)S(1)}, f32[2,512,256]{2,1,0:T(8,128)S(1)}, u32[]{:S(2)}, u32[]{:S(2)}) collective-permute-start(f32[2,512,256]{2,1,0:T(8,128)S(1)} %collective-permute-done.29.first_ref), channel_id=1, source_target_pairs={{0,8},{8,0},{16,24},{24,16},{1,9},{9,1},{17,25},{25,17},{2,10},{10... | collective-permute-start | bytes 3145736 | tf_op jit(solution)/shard_map/ppermute | solution.py:16
